TPU v7x, 256 devices: a whole 4x4x8 slice. The times are simulated.
256 devices in a mesh: row: 32 (over z, y_hi, core), col: 8 (over x, y_lo).
Axes of the slice: x: 4, y: 4 (y_hi: 2, y_lo: 2; y = y_hi * 2 + y_lo), z: 8, core: 2. Of those that a mesh axis runs over, the one named last changes fastest.
Arguments:
- inputs: bfloat16 [32, 8, 2, 128, 1024], P('row', 'col'), may hold values from -6 to 6
- targets: bfloat16 [32, 8, 2, 128, 1024], P('row', 'col'), may hold values from -6 to 6
- up_master: float32 [8, 1024, 2048], P('col', 'row'), may hold values from -6 to 6
- up_momentum: float32 [8, 1024, 2048], P('col', 'row'), may hold values from -0.75 to 0.75
- down_master: float32 [32, 2048, 1024], P('row', 'col'), may hold values from -6 to 6
- down_momentum: float32 [32, 2048, 1024], P('row', 'col'), may hold values from -0.75 to 0.75
Outputs:
- new_up: float32 [8, 1024, 2048], P('col', 'row')
- new_up_momentum: float32 [8, 1024, 2048], P('col', 'row')
- new_down: float32 [32, 2048, 1024], P('row', 'col')
- new_down_momentum: float32 [32, 2048, 1024], P('row', 'col')
All inputs are finite; a program needn't handle non-finite values.
Results may differ from a plain program's by a relative error of at most 0.015.
The roundings to bfloat16 on the way count: a program that leaves them out, or rounds other values in their place, can miss the bound.
Values may be sent and summed in bfloat16 or wider, within the bound.
No kernel may reach another device: no remote copies, remote signals or barrier semaphores. Data moves between devices by JAX's collectives and lax.ppermute only.
A program may use at most 128 MiB of HBM per device.

v0:
```python
import jax
import jax.numpy as jnp
from jax import lax
from jax.experimental import pallas as pl
from jax.experimental.pallas import tpu as pltpu
from jax.sharding import PartitionSpec as P

adam_rate = 0.05
beta_one = 0.9
beta_two = 0.95
adam_eps = 1e-06
decay_rate = 0.1
outer_rate = 0.7
outer_beta = 0.9
norm_eps = 1e-06

bf16 = jnp.bfloat16
f32 = jnp.float32

TOK, D, FFW = 128, 1024, 2048
BLK = 256
SEND, KEEP = 448, 576
EARLY, LATE = 768, 1280
width_scale = D ** (-0.5)
hidden_scale = FFW ** (-0.5)
ROOT = (2 / 3.141592653589793) ** 0.5


def swap_core(a):
    return lax.ppermute(a, "row", [(i, i ^ 1) for i in range(32)])


def swap_yh(a):
    return lax.ppermute(a, "row", [(i, i ^ 2) for i in range(32)])


def from_z(a):
    return lax.ppermute(a, "row", [(i, (i + (4 if i % 2 else -4)) % 32) for i in range(32)])


def to_z(a):
    return lax.ppermute(a, "row", [(i, (i + (-4 if i % 2 else 4)) % 32) for i in range(32)])


def swap_yl(a):
    return lax.ppermute(a, "col", [(i, i ^ 1) for i in range(8)])


def from_x(a, k):
    return lax.ppermute(a, "col", [(i, (i - 2 * k) % 8) for i in range(8)])


def up_order():
    own = [(0, 0, 0), (0, 1, 0), (0, 0, 1), (0, 1, 1)]
    side = [(k, y, c) for k in (1, 2, 3) for _, y, c in own] + [(4, 0, 0), (4, 1, 0)]
    other = [(-k, y, 1 - c) for k, y, c in side]
    return other, side, own


DOWN_ORDER = ((1, 1), (2, 1), (3, 1), (0, 1), (0, 0), (1, 0), (2, 0), (3, 0))


def gather_up(a):
    b = swap_yh(a)
    own = [a, b, swap_core(a), swap_core(b)]
    now, side = jnp.concatenate(own, 0), []
    for k in range(3):
        now = from_z(now)
        side.append(now)
    side.append(from_z(now[:64]))
    return [swap_core(s) for s in side], side, own


def gather_down(a):
    b0 = swap_yl(a)
    a1, a3, a2 = from_x(a, 1), from_x(a, -1), from_x(a, 2)
    return [from_x(b0, 1), swap_yl(a2), from_x(b0, -1), b0, a, a1, a2, a3]


def add(*parts):
    total = parts[0].astype(f32)
    for p in parts[1:]:
        total = total + p.astype(f32)
    return total


def scatter_up(other, keep):
    got = swap_core(other)
    p = to_z(add(keep[384:448], got[384:448]).astype(bf16))
    p = jnp.pad(p, ((0, 64), (0, 0)))
    for at in (256, 128, 0):
        p = to_z(add(keep[at : at + 128], got[at : at + 128], p).astype(bf16))
    away = add(keep[SEND + 64 :], p[64:]).astype(bf16)
    mine = add(keep[SEND : SEND + 64], p[:64], swap_core(away))
    return mine[:32] + swap_yh(mine[32:].astype(bf16)).astype(f32)


def scatter_down(u1, u2, u3, u0, t0, t1, t2, t3):
    p, m, w = from_x(u1, -1), from_x(u3, 1), swap_yl(u2)
    u0 = add(u0, p, m).astype(bf16)
    t2 = add(t2, w).astype(bf16)
    return add(t0, from_x(t1, -1), from_x(t3, 1), from_x(t2, -2), swap_yl(u0))


def hidden_place():
    col = lax.axis_index("col")
    x, yl = col // 2, col % 2
    return jnp.stack([((x + dx) % 4) * 2 + (yl + dyl) % 2 for dx, dyl in DOWN_ORDER]).astype(jnp.int32)


def feature_order():
    row = lax.axis_index("row")
    z, yh, core = row // 4, (row // 2) % 2, row % 2
    sign = 1 - 2 * core
    other, side, own = up_order()
    first = jnp.stack(
        [((z + sign * k) % 8) * 4 + ((yh + y) % 2) * 2 + (core + c) % 2 for k, y, c in other + side + own]
    )
    place = (first[:, None] * 32 + jnp.arange(32)[None]).reshape(1, D)
    return (lax.broadcasted_iota(jnp.int32, (D, D), 0) == place).astype(bf16)


def dot(a, b, dims=((1,), (0,))):
    return lax.dot_general(a, b, (dims, ((), ())), preferred_element_type=f32)


def gelu(x):
    return 0.5 * x * (1.0 + jnp.tanh(ROOT * (x + 0.044715 * x * x * x)))


def gelu_slope(x):
    t = jnp.tanh(ROOT * (x + 0.044715 * x * x * x))
    return 0.5 * (1.0 + t) + 0.5 * x * (1.0 - t * t) * (ROOT * (1.0 + 3 * 0.044715 * x * x))


def first_weight(start, raw, scale):
    part = raw / (jnp.abs(raw) + adam_eps / scale)
    return (1 - adam_rate * decay_rate) * start.astype(f32) - adam_rate * part


def change_of(start, one, two, scale):
    eps = adam_eps / scale
    left = 1 - adam_rate * decay_rate
    ca, cb = (1 - beta_one) * beta_one / (1 - beta_one**2), (1 - beta_one) / (1 - beta_one**2)
    cc, cd = (1 - beta_two) * beta_two / (1 - beta_two**2), (1 - beta_two) / (1 - beta_two**2)
    part_one = one / ((jnp.abs(one) + eps) * (1 / (adam_rate * left)))
    square = one * one + (cd / cc) * (two * two)
    size = square * lax.rsqrt(jnp.maximum(square, 1e-36))
    root = cc**0.5
    part_two = (one + (cb / ca) * two) / ((size + eps / root) * (root / (adam_rate * ca)))
    return (part_one + part_two + (1 - left * left) * start.astype(f32)).astype(bf16)


def inner_kernel(up_pieces, down_pieces, *refs):
    count = len(up_pieces) + len(down_pieces)
    place_ref, nt_ref, x_ref, t_ref = refs[:4]
    pieces = refs[4 : 4 + count]
    act_ref, g_ref, gp_ref, send_ref, keep_ref, early_ref, late_ref = refs[4 + count : 11 + count]
    su, sd, w1u, w1d, pre_ref, n_ref, sem, out_sem = refs[11 + count :]

    up_copies, down_copies = [], []
    for i, (start, rows, at) in enumerate(up_pieces):
        up_copies.append(
            pltpu.make_async_copy(pieces[i].at[pl.ds(start, rows)], su.at[pl.ds(at, rows)], sem.at[i])
        )
    for j, (start, rows, at) in enumerate(down_pieces):
        i = j + len(up_pieces)
        down_copies.append(
            pltpu.make_async_copy(pieces[i].at[pl.ds(start, rows)], sd.at[pl.ds(at, rows)], sem.at[i])
        )
    for c in up_copies + down_copies:
        c.start()
    for t in range(2):
        n_ref[t] = nt_ref[t].T
    for c in up_copies:
        c.wait()

    def columns(k):
        return pl.ds(pl.multiple_of(place_ref[k] * BLK, BLK), BLK)

    def slot(k):
        return pl.ds(pl.multiple_of(k * BLK, BLK), BLK)

    @pl.loop(0, 8)
    def _(k):
        pre = dot(n_ref[0], su[:, columns(k)]) * width_scale
        pre_ref[:, slot(k)] = pre
        act_ref[0, :, slot(k)] = gelu(pre).astype(bf16)

    for c in down_copies:
        c.wait()
    outs = [
        pltpu.make_async_copy(su.at[pl.ds(0, SEND)], send_ref, out_sem.at[0]),
        pltpu.make_async_copy(su.at[pl.ds(SEND, KEEP)], keep_ref, out_sem.at[1]),
        pltpu.make_async_copy(sd.at[pl.ds(0, EARLY)], early_ref, out_sem.at[2]),
        pltpu.make_async_copy(sd.at[pl.ds(EARLY, LATE)], late_ref, out_sem.at[3]),
    ]
    for c in outs:
        c.start()

    def grad_out(t, weight):
        @pl.loop(0, D // BLK)
        def _(j):
            outval = dot(act_ref[t], weight[:, slot(j)]) * hidden_scale
            resid = x_ref[t, :, slot(j)].astype(f32) + outval - t_ref[t, :, slot(j)].astype(f32)
            g_ref[t, :, slot(j)] = (resid * (1.0 / TOK)).astype(bf16)

    def grad_pre(t, weight):
        @pl.loop(0, 8)
        def _(k):
            grad_act = dot(g_ref[t], weight[slot(k), :], ((1,), (1,))) * hidden_scale
            gp_ref[t, :, columns(k)] = (grad_act * gelu_slope(pre_ref[:, slot(k)])).astype(bf16)

    grad_out(0, sd)
    grad_pre(0, sd)

    @pl.loop(0, 8)
    def _(k):
        raw = dot(nt_ref[0], gp_ref[0, :, columns(k)])
        w1u[...] = first_weight(su[:, columns(k)], raw, width_scale).astype(bf16)
        raw = dot(act_ref[0, :, slot(k)], g_ref[0], ((0,), (0,)))
        w1d[slot(k), :] = first_weight(sd[slot(k), :], raw, hidden_scale).astype(bf16)
        pre = dot(n_ref[1], w1u[...]) * width_scale
        pre_ref[:, slot(k)] = pre
        act_ref[1, :, slot(k)] = gelu(pre).astype(bf16)

    grad_out(1, w1d)
    grad_pre(1, w1d)
    for c in outs:
        c.wait()


def inner_steps(place, normed_t, x, t, up_pieces, down_pieces):
    vmem, hbm = pl.BlockSpec(memory_space=pltpu.VMEM), pl.BlockSpec(memory_space=pl.ANY)
    far = pl.BlockSpec(memory_space=pltpu.HBM)
    pieces = [p[0] for p in up_pieces + down_pieces]

    def kernel(*refs):
        inner_kernel([p[1:] for p in up_pieces], [p[1:] for p in down_pieces], *refs)

    return pl.pallas_call(
        kernel,
        out_shape=(
            jax.ShapeDtypeStruct((2, TOK, FFW), bf16),
            jax.ShapeDtypeStruct((2, TOK, D), bf16),
            jax.ShapeDtypeStruct((2, TOK, FFW), bf16),
            jax.ShapeDtypeStruct((SEND, FFW), bf16),
            jax.ShapeDtypeStruct((KEEP, FFW), bf16),
            jax.ShapeDtypeStruct((EARLY, D), bf16),
            jax.ShapeDtypeStruct((LATE, D), bf16),
        ),
        in_specs=[pl.BlockSpec(memory_space=pltpu.SMEM)] + [vmem] * 3 + [far] * len(pieces),
        out_specs=(vmem, vmem, vmem, hbm, hbm, hbm, hbm),
        scratch_shapes=[
            pltpu.VMEM((D, FFW), bf16),
            pltpu.VMEM((FFW, D), bf16),
            pltpu.VMEM((D, BLK), bf16),
            pltpu.VMEM((FFW, D), bf16),
            pltpu.VMEM((TOK, FFW), f32),
            pltpu.VMEM((2, TOK, D), bf16),
            pltpu.SemaphoreType.DMA((len(pieces),)),
            pltpu.SemaphoreType.DMA((4,)),
        ],
        compiler_params=pltpu.CompilerParams(vmem_limit_bytes=36 * 1024 * 1024),
        cost_estimate=pl.CostEstimate(flops=5 * 10**9, bytes_accessed=24 * 2**20, transcendentals=0),
        name="inner_steps",
    )(place, normed_t, x, t, *pieces)


def up_change(start, normed_t, grad_pre, first):
    rows = start.shape[0]
    wide = 2 * BLK

    def kernel(s_ref, n_ref, g_ref, o_ref):
        one = dot(n_ref[0, pl.ds(first, rows)], g_ref[0])
        two = dot(n_ref[1, pl.ds(first, rows)], g_ref[1])
        o_ref[...] = change_of(s_ref[...], one, two, width_scale)

    return pl.pallas_call(
        kernel,
        grid=(FFW // wide,),
        out_shape=jax.ShapeDtypeStruct((rows, FFW), bf16),
        in_specs=[
            pl.BlockSpec((rows, wide), lambda j: (0, j)),
            pl.BlockSpec((2, D, TOK), lambda j: (0, 0, 0)),
            pl.BlockSpec((2, TOK, wide), lambda j: (0, 0, j)),
        ],
        out_specs=pl.BlockSpec((rows, wide), lambda j: (0, j)),
        compiler_params=pltpu.CompilerParams(vmem_limit_bytes=24 * 1024 * 1024),
        cost_estimate=pl.CostEstimate(flops=4 * rows * TOK * FFW, bytes_accessed=4 * rows * FFW, transcendentals=0),
        name="up_change",
    )(start, normed_t, grad_pre)


def down_change(start, act, grad_out, first):
    rows = start.shape[0]

    def kernel(s_ref, a_ref, g_ref, *o_refs):
        one = dot(a_ref[0, :, pl.ds(first, rows)], g_ref[0], ((0,), (0,)))
        two = dot(a_ref[1, :, pl.ds(first, rows)], g_ref[1], ((0,), (0,)))
        change = change_of(s_ref[...], one, two, hidden_scale)
        for i, o_ref in enumerate(o_refs):
            o_ref[...] = change[BLK * i : BLK * i + BLK]

    return pl.pallas_call(
        kernel,
        grid=(D // BLK,),
        out_shape=(jax.ShapeDtypeStruct((BLK, D), bf16),) * (rows // BLK),
        in_specs=[
            pl.BlockSpec((rows, BLK), lambda j: (0, j)),
            pl.BlockSpec((2, TOK, FFW), lambda j: (0, 0, 0)),
            pl.BlockSpec((2, TOK, BLK), lambda j: (0, 0, j)),
        ],
        out_specs=(pl.BlockSpec((BLK, BLK), lambda j: (0, j)),) * (rows // BLK),
        compiler_params=pltpu.CompilerParams(vmem_limit_bytes=24 * 1024 * 1024),
        cost_estimate=pl.CostEstimate(flops=4 * rows * TOK * D, bytes_accessed=4 * rows * D, transcendentals=0),
        name="down_change",
    )(start, act, grad_out)


def local(inputs, targets, up_master, up_momentum, down_master, down_momentum):
    other, side, own = gather_up(up_master[0].astype(bf16))
    down_pieces = [
        (a, 0, BLK, BLK * i) for i, a in enumerate(gather_down(down_master[0].astype(bf16)))
    ]
    up_pieces, at = [], 0
    for a in other + side + own:
        up_pieces.append((a, 0, a.shape[0], at))
        at += a.shape[0]

    x, t = inputs[0, 0], targets[0, 0]
    feats = x.astype(f32)
    square_mean = jnp.mean(feats * feats, axis=-1, keepdims=True)
    normed = (feats * lax.rsqrt(square_mean + norm_eps)).astype(bf16)
    order = feature_order()
    rel_t = jnp.einsum("de,tnd->ten", order, normed, preferred_element_type=f32).astype(bf16)

    act, grad_out, grad_pre, up_other, up_keep, down_early, down_late = inner_steps(
        hidden_place(), rel_t, x, t, up_pieces, down_pieces
    )
    v_early = down_change(down_early, act, grad_out, 0)
    v_late = down_change(down_late, act, grad_out, EARLY)
    down_avg = scatter_down(*v_early, *v_late) / 8
    v_other = up_change(up_other, rel_t, grad_pre, 0)
    v_keep = up_change(up_keep, rel_t, grad_pre, SEND)
    up_avg = scatter_up(v_other, v_keep) / 32
    new_up_momentum = outer_beta * up_momentum + up_avg[None]
    new_up = up_master - outer_rate * (up_avg[None] + outer_beta * new_up_momentum)
    new_down_momentum = outer_beta * down_momentum + down_avg[None]
    new_down = down_master - outer_rate * (down_avg[None] + outer_beta * new_down_momentum)
    return (new_up, new_up_momentum, new_down, new_down_momentum)


def solution(mesh):
    in_specs = (
        P("row", "col", None, None, None),
        P("row", "col", None, None, None),
        P("col", "row", None),
        P("col", "row", None),
        P("row", "col", None),
        P("row", "col", None),
    )
    out_specs = (
        P("col", "row", None),
        P("col", "row", None),
        P("row", "col", None),
        P("row", "col", None),
    )
    return jax.shard_map(local, mesh=mesh, in_specs=in_specs, out_specs=out_specs, check_vma=False)
```

profile of v0, /device:TPU:1, one launch (start us, length us, event | category | flops | bytes accessed | tf_op | source)
XLA Modules:
  0.0 162.3 jit_solution(5733078280463141927)
XLA Ops:
  1.7 3.8 %collective-permute-start = (bf16[32,2048]{1,0:T(8,128)(2,1)S(1)}, bf16[32,2048]{1,0:T(8,128)(2,1)S(1)}, u32[]{:S(2)}, u32[]{:S(2)}) collective-permute-start(bf16[32,2048]{1,0:T(8,128)(2,1)S(1)} %convert_bitcast_fusion.1.refs_12_), channel_id=1, source_target_pairs={{0,16},{8,24},{16,0},{24,8},{32,48},{40,56},{48,32},{56,40},{64,80... | collective-permute-start | bytes 393224 | tf_op jit(solution)/shard_map/ppermute | solution.py:34
  6.5 1.4 collective-permute-done.refs_13_
  7.9 3.6 %collective-permute-start.2 = (bf16[32,2048]{1,0:T(8,128)(2,1)S(1)}, bf16[32,2048]{1,0:T(8,128)(2,1)S(1)}, u32[]{:S(2)}, u32[]{:S(2)}) collective-permute-start(bf16[32,2048]{1,0:T(8,128)(2,1)S(1)} %collective-permute-done.refs_13_), channel_id=1, source_target_pairs={{0,8},{8,0},{16,24},{24,16},{32,40},{40,32},{48,56},{56,48},{64,72... | collective-permute-start | bytes 393224 | tf_op jit(solution)/shard_map/ppermute | solution.py:30
  12.8 10.5 %collective-permute-done.3.refs_8_ = bf16[128,2048]{1,0:T(8,128)(2,1)S(1)} collective-permute-done((bf16[128,2048]{1,0:T(8,128)(2,1)S(1)}, bf16[128,2048]{1,0:T(8,128)(2,1)S(1)}, u32[]{:S(2)}, u32[]{:S(2)}) %collective-permute-start.3) | collective-permute-done | bytes 524320 | tf_op jit(solution)/shard_map/ppermute | solution.py:38
  24.6 2.8 %collective-permute-start.13 = (bf16[256,1024]{1,0:T(8,128)(2,1)S(1)}, bf16[256,1024]{1,0:T(8,128)(2,1)}, u32[]{:S(2)}, u32[]{:S(2)}) collective-permute-start(bf16[256,1024]{1,0:T(8,128)(2,1)S(1)} %convert_bitcast_fusion.refs_20_), channel_id=1, source_target_pairs={{0,4},{1,5},{2,6},{3,7},{4,0},{5,1},{6,2},{7,3},{8,12},{9,13},{10,... | collective-permute-start | bytes 1572872 | tf_op jit(solution)/shard_map/ppermute | solution.py:50
  28.7 3.9 %collective-permute-done.5.refs_9_ = bf16[128,2048]{1,0:T(8,128)(2,1)} collective-permute-done((bf16[128,2048]{1,0:T(8,128)(2,1)S(1)}, bf16[128,2048]{1,0:T(8,128)(2,1)}, u32[]{:S(2)}, u32[]{:S(2)}) %collective-permute-start.5) | collective-permute-done | bytes 524320 | tf_op jit(solution)/shard_map/ppermute | solution.py:38
  33.8 1.5 collective-permute-start.16
  37.9 4.6 %collective-permute-done.7.refs_10_ = bf16[128,2048]{1,0:T(8,128)(2,1)S(1)} collective-permute-done((bf16[128,2048]{1,0:T(8,128)(2,1)}, bf16[128,2048]{1,0:T(8,128)(2,1)S(1)}, u32[]{:S(2)}, u32[]{:S(2)}) %collective-permute-start.7) | collective-permute-done | bytes 524320 | tf_op jit(solution)/shard_map/ppermute | solution.py:38
  42.6 6.2 %collective-permute-done.17.refs_23_ = bf16[256,1024]{1,0:T(8,128)(2,1)} collective-permute-done((bf16[256,1024]{1,0:T(8,128)(2,1)S(1)}, bf16[256,1024]{1,0:T(8,128)(2,1)}, u32[]{:S(2)}, u32[]{:S(2)}) %collective-permute-start.17) | collective-permute-done | bytes 524320 | tf_op jit(solution)/shard_map/ppermute | solution.py:50
  48.9 7.1 %collective-permute-start.4 = (bf16[128,2048]{1,0:T(8,128)(2,1)S(1)}, bf16[128,2048]{1,0:T(8,128)(2,1)}, u32[]{:S(2)}, u32[]{:S(2)}) collective-permute-start(bf16[128,2048]{1,0:T(8,128)(2,1)S(1)} %collective-permute-done.3.refs_8_), channel_id=1, source_target_pairs={{0,8},{8,0},{16,24},{24,16},{32,40},{40,32},{48,56},{56,48},{64,72... | collective-permute-start | bytes 1572872 | tf_op jit(solution)/shard_map/ppermute | solution.py:30
  56.0 4.0 %collective-permute-done.15.refs_18_ = bf16[256,1024]{1,0:T(8,128)(2,1)} collective-permute-done((bf16[256,1024]{1,0:T(8,128)(2,1)}, bf16[256,1024]{1,0:T(8,128)(2,1)}, u32[]{:S(2)}, u32[]{:S(2)}) %collective-permute-start.15) | collective-permute-done | bytes 524320 | tf_op jit(solution)/shard_map/ppermute | solution.py:50
  60.1 3.0 %collective-permute-start.8 = (bf16[128,2048]{1,0:T(8,128)(2,1)S(1)}, bf16[128,2048]{1,0:T(8,128)(2,1)}, u32[]{:S(2)}, u32[]{:S(2)}) collective-permute-start(bf16[128,2048]{1,0:T(8,128)(2,1)S(1)} %collective-permute-done.7.refs_10_), channel_id=1, source_target_pairs={{0,8},{8,0},{16,24},{24,16},{32,40},{40,32},{48,56},{56,48},{64,72... | collective-permute-start | bytes 1572872 | tf_op jit(solution)/shard_map/ppermute | solution.py:30
  65.2 19.6 %inner_steps.1 = (bf16[2,128,2048]{2,1,0:T(8,128)(2,1)S(1)}, bf16[2,128,1024]{2,1,0:T(8,128)(2,1)S(1)}, bf16[2,128,2048]{2,1,0:T(8,128)(2,1)S(1)}, bf16[448,2048...) custom-call(s32[8]{0:T(128)S(1)} %stack.134.refs_0_, ...), custom_call_target="tpu_custom_call" | custom-call | flops 5000000000 | bytes 25165824 | tf_op jit(solution)/shard_map/inner_steps/pallas_call | solution.py:241
  84.9 3.8 %up_change.3 = bf16[448,2048]{1,0:T(8,128)(2,1)S(1)} custom-call(bf16[448,2048]{1,0:T(8,128)(2,1)S(1)} %get-tuple-element.21.s_ref, bf16[2,1024,128]{2,1,0:T(8,128)(2,1)S(1)} %fusion.7.refs_1_.n_ref, bf16[2,128,2048]{2,1,0:T(8,128)(2,1)S(1)} %get-tuple-element.20.g_ref), custom_call_target="tpu_custom_call" | custom-call | flops 469762048 | bytes 3670016 | tf_op jit(solution)/shard_map/up_change/pallas_call | solution.py:279
  89.2 4.7 %up_change.2 = bf16[576,2048]{1,0:T(8,128)(2,1)S(1)} custom-call(bf16[576,2048]{1,0:T(8,128)(2,1)S(1)} %get-tuple-element.19.s_ref, bf16[2,1024,128]{2,1,0:T(8,128)(2,1)S(1)} %fusion.7.refs_1_.n_ref, bf16[2,128,2048]{2,1,0:T(8,128)(2,1)S(1)} %get-tuple-element.20.g_ref), custom_call_target="tpu_custom_call" | custom-call | flops 603979776 | bytes 4718592 | tf_op jit(solution)/shard_map/up_change/pallas_call | solution.py:279
  94.0 2.8 %collective-permute-start.19 = (bf16[64,2048]{1,0:T(8,128)(2,1)S(1)}, bf16[64,2048]{1,0:T(8,128)(2,1)S(1)}, u32[]{:S(2)}, u32[]{:S(2)}) collective-permute-start(bf16[64,2048]{1,0:T(8,128)(2,1)S(1)} %add_convert_fusion.6), channel_id=1, source_target_pairs={{0,32},{8,232},{16,48},{24,248},{32,64},{40,8},{48,80},{56,24},{64... | collective-permute-start | bytes 786440 | tf_op jit(solution)/shard_map/ppermute | solution.py:42
  96.7 3.3 %collective-permute-done.19 = bf16[64,2048]{1,0:T(8,128)(2,1)S(1)} collective-permute-done((bf16[64,2048]{1,0:T(8,128)(2,1)S(1)}, bf16[64,2048]{1,0:T(8,128)(2,1)S(1)}, u32[]{:S(2)}, u32[]{:S(2)}) %collective-permute-start.19) | collective-permute-done | bytes 262176 | tf_op jit(solution)/shard_map/ppermute | solution.py:42
  100.2 3.2 %collective-permute-start.20 = (bf16[128,2048]{1,0:T(8,128)(2,1)S(1)}, bf16[128,2048]{1,0:T(8,128)(2,1)S(1)}, u32[]{:S(2)}, u32[]{:S(2)}) collective-permute-start(bf16[128,2048]{1,0:T(8,128)(2,1)S(1)} %add_convert_fusion.4), channel_id=1, source_target_pairs={{0,32},{8,232},{16,48},{24,248},{32,64},{40,8},{48,80},{56,24},{64... | collective-permute-start | bytes 1572872 | tf_op jit(solution)/shard_map/ppermute | solution.py:42
  103.4 6.1 %collective-permute-done.20 = bf16[128,2048]{1,0:T(8,128)(2,1)S(1)} collective-permute-done((bf16[128,2048]{1,0:T(8,128)(2,1)S(1)}, bf16[128,2048]{1,0:T(8,128)(2,1)S(1)}, u32[]{:S(2)}, u32[]{:S(2)}) %collective-permute-start.20) | collective-permute-done | bytes 524320 | tf_op jit(solution)/shard_map/ppermute | solution.py:42
  109.8 3.2 %collective-permute-start.21 = (bf16[128,2048]{1,0:T(8,128)(2,1)S(1)}, bf16[128,2048]{1,0:T(8,128)(2,1)S(1)}, u32[]{:S(2)}, u32[]{:S(2)}) collective-permute-start(bf16[128,2048]{1,0:T(8,128)(2,1)S(1)} %add_convert_fusion.3), channel_id=1, source_target_pairs={{0,32},{8,232},{16,48},{24,248},{32,64},{40,8},{48,80},{56,24},{64... | collective-permute-start | bytes 1572872 | tf_op jit(solution)/shard_map/ppermute | solution.py:42
  113.0 3.6 %down_change.3 = (bf16[256,1024]{1,0:T(8,128)(2,1)S(1)}, bf16[256,1024]{1,0:T(8,128)(2,1)S(1)}, bf16[256,1024]{1,0:T(8,128)(2,1)S(1)}) custom-call(bf16[768,1024]{1,0:T(8,128)(2,1)S(1)} %get-tuple-element.29.s_ref, bf16[2,128,2048]{2,1,0:T(8,128)(2,1)S(1)} %get-tuple-element.23.a_ref, bf16[2,128,1024]{2,1,0:T(8,128)(2,1)S(1)} %get-tuple-element.24.g_ref), custom_call_target="tpu_custom_call" | custom-call | flops 402653184 | bytes 3145728 | tf_op jit(solution)/shard_map/down_change/pallas_call | solution.py:305
  116.6 1.4 collective-permute-start.27
  119.3 3.2 %collective-permute-start.22 = (bf16[128,2048]{1,0:T(8,128)(2,1)S(1)}, bf16[128,2048]{1,0:T(8,128)(2,1)S(1)}, u32[]{:S(2)}, u32[]{:S(2)}) collective-permute-start(bf16[128,2048]{1,0:T(8,128)(2,1)S(1)} %add_convert_fusion.2), channel_id=1, source_target_pairs={{0,32},{8,232},{16,48},{24,248},{32,64},{40,8},{48,80},{56,24},{64... | collective-permute-start | bytes 1572872 | tf_op jit(solution)/shard_map/ppermute | solution.py:42
  125.2 5.4 %down_change.2 = (bf16[256,1024]{1,0:T(8,128)(2,1)S(1)}, bf16[256,1024]{1,0:T(8,128)(2,1)S(1)}, bf16[256,1024]{1,0:T(8,128)(2,1)S(1)}, bf16[256,1024]{1,0:T(8,128)(2,1)S(1)}, bf16[256,1024]{1,0:T(8,128)(2,1)S(1)}) custom-call(bf16[1280,1024]{1,0:T(8,128)(2,1)S(1)} %copy-done, bf16[2,128,2048]{2,1,0:T(8,128)(2,1)S(1)} %get-tuple-element.23.a_ref, ...), custom_call_target="tpu_custom_call" | custom-call | flops 671088640 | bytes 5242880 | tf_op jit(solution)/shard_map/down_change/pallas_call | solution.py:305
  130.8 2.6 %collective-permute-start.26 = (bf16[256,1024]{1,0:T(8,128)(2,1)S(1)}, bf16[256,1024]{1,0:T(8,128)(2,1)S(1)}, u32[]{:S(2)}, u32[]{:S(2)}) collective-permute-start(bf16[256,1024]{1,0:T(8,128)(2,1)S(1)} %get-tuple-element.27), channel_id=1, source_target_pairs={{0,6},{1,7},{2,0},{3,1},{4,2},{5,3},{6,4},{7,5},{8,14},{9,15},{10,... | collective-permute-start | bytes 1572872 | tf_op jit(solution)/shard_map/ppermute | solution.py:50
  134.4 1.5 collective-permute-done.29
  136.0 3.9 %collective-permute-start.23 = (bf16[64,2048]{1,0:T(8,128)(2,1)S(1)}, bf16[64,2048]{1,0:T(8,128)(2,1)S(1)}, u32[]{:S(2)}, u32[]{:S(2)}) collective-permute-start(bf16[64,2048]{1,0:T(8,128)(2,1)S(1)} %add_convert_fusion.5), channel_id=1, source_target_pairs={{0,8},{8,0},{16,24},{24,16},{32,40},{40,32},{48,56},{56,48},{64,72... | collective-permute-start | bytes 786440 | tf_op jit(solution)/shard_map/ppermute | solution.py:30
  140.1 1.4 collective-permute-start.31
  141.6 2.7 %collective-permute-start.24 = (bf16[32,2048]{1,0:T(8,128)(2,1)S(1)}, bf16[32,2048]{1,0:T(8,128)(2,1)S(1)}, u32[]{:S(2)}, u32[]{:S(2)}) collective-permute-start(bf16[32,2048]{1,0:T(8,128)(2,1)S(1)} %slice.98), channel_id=1, source_target_pairs={{0,16},{8,24},{16,0},{24,8},{32,48},{40,56},{48,32},{56,40},{64,80... | collective-permute-start | bytes 393224 | tf_op jit(solution)/shard_map/ppermute | solution.py:34
  144.3 2.9 %collective-permute-done.25 = bf16[256,1024]{1,0:T(8,128)(2,1)S(1)} collective-permute-done((bf16[256,1024]{1,0:T(8,128)(2,1)S(1)}, bf16[256,1024]{1,0:T(8,128)(2,1)S(1)}, u32[]{:S(2)}, u32[]{:S(2)}) %collective-permute-start.25) | collective-permute-done | bytes 524320 | tf_op jit(solution)/shard_map/ppermute | solution.py:50
  147.2 12.2 %collective-permute-done.28 = bf16[256,1024]{1,0:T(8,128)(2,1)S(1)} collective-permute-done((bf16[256,1024]{1,0:T(8,128)(2,1)S(1)}, bf16[256,1024]{1,0:T(8,128)(2,1)S(1)}, u32[]{:S(2)}, u32[]{:S(2)}) %collective-permute-start.28) | collective-permute-done | bytes 524320 | tf_op jit(solution)/shard_map/ppermute | solution.py:50
  159.4 2.0 %fusion.13 = (f32[1,256,1024]{2,1,0:T(8,128)}, f32[1,256,1024]{2,1,0:T(8,128)}) fusion(f32[1,256,1024]{2,1,0:T(8,128)S(1)} %copy-done.3, bf16[256,1024]{1,0:T(8,128)(2,1)S(1)} %collective-permute-done.31, bf16[256,1024]{1,0:T(8,128)(2,1)S(1)} %collective-permute-done.28, bf16[256,1024]{1,0:T(8,128)(2,1)S(1)} %collective-permute-done.26, ...), kind=kLoop, calls=%fused_computation.13 | loop fusion | flops 4194304 | bytes 6815744 | tf_op jit(solution)/shard_map/sub | solution.py:350
  (74 shorter events, 19.3 us)
Async XLA Ops:
  1.7 6.2 %collective-permute-start = (bf16[32,2048]{1,0:T(8,128)(2,1)S(1)}, bf16[32,2048]{1,0:T(8,128)(2,1)S(1)}, u32[]{:S(2)}, u32[]{:S(2)}) collective-permute-start(bf16[32,2048]{1,0:T(8,128)(2,1)S(1)} %convert_bitcast_fusion.1.refs_12_), channel_id=1, source_target_pairs={{0,16},{8,24},{16,0},{24,8},{32,48},{40,56},{48,32},{56,40},{64,80... | collective-permute-start | bytes 393224 | tf_op jit(solution)/shard_map/ppermute | solution.py:34
  5.5 6.0 %collective-permute-start.1 = (bf16[32,2048]{1,0:T(8,128)(2,1)S(1)}, bf16[32,2048]{1,0:T(8,128)(2,1)S(1)}, u32[]{:S(2)}, u32[]{:S(2)}) collective-permute-start(bf16[32,2048]{1,0:T(8,128)(2,1)S(1)} %convert_bitcast_fusion.1.refs_12_), channel_id=1, source_target_pairs={{0,8},{8,0},{16,24},{24,16},{32,40},{40,32},{48,56},{56,48},{64,72... | collective-permute-start | bytes 393224 | tf_op jit(solution)/shard_map/ppermute | solution.py:30
  7.9 4.6 %collective-permute-start.2 = (bf16[32,2048]{1,0:T(8,128)(2,1)S(1)}, bf16[32,2048]{1,0:T(8,128)(2,1)S(1)}, u32[]{:S(2)}, u32[]{:S(2)}) collective-permute-start(bf16[32,2048]{1,0:T(8,128)(2,1)S(1)} %collective-permute-done.refs_13_), channel_id=1, source_target_pairs={{0,8},{8,0},{16,24},{24,16},{32,40},{40,32},{48,56},{56,48},{64,72... | collective-permute-start | bytes 393224 | tf_op jit(solution)/shard_map/ppermute | solution.py:30
  12.5 10.8 %collective-permute-start.3 = (bf16[128,2048]{1,0:T(8,128)(2,1)S(1)}, bf16[128,2048]{1,0:T(8,128)(2,1)S(1)}, u32[]{:S(2)}, u32[]{:S(2)}) collective-permute-start(bf16[128,2048]{1,0:T(8,128)(2,1)S(1)} %pad_maximum_fusion), channel_id=1, source_target_pairs={{0,224},{8,40},{16,240},{24,56},{32,0},{40,72},{48,16},{56,88},{64... | collective-permute-start | bytes 1572872 | tf_op jit(solution)/shard_map/ppermute | solution.py:38
  23.3 9.3 %collective-permute-start.5 = (bf16[128,2048]{1,0:T(8,128)(2,1)S(1)}, bf16[128,2048]{1,0:T(8,128)(2,1)}, u32[]{:S(2)}, u32[]{:S(2)}) collective-permute-start(bf16[128,2048]{1,0:T(8,128)(2,1)S(1)} %collective-permute-done.3.refs_8_), channel_id=1, source_target_pairs={{0,224},{8,40},{16,240},{24,56},{32,0},{40,72},{48,16},{56,88},{64... | collective-permute-start | bytes 1572872 | tf_op jit(solution)/shard_map/ppermute | solution.py:38
  24.6 10.7 %collective-permute-start.13 = (bf16[256,1024]{1,0:T(8,128)(2,1)S(1)}, bf16[256,1024]{1,0:T(8,128)(2,1)}, u32[]{:S(2)}, u32[]{:S(2)}) collective-permute-start(bf16[256,1024]{1,0:T(8,128)(2,1)S(1)} %convert_bitcast_fusion.refs_20_), channel_id=1, source_target_pairs={{0,4},{1,5},{2,6},{3,7},{4,0},{5,1},{6,2},{7,3},{8,12},{9,13},{10,... | collective-permute-start | bytes 1572872 | tf_op jit(solution)/shard_map/ppermute | solution.py:50
  27.4 9.2 %collective-permute-start.11 = (bf16[256,1024]{1,0:T(8,128)(2,1)S(1)}, bf16[256,1024]{1,0:T(8,128)(2,1)}, u32[]{:S(2)}, u32[]{:S(2)}) collective-permute-start(bf16[256,1024]{1,0:T(8,128)(2,1)S(1)} %convert_bitcast_fusion.refs_20_), channel_id=1, source_target_pairs={{0,1},{1,0},{2,3},{3,2},{4,5},{5,4},{6,7},{7,6},{8,9},{9,8},{10,11... | collective-permute-start | bytes 1572872 | tf_op jit(solution)/shard_map/ppermute | solution.py:46
  32.6 9.9 %collective-permute-start.7 = (bf16[128,2048]{1,0:T(8,128)(2,1)}, bf16[128,2048]{1,0:T(8,128)(2,1)S(1)}, u32[]{:S(2)}, u32[]{:S(2)}) collective-permute-start(bf16[128,2048]{1,0:T(8,128)(2,1)} %collective-permute-done.5.refs_9_), channel_id=1, source_target_pairs={{0,224},{8,40},{16,240},{24,56},{32,0},{40,72},{48,16},{56,88},{64... | collective-permute-start | bytes 1572872 | tf_op jit(solution)/shard_map/ppermute | solution.py:38
  32.6 16.3 %collective-permute-start.17 = (bf16[256,1024]{1,0:T(8,128)(2,1)S(1)}, bf16[256,1024]{1,0:T(8,128)(2,1)}, u32[]{:S(2)}, u32[]{:S(2)}) collective-permute-start(bf16[256,1024]{1,0:T(8,128)(2,1)S(1)} %convert_bitcast_fusion.refs_20_), channel_id=1, source_target_pairs={{0,2},{1,3},{2,4},{3,5},{4,6},{5,7},{6,0},{7,1},{8,10},{9,11},{10,... | collective-permute-start | bytes 1572872 | tf_op jit(solution)/shard_map/ppermute | solution.py:50
  33.8 15.0 %collective-permute-start.16 = (bf16[256,1024]{1,0:T(8,128)(2,1)S(1)}, bf16[256,1024]{1,0:T(8,128)(2,1)}, u32[]{:S(2)}, u32[]{:S(2)}) collective-permute-start(bf16[256,1024]{1,0:T(8,128)(2,1)S(1)} %convert_bitcast_fusion.refs_20_), channel_id=1, source_target_pairs={{0,6},{1,7},{2,0},{3,1},{4,2},{5,3},{6,4},{7,5},{8,14},{9,15},{10,... | collective-permute-start | bytes 1572872 | tf_op jit(solution)/shard_map/ppermute | solution.py:50
  35.3 20.7 %collective-permute-start.14 = (bf16[256,1024]{1,0:T(8,128)(2,1)}, bf16[256,1024]{1,0:T(8,128)(2,1)}, u32[]{:S(2)}, u32[]{:S(2)}) collective-permute-start(bf16[256,1024]{1,0:T(8,128)(2,1)} %collective-permute-done.13.refs_22_), channel_id=1, source_target_pairs={{0,1},{1,0},{2,3},{3,2},{4,5},{5,4},{6,7},{7,6},{8,9},{9,8},{10,11... | collective-permute-start | bytes 1572872 | tf_op jit(solution)/shard_map/ppermute | solution.py:46
  36.6 23.5 %collective-permute-start.15 = (bf16[256,1024]{1,0:T(8,128)(2,1)}, bf16[256,1024]{1,0:T(8,128)(2,1)}, u32[]{:S(2)}, u32[]{:S(2)}) collective-permute-start(bf16[256,1024]{1,0:T(8,128)(2,1)} %collective-permute-done.11.refs_19_), channel_id=1, source_target_pairs={{0,2},{1,3},{2,4},{3,5},{4,6},{5,7},{6,0},{7,1},{8,10},{9,11},{10,... | collective-permute-start | bytes 1572872 | tf_op jit(solution)/shard_map/ppermute | solution.py:50
  42.5 20.8 %collective-permute-start.9 = (bf16[64,2048]{1,0:T(8,128)(2,1)S(1)}, bf16[64,2048]{1,0:T(8,128)(2,1)S(1)}, u32[]{:S(2)}, u32[]{:S(2)}) collective-permute-start(bf16[64,2048]{1,0:T(8,128)(2,1)S(1)} %slice.61), channel_id=1, source_target_pairs={{0,224},{8,40},{16,240},{24,56},{32,0},{40,72},{48,16},{56,88},{64... | collective-permute-start | bytes 786440 | tf_op jit(solution)/shard_map/ppermute | solution.py:38
  48.9 16.3 %collective-permute-start.12 = (bf16[256,1024]{1,0:T(8,128)(2,1)}, bf16[256,1024]{1,0:T(8,128)(2,1)}, u32[]{:S(2)}, u32[]{:S(2)}) collective-permute-start(bf16[256,1024]{1,0:T(8,128)(2,1)} %collective-permute-done.11.refs_19_), channel_id=1, source_target_pairs={{0,6},{1,7},{2,0},{3,1},{4,2},{5,3},{6,4},{7,5},{8,14},{9,15},{10,... | collective-permute-start | bytes 1572872 | tf_op jit(solution)/shard_map/ppermute | solution.py:50
  48.9 16.3 %collective-permute-start.4 = (bf16[128,2048]{1,0:T(8,128)(2,1)S(1)}, bf16[128,2048]{1,0:T(8,128)(2,1)}, u32[]{:S(2)}, u32[]{:S(2)}) collective-permute-start(bf16[128,2048]{1,0:T(8,128)(2,1)S(1)} %collective-permute-done.3.refs_8_), channel_id=1, source_target_pairs={{0,8},{8,0},{16,24},{24,16},{32,40},{40,32},{48,56},{56,48},{64,72... | collective-permute-start | bytes 1572872 | tf_op jit(solution)/shard_map/ppermute | solution.py:30
  56.0 9.2 %collective-permute-start.6 = (bf16[128,2048]{1,0:T(8,128)(2,1)}, bf16[128,2048]{1,0:T(8,128)(2,1)}, u32[]{:S(2)}, u32[]{:S(2)}) collective-permute-start(bf16[128,2048]{1,0:T(8,128)(2,1)} %collective-permute-done.5.refs_9_), channel_id=1, source_target_pairs={{0,8},{8,0},{16,24},{24,16},{32,40},{40,32},{48,56},{56,48},{64,72... | collective-permute-start | bytes 1572872 | tf_op jit(solution)/shard_map/ppermute | solution.py:30
  60.1 5.1 %collective-permute-start.8 = (bf16[128,2048]{1,0:T(8,128)(2,1)S(1)}, bf16[128,2048]{1,0:T(8,128)(2,1)}, u32[]{:S(2)}, u32[]{:S(2)}) collective-permute-start(bf16[128,2048]{1,0:T(8,128)(2,1)S(1)} %collective-permute-done.7.refs_10_), channel_id=1, source_target_pairs={{0,8},{8,0},{16,24},{24,16},{32,40},{40,32},{48,56},{56,48},{64,72... | collective-permute-start | bytes 1572872 | tf_op jit(solution)/shard_map/ppermute | solution.py:30
  63.3 1.9 %collective-permute-start.10 = (bf16[64,2048]{1,0:T(8,128)(2,1)S(1)}, bf16[64,2048]{1,0:T(8,128)(2,1)}, u32[]{:S(2)}, u32[]{:S(2)}) collective-permute-start(bf16[64,2048]{1,0:T(8,128)(2,1)S(1)} %collective-permute-done.9.refs_11_), channel_id=1, source_target_pairs={{0,8},{8,0},{16,24},{24,16},{32,40},{40,32},{48,56},{56,48},{64,72... | collective-permute-start | bytes 786440 | tf_op jit(solution)/shard_map/ppermute | solution.py:30
  88.7 5.2 %collective-permute-start.18 = (bf16[448,2048]{1,0:T(8,128)(2,1)S(1)}, bf16[448,2048]{1,0:T(8,128)(2,1)S(1)}, u32[]{:S(2)}, u32[]{:S(2)}) collective-permute-start(bf16[448,2048]{1,0:T(8,128)(2,1)S(1)} %up_change.3), channel_id=1, source_target_pairs={{0,8},{8,0},{16,24},{24,16},{32,40},{40,32},{48,56},{56,48},{64,72... | collective-permute-start | bytes 5505032 | tf_op jit(solution)/shard_map/ppermute | solution.py:30
  94.0 6.1 %collective-permute-start.19 = (bf16[64,2048]{1,0:T(8,128)(2,1)S(1)}, bf16[64,2048]{1,0:T(8,128)(2,1)S(1)}, u32[]{:S(2)}, u32[]{:S(2)}) collective-permute-start(bf16[64,2048]{1,0:T(8,128)(2,1)S(1)} %add_convert_fusion.6), channel_id=1, source_target_pairs={{0,32},{8,232},{16,48},{24,248},{32,64},{40,8},{48,80},{56,24},{64... | collective-permute-start | bytes 786440 | tf_op jit(solution)/shard_map/ppermute | solution.py:42
  100.2 9.3 %collective-permute-start.20 = (bf16[128,2048]{1,0:T(8,128)(2,1)S(1)}, bf16[128,2048]{1,0:T(8,128)(2,1)S(1)}, u32[]{:S(2)}, u32[]{:S(2)}) collective-permute-start(bf16[128,2048]{1,0:T(8,128)(2,1)S(1)} %add_convert_fusion.4), channel_id=1, source_target_pairs={{0,32},{8,232},{16,48},{24,248},{32,64},{40,8},{48,80},{56,24},{64... | collective-permute-start | bytes 1572872 | tf_op jit(solution)/shard_map/ppermute | solution.py:42
  109.8 9.3 %collective-permute-start.21 = (bf16[128,2048]{1,0:T(8,128)(2,1)S(1)}, bf16[128,2048]{1,0:T(8,128)(2,1)S(1)}, u32[]{:S(2)}, u32[]{:S(2)}) collective-permute-start(bf16[128,2048]{1,0:T(8,128)(2,1)S(1)} %add_convert_fusion.3), channel_id=1, source_target_pairs={{0,32},{8,232},{16,48},{24,248},{32,64},{40,8},{48,80},{56,24},{64... | collective-permute-start | bytes 1572872 | tf_op jit(solution)/shard_map/ppermute | solution.py:42
  116.6 14.3 %collective-permute-start.27 = (bf16[256,1024]{1,0:T(8,128)(2,1)S(1)}, bf16[256,1024]{1,0:T(8,128)(2,1)S(1)}, u32[]{:S(2)}, u32[]{:S(2)}) collective-permute-start(bf16[256,1024]{1,0:T(8,128)(2,1)S(1)} %get-tuple-element.30), channel_id=1, source_target_pairs={{0,1},{1,0},{2,3},{3,2},{4,5},{5,4},{6,7},{7,6},{8,9},{9,8},{10,11... | collective-permute-start | bytes 1572872 | tf_op jit(solution)/shard_map/ppermute | solution.py:46
  119.3 14.3 %collective-permute-start.22 = (bf16[128,2048]{1,0:T(8,128)(2,1)S(1)}, bf16[128,2048]{1,0:T(8,128)(2,1)S(1)}, u32[]{:S(2)}, u32[]{:S(2)}) collective-permute-start(bf16[128,2048]{1,0:T(8,128)(2,1)S(1)} %add_convert_fusion.2), channel_id=1, source_target_pairs={{0,32},{8,232},{16,48},{24,248},{32,64},{40,8},{48,80},{56,24},{64... | collective-permute-start | bytes 1572872 | tf_op jit(solution)/shard_map/ppermute | solution.py:42
  122.5 13.4 %collective-permute-start.29 = (bf16[256,1024]{1,0:T(8,128)(2,1)S(1)}, bf16[256,1024]{1,0:T(8,128)(2,1)S(1)}, u32[]{:S(2)}, u32[]{:S(2)}) collective-permute-start(bf16[256,1024]{1,0:T(8,128)(2,1)S(1)} %get-tuple-element.32), channel_id=1, source_target_pairs={{0,2},{1,3},{2,4},{3,5},{4,6},{5,7},{6,0},{7,1},{8,10},{9,11},{10,... | collective-permute-start | bytes 1572872 | tf_op jit(solution)/shard_map/ppermute | solution.py:50
  123.8 16.0 %collective-permute-start.30 = (bf16[256,1024]{1,0:T(8,128)(2,1)S(1)}, bf16[256,1024]{1,0:T(8,128)(2,1)S(1)}, u32[]{:S(2)}, u32[]{:S(2)}) collective-permute-start(bf16[256,1024]{1,0:T(8,128)(2,1)S(1)} %get-tuple-element.33), channel_id=1, source_target_pairs={{0,6},{1,7},{2,0},{3,1},{4,2},{5,3},{6,4},{7,5},{8,14},{9,15},{10,... | collective-permute-start | bytes 1572872 | tf_op jit(solution)/shard_map/ppermute | solution.py:50
  130.7 16.5 %collective-permute-start.25 = (bf16[256,1024]{1,0:T(8,128)(2,1)S(1)}, bf16[256,1024]{1,0:T(8,128)(2,1)S(1)}, u32[]{:S(2)}, u32[]{:S(2)}) collective-permute-start(bf16[256,1024]{1,0:T(8,128)(2,1)S(1)} %get-tuple-element.26), channel_id=1, source_target_pairs={{0,2},{1,3},{2,4},{3,5},{4,6},{5,7},{6,0},{7,1},{8,10},{9,11},{10,... | collective-permute-start | bytes 1572872 | tf_op jit(solution)/shard_map/ppermute | solution.py:50
  130.8 16.4 %collective-permute-start.26 = (bf16[256,1024]{1,0:T(8,128)(2,1)S(1)}, bf16[256,1024]{1,0:T(8,128)(2,1)S(1)}, u32[]{:S(2)}, u32[]{:S(2)}) collective-permute-start(bf16[256,1024]{1,0:T(8,128)(2,1)S(1)} %get-tuple-element.27), channel_id=1, source_target_pairs={{0,6},{1,7},{2,0},{3,1},{4,2},{5,3},{6,4},{7,5},{8,14},{9,15},{10,... | collective-permute-start | bytes 1572872 | tf_op jit(solution)/shard_map/ppermute | solution.py:50
  133.7 25.7 %collective-permute-start.28 = (bf16[256,1024]{1,0:T(8,128)(2,1)S(1)}, bf16[256,1024]{1,0:T(8,128)(2,1)S(1)}, u32[]{:S(2)}, u32[]{:S(2)}) collective-permute-start(bf16[256,1024]{1,0:T(8,128)(2,1)S(1)} %add_convert_fusion.1), channel_id=1, source_target_pairs={{0,4},{1,5},{2,6},{3,7},{4,0},{5,1},{6,2},{7,3},{8,12},{9,13},{10,... | collective-permute-start | bytes 1572872 | tf_op jit(solution)/shard_map/ppermute | solution.py:50
  136.0 5.6 %collective-permute-start.23 = (bf16[64,2048]{1,0:T(8,128)(2,1)S(1)}, bf16[64,2048]{1,0:T(8,128)(2,1)S(1)}, u32[]{:S(2)}, u32[]{:S(2)}) collective-permute-start(bf16[64,2048]{1,0:T(8,128)(2,1)S(1)} %add_convert_fusion.5), channel_id=1, source_target_pairs={{0,8},{8,0},{16,24},{24,16},{32,40},{40,32},{48,56},{56,48},{64,72... | collective-permute-start | bytes 786440 | tf_op jit(solution)/shard_map/ppermute | solution.py:30
  140.1 19.3 %collective-permute-start.31 = (bf16[256,1024]{1,0:T(8,128)(2,1)S(1)}, bf16[256,1024]{1,0:T(8,128)(2,1)S(1)}, u32[]{:S(2)}, u32[]{:S(2)}) collective-permute-start(bf16[256,1024]{1,0:T(8,128)(2,1)S(1)} %add_convert_fusion), channel_id=1, source_target_pairs={{0,1},{1,0},{2,3},{3,2},{4,5},{5,4},{6,7},{7,6},{8,9},{9,8},{10,11... | collective-permute-start | bytes 1572872 | tf_op jit(solution)/shard_map/ppermute | solution.py:46
  141.6 19.8 %collective-permute-start.24 = (bf16[32,2048]{1,0:T(8,128)(2,1)S(1)}, bf16[32,2048]{1,0:T(8,128)(2,1)S(1)}, u32[]{:S(2)}, u32[]{:S(2)}) collective-permute-start(bf16[32,2048]{1,0:T(8,128)(2,1)S(1)} %slice.98), channel_id=1, source_target_pairs={{0,16},{8,24},{16,0},{24,8},{32,48},{40,56},{48,32},{56,40},{64,80... | collective-permute-start | bytes 393224 | tf_op jit(solution)/shard_map/ppermute | solution.py:34
  (7 other events, 157.7 us)
where the time goes:
time: 163 us; the launch traced here: 162 us
  waiting for transfers between devices  58.9 us (36%)
  starting transfers between devices  56.7 us (35%)
  Pallas kernels  37.2 us (23%)
  other arithmetic  6.84 us (4%)
    ppermute x10, waiting for transfers between devices, from_x(): return lax.ppermute(a, 'col', [(i, (i - 2 * k) % 8) for i in range(8)])  26.9 us
    pallas_call x1, Pallas kernels, inner_steps(): pl.pallas_call(kernel, out_shape=(jax.ShapeDtypeStruct((2, TOK, FFW), bf1...  19.6 us
    ppermute x8, starting transfers between devices, swap_core(): return lax.ppermute(a, 'row', [(i, i ^ 1) for i in range(32)])  19.3 us
    ppermute x4, waiting for transfers between devices, from_z(): lax.ppermute(a, 'row', [(i, (i + (4 if i % 2 else -4)) % 32) for i in ran...  19 us
    ppermute x10, starting transfers between devices, from_x(): return lax.ppermute(a, 'col', [(i, (i - 2 * k) % 8) for i in range(8)])  12.8 us
    ppermute x4, starting transfers between devices, to_z(): lax.ppermute(a, 'row', [(i, (i + (-4 if i % 2 else 4)) % 32) for i in ran...  12.3 us
    ppermute x4, waiting for transfers between devices, to_z(): lax.ppermute(a, 'row', [(i, (i + (-4 if i % 2 else 4)) % 32) for i in ran...  10.6 us
    pallas_call x2, Pallas kernels, down_change(): pl.pallas_call(kernel, grid=(D // BLK,), out_shape=(jax.ShapeDtypeStruct(...  9.04 us
  transfers between devices with their start and end apart: 32, of which 13 were waited for; matrix products, arithmetic and copies ran while one was open for 4% of the time, Pallas kernels for 8%

commit v1 on v0

--- a/solution.py
+++ b/solution.py
@@ -60,21 +60,34 @@
 DOWN_ORDER = ((1, 1), (2, 1), (3, 1), (0, 1), (0, 0), (1, 0), (2, 0), (3, 0))
 
 
-def gather_up(a):
-    b = swap_yh(a)
-    own = [a, b, swap_core(a), swap_core(b)]
-    now, side = jnp.concatenate(own, 0), []
-    for k in range(3):
-        now = from_z(now)
-        side.append(now)
-    side.append(from_z(now[:64]))
-    return [swap_core(s) for s in side], side, own
-
-
-def gather_down(a):
-    b0 = swap_yl(a)
-    a1, a3, a2 = from_x(a, 1), from_x(a, -1), from_x(a, 2)
-    return [from_x(b0, 1), swap_yl(a2), from_x(b0, -1), b0, a, a1, a2, a3]
+def after(a, *others):
+    def kernel(*refs):
+        pass
+
+    anywhere = pl.BlockSpec(memory_space=pl.ANY)
+    return pl.pallas_call(
+        kernel,
+        out_shape=jax.ShapeDtypeStruct(a.shape, a.dtype),
+        in_specs=[anywhere] * (1 + len(others)),
+        out_specs=anywhere,
+        input_output_aliases={0: 0},
+        name="after",
+    )(a, *others)
+
+
+def gather(up, down):
+    b, d0 = swap_yh(up), swap_yl(down)
+    c2 = from_x(down, 2)
+    own = [up, b, swap_core(up), swap_core(b)]
+    one = from_z(jnp.concatenate(own, 0))
+    one = after(one, c2, d0)
+    c1, c3, d2 = from_x(down, 1), from_x(down, -1), swap_yl(c2)
+    two = from_z(one)
+    two = after(two, c1, c3, d2)
+    d1, d3 = from_x(d0, 1), from_x(d0, -1)
+    three = from_z(two)
+    side = [one, two, three, from_z(three[:64])]
+    return [swap_core(s) for s in side], side, own, [d1, d2, d3, d0, down, c1, c2, c3]
 
 
 def add(*parts):
@@ -84,22 +97,33 @@
     return total
 
 
-def scatter_up(other, keep):
-    got = swap_core(other)
-    p = to_z(add(keep[384:448], got[384:448]).astype(bf16))
-    p = jnp.pad(p, ((0, 64), (0, 0)))
-    for at in (256, 128, 0):
-        p = to_z(add(keep[at : at + 128], got[at : at + 128], p).astype(bf16))
-    away = add(keep[SEND + 64 :], p[64:]).astype(bf16)
-    mine = add(keep[SEND : SEND + 64], p[:64], swap_core(away))
-    return mine[:32] + swap_yh(mine[32:].astype(bf16)).astype(f32)
-
-
-def scatter_down(u1, u2, u3, u0, t0, t1, t2, t3):
+def scatter(v_other, v_keep, v_early, v_late):
+    u1, u2, u3 = v_early
+    u0, t0, t1, t2, t3 = v_late
+    got = swap_core(v_other)
+
+    def side(at, rows, *more):
+        return add(v_keep[at : at + rows], got[at : at + rows], *more).astype(bf16)
+
+    def wide(p):
+        return jnp.pad(p, ((0, 64), (0, 0)))
+
+    r = to_z(side(384, 64))
     p, m, w = from_x(u1, -1), from_x(u3, 1), swap_yl(u2)
+    r = after(r, u1)
+    r = to_z(side(256, 128, wide(r)))
+    r = after(r, p, m, w, t0)
+    r = to_z(side(128, 128, r))
     u0 = add(u0, p, m).astype(bf16)
     t2 = add(t2, w).astype(bf16)
-    return add(t0, from_x(t1, -1), from_x(t3, 1), from_x(t2, -2), swap_yl(u0))
+    p, m = from_x(t1, -1), from_x(t3, 1)
+    r = after(r, p, m)
+    down = add(t0, p, m, from_x(t2, -2), swap_yl(u0))
+    r = to_z(side(0, 128, r))
+    away = add(v_keep[SEND + 64 :], r[64:]).astype(bf16)
+    mine = add(v_keep[SEND : SEND + 64], r[:64], swap_core(away))
+    up = mine[:32] + swap_yh(mine[32:].astype(bf16)).astype(f32)
+    return up, down
 
 
 def hidden_place():
@@ -319,10 +343,8 @@
 
 
 def local(inputs, targets, up_master, up_momentum, down_master, down_momentum):
-    other, side, own = gather_up(up_master[0].astype(bf16))
-    down_pieces = [
-        (a, 0, BLK, BLK * i) for i, a in enumerate(gather_down(down_master[0].astype(bf16)))
-    ]
+    other, side, own, down_blocks = gather(up_master[0].astype(bf16), down_master[0].astype(bf16))
+    down_pieces = [(a, 0, BLK, BLK * i) for i, a in enumerate(down_blocks)]
     up_pieces, at = [], 0
     for a in other + side + own:
         up_pieces.append((a, 0, a.shape[0], at))
@@ -338,12 +360,13 @@
     act, grad_out, grad_pre, up_other, up_keep, down_early, down_late = inner_steps(
         hidden_place(), rel_t, x, t, up_pieces, down_pieces
     )
-    v_early = down_change(down_early, act, grad_out, 0)
-    v_late = down_change(down_late, act, grad_out, EARLY)
-    down_avg = scatter_down(*v_early, *v_late) / 8
-    v_other = up_change(up_other, rel_t, grad_pre, 0)
-    v_keep = up_change(up_keep, rel_t, grad_pre, SEND)
-    up_avg = scatter_up(v_other, v_keep) / 32
+    up_sum, down_sum = scatter(
+        up_change(up_other, rel_t, grad_pre, 0),
+        up_change(up_keep, rel_t, grad_pre, SEND),
+        down_change(down_early, act, grad_out, 0),
+        down_change(down_late, act, grad_out, EARLY),
+    )
+    up_avg, down_avg = up_sum / 32, down_sum / 8
     new_up_momentum = outer_beta * up_momentum + up_avg[None]
     new_up = up_master - outer_rate * (up_avg[None] + outer_beta * new_up_momentum)
     new_down_momentum = outer_beta * down_momentum + down_avg[None]

time: 163 us -> 177 us (1.086)
  local copies, waits for them, and re-layouts: 0.34 us -> 15.4 us
  starting transfers between devices: 56.7 us -> 48.3 us
  other arithmetic: 6.84 us -> 14.2 us
    unnamed x14 -> x72, local copies, waits for them, and re-layouts: 0.04 us -> 13.5 us
    ppermute x4, waiting for transfers between devices: 0.01 us -> 10.4 us  [swap_yl(): return lax.ppermute(a, 'col', [(i, i ^ 1) for i in range(8)])]
    ppermute x4, starting transfers between devices: 12.3 us -> 3.21 us  [to_z(): lax.ppermute(a, 'row', [(i, (i + (-4 if i % 2 else 4)) % 32) for i in ran...]
    ppermute x4, waiting for transfers between devices: 19 us -> 10.3 us  [from_z(): lax.ppermute(a, 'row', [(i, (i + (4 if i % 2 else -4)) % 32) for i in ran...]
    convert_element_type x8, other arithmetic: 2.27 us -> 8.01 us  [the longest x4 4.28 us: side(): return add(v_keep[at:at + rows], got[at:at + rows], *more).astype(bf16)]
    ppermute x4, waiting for transfers between devices: 10.6 us -> 5.48 us  [to_z(): lax.ppermute(a, 'row', [(i, (i + (-4 if i % 2 else 4)) % 32) for i in ran...]
    ppermute x10, starting transfers between devices: 12.8 us -> 15.9 us  [from_x(): return lax.ppermute(a, 'col', [(i, (i - 2 * k) % 8) for i in range(8)])]
    ppermute x4, starting transfers between devices: 5.41 us -> 2.68 us  [swap_yl(): return lax.ppermute(a, 'col', [(i, i ^ 1) for i in range(8)])]
  transfers between devices with their start and end apart: 32 -> 32, of which waited for: 13 -> 10; matrix products, arithmetic and copies ran while one was open for 4% -> 8% of each run, Pallas kernels for 8% -> 8%
where the time goes in v1:
time: 177 us
  waiting for transfers between devices  57.3 us (32%)
  starting transfers between devices  48.3 us (27%)
  Pallas kernels  38.6 us (22%)
  local copies, waits for them, and re-layouts  15.4 us (9%)
  other arithmetic  14.2 us (8%)
  matrix products  2.06 us (1%)
    ppermute x10, waiting for transfers between devices, from_x(): return lax.ppermute(a, 'col', [(i, (i - 2 * k) % 8) for i in range(8)])  27.5 us
    pallas_call x1, Pallas kernels, inner_steps(): pl.pallas_call(kernel, out_shape=(jax.ShapeDtypeStruct((2, TOK, FFW), bf1...  19.9 us
    ppermute x8, starting transfers between devices, swap_core(): return lax.ppermute(a, 'row', [(i, i ^ 1) for i in range(32)])  17.2 us
    ppermute x10, starting transfers between devices, from_x(): return lax.ppermute(a, 'col', [(i, (i - 2 * k) % 8) for i in range(8)])  15.9 us
    unnamed x72, local copies, waits for them, and re-layouts  13.5 us
    ppermute x4, waiting for transfers between devices, swap_yl(): return lax.ppermute(a, 'col', [(i, i ^ 1) for i in range(8)])  10.4 us
    ppermute x4, waiting for transfers between devices, from_z(): lax.ppermute(a, 'row', [(i, (i + (4 if i % 2 else -4)) % 32) for i in ran...  10.3 us
    pallas_call x2, Pallas kernels, down_change(): pl.pallas_call(kernel, grid=(D // BLK,), out_shape=(jax.ShapeDtypeStruct(...  10.1 us
  transfers between devices with their start and end apart: 32, of which 10 were waited for; matrix products, arithmetic and copies ran while one was open for 8% of the time, Pallas kernels for 8%

profile of v1, /device:TPU:1, one launch (start us, length us, event | category | flops | bytes accessed | tf_op | source)
XLA Modules:
  0.0 176.8 jit_solution(1387297004278209954)
XLA Ops:
  1.6 3.8 %collective-permute-start = (bf16[32,2048]{1,0:T(8,128)(2,1)S(1)}, bf16[32,2048]{1,0:T(8,128)(2,1)S(1)}, u32[]{:S(2)}, u32[]{:S(2)}) collective-permute-start(bf16[32,2048]{1,0:T(8,128)(2,1)S(1)} %convert_bitcast_fusion.1.refs_12_), channel_id=1, source_target_pairs={{0,16},{8,24},{16,0},{24,8},{32,48},{40,56},{48,32},{56,40},{64,80... | collective-permute-start | bytes 393224 | tf_op jit(solution)/shard_map/ppermute | solution.py:34
  7.8 3.6 %collective-permute-start.2 = (bf16[32,2048]{1,0:T(8,128)(2,1)S(1)}, bf16[32,2048]{1,0:T(8,128)(2,1)S(1)}, u32[]{:S(2)}, u32[]{:S(2)}) collective-permute-start(bf16[32,2048]{1,0:T(8,128)(2,1)S(1)} %collective-permute-done.refs_13_), channel_id=1, source_target_pairs={{0,8},{8,0},{16,24},{24,16},{32,40},{40,32},{48,56},{56,48},{64,72... | collective-permute-start | bytes 393224 | tf_op jit(solution)/shard_map/ppermute | solution.py:30
  12.8 2.6 %collective-permute-start.4 = (bf16[256,1024]{1,0:T(8,128)(2,1)S(1)}, bf16[256,1024]{1,0:T(8,128)(2,1)}, u32[]{:S(2)}, u32[]{:S(2)}) collective-permute-start(bf16[256,1024]{1,0:T(8,128)(2,1)S(1)} %convert_bitcast_fusion.refs_20_), channel_id=1, source_target_pairs={{0,4},{1,5},{2,6},{3,7},{4,0},{5,1},{6,2},{7,3},{8,12},{9,13},{10,... | collective-permute-start | bytes 1572872 | tf_op jit(solution)/shard_map/ppermute | solution.py:50
  16.1 1.6 collective-permute-start.3
  18.0 2.4 %collective-permute-start.8 = (bf16[256,1024]{1,0:T(8,128)(2,1)S(1)}, bf16[256,1024]{1,0:T(8,128)(2,1)S(1)}, u32[]{:S(2)}, u32[]{:S(2)}) collective-permute-start(bf16[256,1024]{1,0:T(8,128)(2,1)S(1)} %convert_bitcast_fusion.refs_20_), channel_id=1, source_target_pairs={{0,6},{1,7},{2,0},{3,1},{4,2},{5,3},{6,4},{7,5},{8,14},{9,15},{10,... | collective-permute-start | bytes 1572872 | tf_op jit(solution)/shard_map/ppermute | solution.py:50
  20.4 7.7 %collective-permute-done.4.refs_1_.refs_22_ = bf16[256,1024]{1,0:T(8,128)(2,1)} collective-permute-done((bf16[256,1024]{1,0:T(8,128)(2,1)S(1)}, bf16[256,1024]{1,0:T(8,128)(2,1)}, u32[]{:S(2)}, u32[]{:S(2)}) %collective-permute-start.4) | collective-permute-done | bytes 524320 | tf_op jit(solution)/shard_map/ppermute | solution.py:50
  30.1 9.3 %collective-permute-done.9.refs_2_.refs_23_ = bf16[256,1024]{1,0:T(8,128)(2,1)S(1)} collective-permute-done((bf16[256,1024]{1,0:T(8,128)(2,1)S(1)}, bf16[256,1024]{1,0:T(8,128)(2,1)S(1)}, u32[]{:S(2)}, u32[]{:S(2)}) %collective-permute-start.9) | collective-permute-done | bytes 524320 | tf_op jit(solution)/shard_map/ppermute | solution.py:50
  43.4 9.8 %collective-permute-done.12.refs_10_ = bf16[128,2048]{1,0:T(8,128)(2,1)} collective-permute-done((bf16[128,2048]{1,0:T(8,128)(2,1)}, bf16[128,2048]{1,0:T(8,128)(2,1)}, u32[]{:S(2)}, u32[]{:S(2)}) %collective-permute-start.12) | collective-permute-done | bytes 524320 | tf_op jit(solution)/shard_map/ppermute | solution.py:38
  54.4 2.0 %collective-permute-start.16 = (bf16[256,1024]{1,0:T(8,128)(2,1)S(1)}, bf16[256,1024]{1,0:T(8,128)(2,1)}, u32[]{:S(2)}, u32[]{:S(2)}) collective-permute-start(bf16[256,1024]{1,0:T(8,128)(2,1)S(1)} %copy-done.16), channel_id=1, source_target_pairs={{0,6},{1,7},{2,0},{3,1},{4,2},{5,3},{6,4},{7,5},{8,14},{9,15},{10,... | collective-permute-start | bytes 1572872 | tf_op jit(solution)/shard_map/ppermute | solution.py:50
  56.4 6.9 %collective-permute-start.6 = (bf16[128,2048]{1,0:T(8,128)(2,1)}, bf16[128,2048]{1,0:T(8,128)(2,1)}, u32[]{:S(2)}, u32[]{:S(2)}) collective-permute-start(bf16[128,2048]{1,0:T(8,128)(2,1)} %after.5.refs_8_), channel_id=1, source_target_pairs={{0,8},{8,0},{16,24},{24,16},{32,40},{40,32},{48,56},{56,48},{64,72... | collective-permute-start | bytes 1572872 | tf_op jit(solution)/shard_map/ppermute | solution.py:30
  65.6 2.1 %fusion.7.refs_1_.n_ref = bf16[2,1024,128]{2,1,0:T(8,128)(2,1)S(1)} fusion(s32[1024]{0:T(1024)} %add.647, f32[2,128]{1,0:T(2,128)} %add_rsqrt_fusion, bf16[1,1,2,128,1024]{4,3,2,1,0:T(8,128)(2,1)S(1)} %copy-done.13), kind=kOutput, calls=%fused_computation.7 | convolution fusion | flops 538968064 | bytes 1053696 | tf_op jit(solution)/shard_map/de,tnd->ten/dot_general | solution.py:358
  73.6 19.9 %inner_steps.1 = (bf16[2,128,2048]{2,1,0:T(8,128)(2,1)S(1)}, bf16[2,128,1024]{2,1,0:T(8,128)(2,1)S(1)}, bf16[2,128,2048]{2,1,0:T(8,128)(2,1)S(1)}, bf16[448,2048...) custom-call(s32[8]{0:T(128)S(1)} %stack.134.refs_0_, ...), custom_call_target="tpu_custom_call" | custom-call | flops 5000000000 | bytes 25165824 | tf_op jit(solution)/shard_map/inner_steps/pallas_call | solution.py:265
  93.5 3.8 %up_change.3 = bf16[448,2048]{1,0:T(8,128)(2,1)S(1)} custom-call(bf16[448,2048]{1,0:T(8,128)(2,1)S(1)} %get-tuple-element.21.s_ref, bf16[2,1024,128]{2,1,0:T(8,128)(2,1)S(1)} %fusion.7.refs_1_.n_ref, bf16[2,128,2048]{2,1,0:T(8,128)(2,1)S(1)} %get-tuple-element.20.g_ref), custom_call_target="tpu_custom_call" | custom-call | flops 469762048 | bytes 3670016 | tf_op jit(solution)/shard_map/up_change/pallas_call | solution.py:303
  97.3 2.3 %collective-permute-start.18 = (bf16[448,2048]{1,0:T(8,128)(2,1)S(1)}, bf16[448,2048]{1,0:T(8,128)(2,1)S(1)}, u32[]{:S(2)}, u32[]{:S(2)}) collective-permute-start(bf16[448,2048]{1,0:T(8,128)(2,1)S(1)} %up_change.3), channel_id=1, source_target_pairs={{0,8},{8,0},{16,24},{24,16},{32,40},{40,32},{48,56},{56,48},{64,72... | collective-permute-start | bytes 5505032 | tf_op jit(solution)/shard_map/ppermute | solution.py:30
  99.6 4.7 %up_change.2 = bf16[576,2048]{1,0:T(8,128)(2,1)S(1)} custom-call(bf16[576,2048]{1,0:T(8,128)(2,1)S(1)} %get-tuple-element.19.s_ref, bf16[2,1024,128]{2,1,0:T(8,128)(2,1)S(1)} %fusion.7.refs_1_.n_ref, bf16[2,128,2048]{2,1,0:T(8,128)(2,1)S(1)} %get-tuple-element.20.g_ref), custom_call_target="tpu_custom_call" | custom-call | flops 603979776 | bytes 4718592 | tf_op jit(solution)/shard_map/up_change/pallas_call | solution.py:303
  104.4 1.6 collective-permute-start.19
  106.0 4.1 %down_change.2 = (bf16[256,1024]{1,0:T(8,128)(2,1)}, bf16[256,1024]{1,0:T(8,128)(2,1)}, bf16[256,1024]{1,0:T(8,128)(2,1)}) custom-call(bf16[768,1024]{1,0:T(8,128)(2,1)S(1)} %get-tuple-element.22.s_ref, bf16[2,128,2048]{2,1,0:T(8,128)(2,1)S(1)} %get-tuple-element.23.a_ref, bf16[2,128,1024]{2,1,0:T(8,128)(2,1)S(1)} %get-tuple-element.24.g_ref), custom_call_target="tpu_custom_call" | custom-call | flops 402653184 | bytes 3145728 | tf_op jit(solution)/shard_map/down_change/pallas_call | solution.py:329
  110.2 3.2 %collective-permute-start.22 = (bf16[256,1024]{1,0:T(8,128)(2,1)}, bf16[256,1024]{1,0:T(8,128)(2,1)}, u32[]{:S(2)}, u32[]{:S(2)}) collective-permute-start(bf16[256,1024]{1,0:T(8,128)(2,1)} %get-tuple-element.26), channel_id=1, source_target_pairs={{0,6},{1,7},{2,0},{3,1},{4,2},{5,3},{6,4},{7,5},{8,14},{9,15},{10,... | collective-permute-start | bytes 1572872 | tf_op jit(solution)/shard_map/ppermute | solution.py:50
  115.7 1.7 copy-done
  118.5 6.0 %down_change.3 = (bf16[256,1024]{1,0:T(8,128)(2,1)S(1)}, bf16[256,1024]{1,0:T(8,128)(2,1)S(1)}, bf16[256,1024]{1,0:T(8,128)(2,1)}, bf16[256,1024]{1,0:T(8,128)(2,1)S(1)}, bf16[256,1024]{1,0:T(8,128)(2,1)}) custom-call(bf16[1280,1024]{1,0:T(8,128)(2,1)S(1)} %copy-done, bf16[2,128,2048]{2,1,0:T(8,128)(2,1)S(1)} %get-tuple-element.23.a_ref, ...), custom_call_target="tpu_custom_call" | custom-call | flops 671088640 | bytes 5242880 | tf_op jit(solution)/shard_map/down_change/pallas_call | solution.py:329
  126.9 2.7 %collective-permute-start.26 = (bf16[256,1024]{1,0:T(8,128)(2,1)}, bf16[256,1024]{1,0:T(8,128)(2,1)}, u32[]{:S(2)}, u32[]{:S(2)}) collective-permute-start(bf16[256,1024]{1,0:T(8,128)(2,1)} %get-tuple-element.31), channel_id=1, source_target_pairs={{0,6},{1,7},{2,0},{3,1},{4,2},{5,3},{6,4},{7,5},{8,14},{9,15},{10,... | collective-permute-start | bytes 1572872 | tf_op jit(solution)/shard_map/ppermute | solution.py:50
  129.6 1.4 add_convert_fusion.3
  131.7 10.4 %collective-permute-done.25.refs_1_ = bf16[256,1024]{1,0:T(8,128)(2,1)S(1)} collective-permute-done((bf16[256,1024]{1,0:T(8,128)(2,1)}, bf16[256,1024]{1,0:T(8,128)(2,1)S(1)}, u32[]{:S(2)}, u32[]{:S(2)}) %collective-permute-start.25) | collective-permute-done | bytes 524320 | tf_op jit(solution)/shard_map/ppermute | solution.py:50
  143.0 1.5 add_convert_fusion.2
  145.9 1.5 collective-permute-start.30
  147.4 5.5 %collective-permute-done.27 = bf16[128,2048]{1,0:T(8,128)(2,1)S(1)} collective-permute-done((bf16[128,2048]{1,0:T(8,128)(2,1)S(1)}, bf16[128,2048]{1,0:T(8,128)(2,1)S(1)}, u32[]{:S(2)}, u32[]{:S(2)}) %collective-permute-start.27) | collective-permute-done | bytes 524320 | tf_op jit(solution)/shard_map/ppermute | solution.py:42
  152.9 2.6 %collective-permute-start.28 = (bf16[64,2048]{1,0:T(8,128)(2,1)S(1)}, bf16[64,2048]{1,0:T(8,128)(2,1)S(1)}, u32[]{:S(2)}, u32[]{:S(2)}) collective-permute-start(bf16[64,2048]{1,0:T(8,128)(2,1)S(1)} %add_convert_fusion.5), channel_id=1, source_target_pairs={{0,8},{8,0},{16,24},{24,16},{32,40},{40,32},{48,56},{56,48},{64,72... | collective-permute-start | bytes 786440 | tf_op jit(solution)/shard_map/ppermute | solution.py:30
  155.5 1.5 add_convert_fusion
  158.6 2.7 %collective-permute-start.29 = (bf16[32,2048]{1,0:T(8,128)(2,1)S(1)}, bf16[32,2048]{1,0:T(8,128)(2,1)S(1)}, u32[]{:S(2)}, u32[]{:S(2)}) collective-permute-start(bf16[32,2048]{1,0:T(8,128)(2,1)S(1)} %slice.98), channel_id=1, source_target_pairs={{0,16},{8,24},{16,0},{24,8},{32,48},{40,56},{48,32},{56,40},{64,80... | collective-permute-start | bytes 393224 | tf_op jit(solution)/shard_map/ppermute | solution.py:34
  161.3 9.4 %collective-permute-done.31 = bf16[256,1024]{1,0:T(8,128)(2,1)S(1)} collective-permute-done((bf16[256,1024]{1,0:T(8,128)(2,1)S(1)}, bf16[256,1024]{1,0:T(8,128)(2,1)S(1)}, u32[]{:S(2)}, u32[]{:S(2)}) %collective-permute-start.31) | collective-permute-done | bytes 524320 | tf_op jit(solution)/shard_map/ppermute | solution.py:46
  170.7 3.0 %fusion.13 = (f32[1,256,1024]{2,1,0:T(8,128)}, f32[1,256,1024]{2,1,0:T(8,128)}) fusion(f32[1,256,1024]{2,1,0:T(8,128)S(1)} %copy-done.29, bf16[256,1024]{1,0:T(8,128)(2,1)S(1)} %collective-permute-done.31, bf16[256,1024]{1,0:T(8,128)(2,1)S(1)} %collective-permute-done.30, bf16[256,1024]{1,0:T(8,128)(2,1)} %collective-permute-done.26.refs_2_, ...), kind=kLoop, calls=%fused_computation.13 | loop fusion | flops 4194304 | bytes 6815744 | tf_op jit(solution)/shard_map/sub | solution.py:373
  173.7 2.2 %collective-permute-done.29 = bf16[32,2048]{1,0:T(8,128)(2,1)S(1)} collective-permute-done((bf16[32,2048]{1,0:T(8,128)(2,1)S(1)}, bf16[32,2048]{1,0:T(8,128)(2,1)S(1)}, u32[]{:S(2)}, u32[]{:S(2)}) %collective-permute-start.29) | collective-permute-done | bytes 131104 | tf_op jit(solution)/shard_map/ppermute | solution.py:34
  (137 shorter events, 32.0 us)
Async XLA Ops:
  1.6 6.2 %collective-permute-start = (bf16[32,2048]{1,0:T(8,128)(2,1)S(1)}, bf16[32,2048]{1,0:T(8,128)(2,1)S(1)}, u32[]{:S(2)}, u32[]{:S(2)}) collective-permute-start(bf16[32,2048]{1,0:T(8,128)(2,1)S(1)} %convert_bitcast_fusion.1.refs_12_), channel_id=1, source_target_pairs={{0,16},{8,24},{16,0},{24,8},{32,48},{40,56},{48,32},{56,40},{64,80... | collective-permute-start | bytes 393224 | tf_op jit(solution)/shard_map/ppermute | solution.py:34
  5.4 9.9 %collective-permute-start.1 = (bf16[32,2048]{1,0:T(8,128)(2,1)S(1)}, bf16[32,2048]{1,0:T(8,128)(2,1)S(1)}, u32[]{:S(2)}, u32[]{:S(2)}) collective-permute-start(bf16[32,2048]{1,0:T(8,128)(2,1)S(1)} %convert_bitcast_fusion.1.refs_12_), channel_id=1, source_target_pairs={{0,8},{8,0},{16,24},{24,16},{32,40},{40,32},{48,56},{56,48},{64,72... | collective-permute-start | bytes 393224 | tf_op jit(solution)/shard_map/ppermute | solution.py:30
  7.8 7.6 %collective-permute-start.2 = (bf16[32,2048]{1,0:T(8,128)(2,1)S(1)}, bf16[32,2048]{1,0:T(8,128)(2,1)S(1)}, u32[]{:S(2)}, u32[]{:S(2)}) collective-permute-start(bf16[32,2048]{1,0:T(8,128)(2,1)S(1)} %collective-permute-done.refs_13_), channel_id=1, source_target_pairs={{0,8},{8,0},{16,24},{24,16},{32,40},{40,32},{48,56},{56,48},{64,72... | collective-permute-start | bytes 393224 | tf_op jit(solution)/shard_map/ppermute | solution.py:30
  12.7 16.4 %collective-permute-start.5 = (bf16[256,1024]{1,0:T(8,128)(2,1)S(1)}, bf16[256,1024]{1,0:T(8,128)(2,1)S(1)}, u32[]{:S(2)}, u32[]{:S(2)}) collective-permute-start(bf16[256,1024]{1,0:T(8,128)(2,1)S(1)} %convert_bitcast_fusion.refs_20_), channel_id=1, source_target_pairs={{0,1},{1,0},{2,3},{3,2},{4,5},{5,4},{6,7},{7,6},{8,9},{9,8},{10,11... | collective-permute-start | bytes 1572872 | tf_op jit(solution)/shard_map/ppermute | solution.py:46
  12.8 15.2 %collective-permute-start.4 = (bf16[256,1024]{1,0:T(8,128)(2,1)S(1)}, bf16[256,1024]{1,0:T(8,128)(2,1)}, u32[]{:S(2)}, u32[]{:S(2)}) collective-permute-start(bf16[256,1024]{1,0:T(8,128)(2,1)S(1)} %convert_bitcast_fusion.refs_20_), channel_id=1, source_target_pairs={{0,4},{1,5},{2,6},{3,7},{4,0},{5,1},{6,2},{7,3},{8,12},{9,13},{10,... | collective-permute-start | bytes 1572872 | tf_op jit(solution)/shard_map/ppermute | solution.py:50
  16.1 13.0 %collective-permute-start.3 = (bf16[128,2048]{1,0:T(8,128)(2,1)S(1)}, bf16[128,2048]{1,0:T(8,128)(2,1)}, u32[]{:S(2)}, u32[]{:S(2)}) collective-permute-start(bf16[128,2048]{1,0:T(8,128)(2,1)S(1)} %pad_maximum_fusion), channel_id=1, source_target_pairs={{0,224},{8,40},{16,240},{24,56},{32,0},{40,72},{48,16},{56,88},{64... | collective-permute-start | bytes 1572872 | tf_op jit(solution)/shard_map/ppermute | solution.py:38
  17.7 21.8 %collective-permute-start.9 = (bf16[256,1024]{1,0:T(8,128)(2,1)S(1)}, bf16[256,1024]{1,0:T(8,128)(2,1)S(1)}, u32[]{:S(2)}, u32[]{:S(2)}) collective-permute-start(bf16[256,1024]{1,0:T(8,128)(2,1)S(1)} %convert_bitcast_fusion.refs_20_), channel_id=1, source_target_pairs={{0,2},{1,3},{2,4},{3,5},{4,6},{5,7},{6,0},{7,1},{8,10},{9,11},{10,... | collective-permute-start | bytes 1572872 | tf_op jit(solution)/shard_map/ppermute | solution.py:50
  18.0 21.5 %collective-permute-start.8 = (bf16[256,1024]{1,0:T(8,128)(2,1)S(1)}, bf16[256,1024]{1,0:T(8,128)(2,1)S(1)}, u32[]{:S(2)}, u32[]{:S(2)}) collective-permute-start(bf16[256,1024]{1,0:T(8,128)(2,1)S(1)} %convert_bitcast_fusion.refs_20_), channel_id=1, source_target_pairs={{0,6},{1,7},{2,0},{3,1},{4,2},{5,3},{6,4},{7,5},{8,14},{9,15},{10,... | collective-permute-start | bytes 1572872 | tf_op jit(solution)/shard_map/ppermute | solution.py:50
  28.0 12.4 %collective-permute-start.10 = (bf16[256,1024]{1,0:T(8,128)(2,1)}, bf16[256,1024]{1,0:T(8,128)(2,1)S(1)}, u32[]{:S(2)}, u32[]{:S(2)}) collective-permute-start(bf16[256,1024]{1,0:T(8,128)(2,1)} %collective-permute-done.4.refs_1_.refs_22_), channel_id=1, source_target_pairs={{0,1},{1,0},{2,3},{3,2},{4,5},{5,4},{6,7},{7,6},{8,9},{9,8},{10,11... | collective-permute-start | bytes 1572872 | tf_op jit(solution)/shard_map/ppermute | solution.py:46
  29.9 11.1 %collective-permute-start.7 = (bf16[128,2048]{1,0:T(8,128)(2,1)}, bf16[128,2048]{1,0:T(8,128)(2,1)}, u32[]{:S(2)}, u32[]{:S(2)}) collective-permute-start(bf16[128,2048]{1,0:T(8,128)(2,1)} %after.5.refs_8_), channel_id=1, source_target_pairs={{0,224},{8,40},{16,240},{24,56},{32,0},{40,72},{48,16},{56,88},{64... | collective-permute-start | bytes 1572872 | tf_op jit(solution)/shard_map/ppermute | solution.py:38
  41.3 11.9 %collective-permute-start.12 = (bf16[128,2048]{1,0:T(8,128)(2,1)}, bf16[128,2048]{1,0:T(8,128)(2,1)}, u32[]{:S(2)}, u32[]{:S(2)}) collective-permute-start(bf16[128,2048]{1,0:T(8,128)(2,1)} %after.6.refs_9_), channel_id=1, source_target_pairs={{0,224},{8,40},{16,240},{24,56},{32,0},{40,72},{48,16},{56,88},{64... | collective-permute-start | bytes 1572872 | tf_op jit(solution)/shard_map/ppermute | solution.py:38
  42.1 21.2 %collective-permute-start.17 = (bf16[256,1024]{1,0:T(8,128)(2,1)S(1)}, bf16[256,1024]{1,0:T(8,128)(2,1)}, u32[]{:S(2)}, u32[]{:S(2)}) collective-permute-start(bf16[256,1024]{1,0:T(8,128)(2,1)S(1)} %copy-done.16), channel_id=1, source_target_pairs={{0,2},{1,3},{2,4},{3,5},{4,6},{5,7},{6,0},{7,1},{8,10},{9,11},{10,... | collective-permute-start | bytes 1572872 | tf_op jit(solution)/shard_map/ppermute | solution.py:50
  54.2 9.8 %collective-permute-start.14 = (bf16[64,2048]{1,0:T(8,128)(2,1)S(1)}, bf16[64,2048]{1,0:T(8,128)(2,1)S(1)}, u32[]{:S(2)}, u32[]{:S(2)}) collective-permute-start(bf16[64,2048]{1,0:T(8,128)(2,1)S(1)} %slice.61), channel_id=1, source_target_pairs={{0,224},{8,40},{16,240},{24,56},{32,0},{40,72},{48,16},{56,88},{64... | collective-permute-start | bytes 786440 | tf_op jit(solution)/shard_map/ppermute | solution.py:38
  54.4 13.4 %collective-permute-start.16 = (bf16[256,1024]{1,0:T(8,128)(2,1)S(1)}, bf16[256,1024]{1,0:T(8,128)(2,1)}, u32[]{:S(2)}, u32[]{:S(2)}) collective-permute-start(bf16[256,1024]{1,0:T(8,128)(2,1)S(1)} %copy-done.16), channel_id=1, source_target_pairs={{0,6},{1,7},{2,0},{3,1},{4,2},{5,3},{6,4},{7,5},{8,14},{9,15},{10,... | collective-permute-start | bytes 1572872 | tf_op jit(solution)/shard_map/ppermute | solution.py:50
  56.4 11.3 %collective-permute-start.6 = (bf16[128,2048]{1,0:T(8,128)(2,1)}, bf16[128,2048]{1,0:T(8,128)(2,1)}, u32[]{:S(2)}, u32[]{:S(2)}) collective-permute-start(bf16[128,2048]{1,0:T(8,128)(2,1)} %after.5.refs_8_), channel_id=1, source_target_pairs={{0,8},{8,0},{16,24},{24,16},{32,40},{40,32},{48,56},{56,48},{64,72... | collective-permute-start | bytes 1572872 | tf_op jit(solution)/shard_map/ppermute | solution.py:30
  63.3 4.5 %collective-permute-start.11 = (bf16[128,2048]{1,0:T(8,128)(2,1)}, bf16[128,2048]{1,0:T(8,128)(2,1)}, u32[]{:S(2)}, u32[]{:S(2)}) collective-permute-start(bf16[128,2048]{1,0:T(8,128)(2,1)} %after.6.refs_9_), channel_id=1, source_target_pairs={{0,8},{8,0},{16,24},{24,16},{32,40},{40,32},{48,56},{56,48},{64,72... | collective-permute-start | bytes 1572872 | tf_op jit(solution)/shard_map/ppermute | solution.py:30
  63.3 4.5 %collective-permute-start.13 = (bf16[128,2048]{1,0:T(8,128)(2,1)}, bf16[128,2048]{1,0:T(8,128)(2,1)}, u32[]{:S(2)}, u32[]{:S(2)}) collective-permute-start(bf16[128,2048]{1,0:T(8,128)(2,1)} %collective-permute-done.12.refs_10_), channel_id=1, source_target_pairs={{0,8},{8,0},{16,24},{24,16},{32,40},{40,32},{48,56},{56,48},{64,72... | collective-permute-start | bytes 1572872 | tf_op jit(solution)/shard_map/ppermute | solution.py:30
  64.0 3.8 %collective-permute-start.15 = (bf16[64,2048]{1,0:T(8,128)(2,1)S(1)}, bf16[64,2048]{1,0:T(8,128)(2,1)}, u32[]{:S(2)}, u32[]{:S(2)}) collective-permute-start(bf16[64,2048]{1,0:T(8,128)(2,1)S(1)} %collective-permute-done.14.refs_11_), channel_id=1, source_target_pairs={{0,8},{8,0},{16,24},{24,16},{32,40},{40,32},{48,56},{56,48},{64,72... | collective-permute-start | bytes 786440 | tf_op jit(solution)/shard_map/ppermute | solution.py:30
  97.3 7.0 %collective-permute-start.18 = (bf16[448,2048]{1,0:T(8,128)(2,1)S(1)}, bf16[448,2048]{1,0:T(8,128)(2,1)S(1)}, u32[]{:S(2)}, u32[]{:S(2)}) collective-permute-start(bf16[448,2048]{1,0:T(8,128)(2,1)S(1)} %up_change.3), channel_id=1, source_target_pairs={{0,8},{8,0},{16,24},{24,16},{32,40},{40,32},{48,56},{56,48},{64,72... | collective-permute-start | bytes 5505032 | tf_op jit(solution)/shard_map/ppermute | solution.py:30
  104.4 9.1 %collective-permute-start.19 = (bf16[64,2048]{1,0:T(8,128)(2,1)S(1)}, bf16[64,2048]{1,0:T(8,128)(2,1)}, u32[]{:S(2)}, u32[]{:S(2)}) collective-permute-start(bf16[64,2048]{1,0:T(8,128)(2,1)S(1)} %add_convert_fusion.6), channel_id=1, source_target_pairs={{0,32},{8,232},{16,48},{24,248},{32,64},{40,8},{48,80},{56,24},{64... | collective-permute-start | bytes 786440 | tf_op jit(solution)/shard_map/ppermute | solution.py:42
  110.2 16.7 %collective-permute-start.22 = (bf16[256,1024]{1,0:T(8,128)(2,1)}, bf16[256,1024]{1,0:T(8,128)(2,1)}, u32[]{:S(2)}, u32[]{:S(2)}) collective-permute-start(bf16[256,1024]{1,0:T(8,128)(2,1)} %get-tuple-element.26), channel_id=1, source_target_pairs={{0,6},{1,7},{2,0},{3,1},{4,2},{5,3},{6,4},{7,5},{8,14},{9,15},{10,... | collective-permute-start | bytes 1572872 | tf_op jit(solution)/shard_map/ppermute | solution.py:50
  113.4 16.2 %collective-permute-start.23 = (bf16[256,1024]{1,0:T(8,128)(2,1)}, bf16[256,1024]{1,0:T(8,128)(2,1)}, u32[]{:S(2)}, u32[]{:S(2)}) collective-permute-start(bf16[256,1024]{1,0:T(8,128)(2,1)} %get-tuple-element.27), channel_id=1, source_target_pairs={{0,1},{1,0},{2,3},{3,2},{4,5},{5,4},{6,7},{7,6},{8,9},{9,8},{10,11... | collective-permute-start | bytes 1572872 | tf_op jit(solution)/shard_map/ppermute | solution.py:46
  113.5 16.0 %collective-permute-start.21 = (bf16[256,1024]{1,0:T(8,128)(2,1)}, bf16[256,1024]{1,0:T(8,128)(2,1)}, u32[]{:S(2)}, u32[]{:S(2)}) collective-permute-start(bf16[256,1024]{1,0:T(8,128)(2,1)} %get-tuple-element.25.refs_1_), channel_id=1, source_target_pairs={{0,2},{1,3},{2,4},{3,5},{4,6},{5,7},{6,0},{7,1},{8,10},{9,11},{10,... | collective-permute-start | bytes 1572872 | tf_op jit(solution)/shard_map/ppermute | solution.py:50
  114.8 14.7 %collective-permute-start.20 = (bf16[128,2048]{1,0:T(8,128)(2,1)S(1)}, bf16[128,2048]{1,0:T(8,128)(2,1)}, u32[]{:S(2)}, u32[]{:S(2)}) collective-permute-start(bf16[128,2048]{1,0:T(8,128)(2,1)S(1)} %add_convert_fusion.4), channel_id=1, source_target_pairs={{0,32},{8,232},{16,48},{24,248},{32,64},{40,8},{48,80},{56,24},{64... | collective-permute-start | bytes 1572872 | tf_op jit(solution)/shard_map/ppermute | solution.py:42
  126.9 15.3 %collective-permute-start.25 = (bf16[256,1024]{1,0:T(8,128)(2,1)}, bf16[256,1024]{1,0:T(8,128)(2,1)S(1)}, u32[]{:S(2)}, u32[]{:S(2)}) collective-permute-start(bf16[256,1024]{1,0:T(8,128)(2,1)} %get-tuple-element.30), channel_id=1, source_target_pairs={{0,2},{1,3},{2,4},{3,5},{4,6},{5,7},{6,0},{7,1},{8,10},{9,11},{10,... | collective-permute-start | bytes 1572872 | tf_op jit(solution)/shard_map/ppermute | solution.py:50
  126.9 15.3 %collective-permute-start.26 = (bf16[256,1024]{1,0:T(8,128)(2,1)}, bf16[256,1024]{1,0:T(8,128)(2,1)}, u32[]{:S(2)}, u32[]{:S(2)}) collective-permute-start(bf16[256,1024]{1,0:T(8,128)(2,1)} %get-tuple-element.31), channel_id=1, source_target_pairs={{0,6},{1,7},{2,0},{3,1},{4,2},{5,3},{6,4},{7,5},{8,14},{9,15},{10,... | collective-permute-start | bytes 1572872 | tf_op jit(solution)/shard_map/ppermute | solution.py:50
  131.0 11.2 %collective-permute-start.24 = (bf16[128,2048]{1,0:T(8,128)(2,1)S(1)}, bf16[128,2048]{1,0:T(8,128)(2,1)}, u32[]{:S(2)}, u32[]{:S(2)}) collective-permute-start(bf16[128,2048]{1,0:T(8,128)(2,1)S(1)} %add_convert_fusion.3), channel_id=1, source_target_pairs={{0,32},{8,232},{16,48},{24,248},{32,64},{40,8},{48,80},{56,24},{64... | collective-permute-start | bytes 1572872 | tf_op jit(solution)/shard_map/ppermute | solution.py:42
  144.5 8.4 %collective-permute-start.27 = (bf16[128,2048]{1,0:T(8,128)(2,1)S(1)}, bf16[128,2048]{1,0:T(8,128)(2,1)S(1)}, u32[]{:S(2)}, u32[]{:S(2)}) collective-permute-start(bf16[128,2048]{1,0:T(8,128)(2,1)S(1)} %add_convert_fusion.2), channel_id=1, source_target_pairs={{0,32},{8,232},{16,48},{24,248},{32,64},{40,8},{48,80},{56,24},{64... | collective-permute-start | bytes 1572872 | tf_op jit(solution)/shard_map/ppermute | solution.py:42
  145.9 15.4 %collective-permute-start.30 = (bf16[256,1024]{1,0:T(8,128)(2,1)S(1)}, bf16[256,1024]{1,0:T(8,128)(2,1)S(1)}, u32[]{:S(2)}, u32[]{:S(2)}) collective-permute-start(bf16[256,1024]{1,0:T(8,128)(2,1)S(1)} %add_convert_fusion.1), channel_id=1, source_target_pairs={{0,4},{1,5},{2,6},{3,7},{4,0},{5,1},{6,2},{7,3},{8,12},{9,13},{10,... | collective-permute-start | bytes 1572872 | tf_op jit(solution)/shard_map/ppermute | solution.py:50
  152.9 5.5 %collective-permute-start.28 = (bf16[64,2048]{1,0:T(8,128)(2,1)S(1)}, bf16[64,2048]{1,0:T(8,128)(2,1)S(1)}, u32[]{:S(2)}, u32[]{:S(2)}) collective-permute-start(bf16[64,2048]{1,0:T(8,128)(2,1)S(1)} %add_convert_fusion.5), channel_id=1, source_target_pairs={{0,8},{8,0},{16,24},{24,16},{32,40},{40,32},{48,56},{56,48},{64,72... | collective-permute-start | bytes 786440 | tf_op jit(solution)/shard_map/ppermute | solution.py:30
  157.0 13.6 %collective-permute-start.31 = (bf16[256,1024]{1,0:T(8,128)(2,1)S(1)}, bf16[256,1024]{1,0:T(8,128)(2,1)S(1)}, u32[]{:S(2)}, u32[]{:S(2)}) collective-permute-start(bf16[256,1024]{1,0:T(8,128)(2,1)S(1)} %add_convert_fusion), channel_id=1, source_target_pairs={{0,1},{1,0},{2,3},{3,2},{4,5},{5,4},{6,7},{7,6},{8,9},{9,8},{10,11... | collective-permute-start | bytes 1572872 | tf_op jit(solution)/shard_map/ppermute | solution.py:46
  158.6 17.3 %collective-permute-start.29 = (bf16[32,2048]{1,0:T(8,128)(2,1)S(1)}, bf16[32,2048]{1,0:T(8,128)(2,1)S(1)}, u32[]{:S(2)}, u32[]{:S(2)}) collective-permute-start(bf16[32,2048]{1,0:T(8,128)(2,1)S(1)} %slice.98), channel_id=1, source_target_pairs={{0,16},{8,24},{16,0},{24,8},{32,48},{40,56},{48,32},{56,40},{64,80... | collective-permute-start | bytes 393224 | tf_op jit(solution)/shard_map/ppermute | solution.py:34
  (36 other events, 368.7 us)

commit v2 on v1

--- a/solution.py
+++ b/solution.py
@@ -34,6 +34,10 @@
     return lax.ppermute(a, "row", [(i, i ^ 2) for i in range(32)])
 
 
+def swap_both(a):
+    return lax.ppermute(a, "row", [(i, i ^ 3) for i in range(32)])
+
+
 def from_z(a):
     return lax.ppermute(a, "row", [(i, (i + (4 if i % 2 else -4)) % 32) for i in range(32)])
 
@@ -60,34 +64,30 @@
 DOWN_ORDER = ((1, 1), (2, 1), (3, 1), (0, 1), (0, 0), (1, 0), (2, 0), (3, 0))
 
 
-def after(a, *others):
-    def kernel(*refs):
-        pass
-
-    anywhere = pl.BlockSpec(memory_space=pl.ANY)
-    return pl.pallas_call(
-        kernel,
-        out_shape=jax.ShapeDtypeStruct(a.shape, a.dtype),
-        in_specs=[anywhere] * (1 + len(others)),
-        out_specs=anywhere,
-        input_output_aliases={0: 0},
-        name="after",
-    )(a, *others)
-
-
-def gather(up, down):
-    b, d0 = swap_yh(up), swap_yl(down)
-    c2 = from_x(down, 2)
-    own = [up, b, swap_core(up), swap_core(b)]
+def after(*others):
+    total = others[0][:1, :1]
+    for o in others[1:]:
+        total = total + o[:1, :1]
+    return 0 * total
+
+
+def hold(a, *others):
+    return lax.dynamic_update_slice(a, a[:16, :128] + after(*others), (0, 0))
+
+
+def gather(up, down, normed_t):
+    own = [up, swap_yh(up), swap_core(up), swap_both(up)]
+    c1, c3, d0 = from_x(down, 1), from_x(down, -1), swap_yl(down)
     one = from_z(jnp.concatenate(own, 0))
-    one = after(one, c2, d0)
-    c1, c3, d2 = from_x(down, 1), from_x(down, -1), swap_yl(c2)
+    one = hold(one, c1, c3)
+    c2a, c2b = from_x(c1[:128], 1), from_x(c3[128:], -1)
+    d1, d3 = from_x(d0, 1), from_x(d0, -1)
     two = from_z(one)
-    two = after(two, c1, c3, d2)
-    d1, d3 = from_x(d0, 1), from_x(d0, -1)
+    two = hold(two, c2a, c2b, d0, normed_t[0])
+    d2 = swap_yl(jnp.concatenate([c2a, c2b], 0))
     three = from_z(two)
     side = [one, two, three, from_z(three[:64])]
-    return [swap_core(s) for s in side], side, own, [d1, d2, d3, d0, down, c1, c2, c3]
+    return [swap_core(s) for s in side], side, own, [d1, d2, d3, d0, down, c1, c2a, c2b, c3]
 
 
 def add(*parts):
@@ -110,19 +110,19 @@
 
     r = to_z(side(384, 64))
     p, m, w = from_x(u1, -1), from_x(u3, 1), swap_yl(u2)
-    r = after(r, u1)
-    r = to_z(side(256, 128, wide(r)))
-    r = after(r, p, m, w, t0)
-    r = to_z(side(128, 128, r))
+    r = to_z(side(256, 128, wide(r), after(u1)))
     u0 = add(u0, p, m).astype(bf16)
     t2 = add(t2, w).astype(bf16)
+    r = to_z(side(128, 128, r, after(u0, t2)))
+    p, m, w = from_x(t2[:128], -1), from_x(t2[128:], 1), swap_yl(u0)
+    t1 = add(t1, jnp.pad(p, ((0, 128), (0, 0)))).astype(bf16)
+    t3 = add(t3, jnp.pad(m, ((128, 0), (0, 0)))).astype(bf16)
+    r = to_z(side(0, 128, r, after(t1, t3)))
     p, m = from_x(t1, -1), from_x(t3, 1)
-    r = after(r, p, m)
-    down = add(t0, p, m, from_x(t2, -2), swap_yl(u0))
-    r = to_z(side(0, 128, r))
-    away = add(v_keep[SEND + 64 :], r[64:]).astype(bf16)
-    mine = add(v_keep[SEND : SEND + 64], r[:64], swap_core(away))
-    up = mine[:32] + swap_yh(mine[32:].astype(bf16)).astype(f32)
+    down = add(t0, w, p, m)
+    last = [add(v_keep[at : at + 32], r[at - SEND : at - SEND + 32]) for at in range(SEND, SEND + 128, 32)]
+    yh, core, both = [a.astype(bf16) for a in last[1:]]
+    up = add(last[0], swap_yh(yh), swap_core(core), swap_both(both))
     return up, down
 
 
@@ -343,19 +343,24 @@
 
 
 def local(inputs, targets, up_master, up_momentum, down_master, down_momentum):
-    other, side, own, down_blocks = gather(up_master[0].astype(bf16), down_master[0].astype(bf16))
-    down_pieces = [(a, 0, BLK, BLK * i) for i, a in enumerate(down_blocks)]
-    up_pieces, at = [], 0
-    for a in other + side + own:
-        up_pieces.append((a, 0, a.shape[0], at))
-        at += a.shape[0]
-
     x, t = inputs[0, 0], targets[0, 0]
     feats = x.astype(f32)
     square_mean = jnp.mean(feats * feats, axis=-1, keepdims=True)
     normed = (feats * lax.rsqrt(square_mean + norm_eps)).astype(bf16)
     order = feature_order()
     rel_t = jnp.einsum("de,tnd->ten", order, normed, preferred_element_type=f32).astype(bf16)
+
+    other, side, own, down_blocks = gather(
+        up_master[0].astype(bf16), down_master[0].astype(bf16), rel_t
+    )
+    down_pieces, at = [], 0
+    for a in down_blocks:
+        down_pieces.append((a, 0, a.shape[0], at))
+        at += a.shape[0]
+    up_pieces, at = [], 0
+    for a in other + side + own:
+        up_pieces.append((a, 0, a.shape[0], at))
+        at += a.shape[0]
 
     act, grad_out, grad_pre, up_other, up_keep, down_early, down_late = inner_steps(
         hidden_place(), rel_t, x, t, up_pieces, down_pieces

time: 177 us -> 188 us (1.062)
  waiting for transfers between devices: 57.3 us -> 25.9 us
  local copies, waits for them, and re-layouts: 15.4 us -> 35.8 us
  starting transfers between devices: 48.3 us -> 61 us
  between operations: 1.08 us -> 8.42 us
  other arithmetic: 14.2 us -> 17.6 us
    unnamed x72 -> x108, local copies, waits for them, and re-layouts: 13.5 us -> 27.5 us
    ppermute x10 -> x12, waiting for transfers between devices: 27.5 us -> 14.3 us  [from_x(): return lax.ppermute(a, 'col', [(i, (i - 2 * k) % 8) for i in range(8)])]
    ppermute x0 -> x2, starting transfers between devices: none -> 10.6 us  [swap_both(): return lax.ppermute(a, 'row', [(i, i ^ 3) for i in range(32)])]
    ppermute x4, waiting for transfers between devices: 10.4 us -> 0.01 us  [swap_yl(): return lax.ppermute(a, 'col', [(i, i ^ 1) for i in range(8)])]
    ppermute x4, waiting for transfers between devices: 10.3 us -> 0.98 us  [from_z(): lax.ppermute(a, 'row', [(i, (i + (4 if i % 2 else -4)) % 32) for i in ran...]
    slice x1 -> x14, local copies, waits for them, and re-layouts: 0.02 us -> 8.06 us  [the longest x6 3.85 us: after(): total = total + o[:1, :1]]
    ppermute x4, starting transfers between devices: 2.72 us -> 9.84 us  [from_z(): lax.ppermute(a, 'row', [(i, (i + (4 if i % 2 else -4)) % 32) for i in ran...]
    ppermute x8 -> x7, starting transfers between devices: 17.2 us -> 13 us  [swap_core(): return lax.ppermute(a, 'row', [(i, i ^ 1) for i in range(32)])]
  transfers between devices with their start and end apart: 32 -> 35, of which waited for: 10 -> 8; matrix products, arithmetic and copies ran while one was open for 8% -> 12% of each run, Pallas kernels for 8% -> 7%
where the time goes in v2:
time: 188 us; the launch traced here: 187 us
  starting transfers between devices  61 us (32%)
  Pallas kernels  37.1 us (20%)
  local copies, waits for them, and re-layouts  35.8 us (19%)
  waiting for transfers between devices  25.9 us (14%)
  other arithmetic  17.6 us (9%)
  between operations  8.42 us (4%)
    unnamed x108, local copies, waits for them, and re-layouts  27.5 us
    pallas_call x1, Pallas kernels, inner_steps(): pl.pallas_call(kernel, out_shape=(jax.ShapeDtypeStruct((2, TOK, FFW), bf1...  19.4 us
    ppermute x12, starting transfers between devices, from_x(): return lax.ppermute(a, 'col', [(i, (i - 2 * k) % 8) for i in range(8)])  14.9 us
    ppermute x12, waiting for transfers between devices, from_x(): return lax.ppermute(a, 'col', [(i, (i - 2 * k) % 8) for i in range(8)])  14.3 us
    ppermute x7, starting transfers between devices, swap_core(): return lax.ppermute(a, 'row', [(i, i ^ 1) for i in range(32)])  13 us
    ppermute x2, starting transfers between devices, swap_both(): return lax.ppermute(a, 'row', [(i, i ^ 3) for i in range(32)])  10.6 us
    ppermute x4, starting transfers between devices, from_z(): lax.ppermute(a, 'row', [(i, (i + (4 if i % 2 else -4)) % 32) for i in ran...  9.84 us
    pallas_call x2, Pallas kernels, down_change(): pl.pallas_call(kernel, grid=(D // BLK,), out_shape=(jax.ShapeDtypeStruct(...  9.19 us
  transfers between devices with their start and end apart: 35, of which 8 were waited for; matrix products, arithmetic and copies ran while one was open for 12% of the time, Pallas kernels for 7%

profile of v2, /device:TPU:1, one launch (start us, length us, event | category | flops | bytes accessed | tf_op | source)
XLA Modules:
  0.0 187.1 jit_solution(4548999472456714767)
XLA Ops:
  1.7 4.4 %collective-permute-start.2 = (bf16[32,2048]{1,0:T(8,128)(2,1)S(1)}, bf16[32,2048]{1,0:T(8,128)(2,1)S(1)}, u32[]{:S(2)}, u32[]{:S(2)}) collective-permute-start(bf16[32,2048]{1,0:T(8,128)(2,1)S(1)} %convert_bitcast_fusion.1.refs_12_), channel_id=1, source_target_pairs={{0,24},{8,16},{16,8},{24,0},{32,56},{40,48},{48,40},{56,32},{64,88... | collective-permute-start | bytes 393224 | tf_op jit(solution)/shard_map/ppermute | solution.py:38
  6.1 1.8 collective-permute-start
  10.2 2.2 %collective-permute-start.4 = (bf16[256,1024]{1,0:T(8,128)(2,1)S(1)}, bf16[256,1024]{1,0:T(8,128)(2,1)S(1)}, u32[]{:S(2)}, u32[]{:S(2)}) collective-permute-start(bf16[256,1024]{1,0:T(8,128)(2,1)S(1)} %convert_bitcast_fusion.refs_20_), channel_id=1, source_target_pairs={{0,6},{1,7},{2,0},{3,1},{4,2},{5,3},{6,4},{7,5},{8,14},{9,15},{10,... | collective-permute-start | bytes 1572872 | tf_op jit(solution)/shard_map/ppermute | solution.py:54
  12.5 1.6 collective-permute-start.3
  14.5 8.8 %collective-permute-done.5.refs_24_ = bf16[256,1024]{1,0:T(8,128)(2,1)S(1)} collective-permute-done((bf16[256,1024]{1,0:T(8,128)(2,1)S(1)}, bf16[256,1024]{1,0:T(8,128)(2,1)S(1)}, u32[]{:S(2)}, u32[]{:S(2)}) %collective-permute-start.5) | collective-permute-done | bytes 524320 | tf_op jit(solution)/shard_map/ppermute | solution.py:54
  29.4 2.8 %collective-permute-start.8 = (bf16[128,1024]{1,0:T(8,128)(2,1)S(1)}, bf16[128,1024]{1,0:T(8,128)(2,1)S(1)}, u32[]{:S(2)}, u32[]{:S(2)}) collective-permute-start(bf16[128,1024]{1,0:T(8,128)(2,1)S(1)} %slice.144), channel_id=1, source_target_pairs={{0,6},{1,7},{2,0},{3,1},{4,2},{5,3},{6,4},{7,5},{8,14},{9,15},{10,... | collective-permute-start | bytes 786440 | tf_op jit(solution)/shard_map/ppermute | solution.py:54
  39.1 4.0 %collective-permute-start.12 = (bf16[128,2048]{1,0:T(8,128)(2,1)S(1)}, bf16[128,2048]{1,0:T(8,128)(2,1)S(1)}, u32[]{:S(2)}, u32[]{:S(2)}) collective-permute-start(bf16[128,2048]{1,0:T(8,128)(2,1)S(1)} %fusion.18.refs_9_), channel_id=1, source_target_pairs={{0,224},{8,40},{16,240},{24,56},{32,0},{40,72},{48,16},{56,88},{64... | collective-permute-start | bytes 1572872 | tf_op jit(solution)/shard_map/ppermute | solution.py:42
  45.8 4.3 %collective-permute-start.6 = (bf16[128,2048]{1,0:T(8,128)(2,1)}, bf16[128,2048]{1,0:T(8,128)(2,1)}, u32[]{:S(2)}, u32[]{:S(2)}) collective-permute-start(bf16[128,2048]{1,0:T(8,128)(2,1)} %fusion.19.refs_8_), channel_id=1, source_target_pairs={{0,8},{8,0},{16,24},{24,16},{32,40},{40,32},{48,56},{56,48},{64,72... | collective-permute-start | bytes 1572872 | tf_op jit(solution)/shard_map/ppermute | solution.py:30
  51.0 1.6 collective-permute-start.17
  52.6 2.3 %collective-permute-start.11 = (bf16[128,2048]{1,0:T(8,128)(2,1)S(1)}, bf16[128,2048]{1,0:T(8,128)(2,1)}, u32[]{:S(2)}, u32[]{:S(2)}) collective-permute-start(bf16[128,2048]{1,0:T(8,128)(2,1)S(1)} %fusion.18.refs_9_), channel_id=1, source_target_pairs={{0,8},{8,0},{16,24},{24,16},{32,40},{40,32},{48,56},{56,48},{64,72... | collective-permute-start | bytes 1572872 | tf_op jit(solution)/shard_map/ppermute | solution.py:30
  55.7 3.3 %collective-permute-start.14 = (bf16[64,2048]{1,0:T(8,128)(2,1)S(1)}, bf16[64,2048]{1,0:T(8,128)(2,1)S(1)}, u32[]{:S(2)}, u32[]{:S(2)}) collective-permute-start(bf16[64,2048]{1,0:T(8,128)(2,1)S(1)} %slice.151), channel_id=1, source_target_pairs={{0,224},{8,40},{16,240},{24,56},{32,0},{40,72},{48,16},{56,88},{64... | collective-permute-start | bytes 786440 | tf_op jit(solution)/shard_map/ppermute | solution.py:42
  62.3 4.4 %collective-permute-start.15 = (bf16[64,2048]{1,0:T(8,128)(2,1)S(1)}, bf16[64,2048]{1,0:T(8,128)(2,1)S(1)}, u32[]{:S(2)}, u32[]{:S(2)}) collective-permute-start(bf16[64,2048]{1,0:T(8,128)(2,1)S(1)} %collective-permute-done.14.refs_11_), channel_id=1, source_target_pairs={{0,8},{8,0},{16,24},{24,16},{32,40},{40,32},{48,56},{56,48},{64,72... | collective-permute-start | bytes 786440 | tf_op jit(solution)/shard_map/ppermute | solution.py:30
  86.3 19.4 %inner_steps.1 = (bf16[2,128,2048]{2,1,0:T(8,128)(2,1)S(1)}, bf16[2,128,1024]{2,1,0:T(8,128)(2,1)S(1)}, bf16[2,128,2048]{2,1,0:T(8,128)(2,1)S(1)}, bf16[448,2048...) custom-call(s32[8]{0:T(128)S(1)} %stack.134.refs_0_, ...), custom_call_target="tpu_custom_call" | custom-call | flops 5000000000 | bytes 25165824 | tf_op jit(solution)/shard_map/inner_steps/pallas_call | solution.py:265
  105.7 3.8 %up_change.3 = bf16[448,2048]{1,0:T(8,128)(2,1)S(1)} custom-call(bf16[448,2048]{1,0:T(8,128)(2,1)S(1)} %get-tuple-element.21.s_ref, bf16[2,1024,128]{2,1,0:T(8,128)(2,1)S(1)} %fusion.7.refs_1_.n_ref, bf16[2,128,2048]{2,1,0:T(8,128)(2,1)S(1)} %get-tuple-element.20.g_ref), custom_call_target="tpu_custom_call" | custom-call | flops 469762048 | bytes 3670016 | tf_op jit(solution)/shard_map/up_change/pallas_call | solution.py:303
  111.0 4.7 %up_change.2 = bf16[576,2048]{1,0:T(8,128)(2,1)S(1)} custom-call(bf16[576,2048]{1,0:T(8,128)(2,1)S(1)} %get-tuple-element.19.s_ref, bf16[2,1024,128]{2,1,0:T(8,128)(2,1)S(1)} %copy-done.1, bf16[2,128,2048]{2,1,0:T(8,128)(2,1)S(1)} %get-tuple-element.20.g_ref), custom_call_target="tpu_custom_call" | custom-call | flops 603979776 | bytes 4718592 | tf_op jit(solution)/shard_map/up_change/pallas_call | solution.py:303
  117.8 3.8 %down_change.2 = (bf16[256,1024]{1,0:T(8,128)(2,1)}, bf16[256,1024]{1,0:T(8,128)(2,1)S(1)}, bf16[256,1024]{1,0:T(8,128)(2,1)S(1)}) custom-call(bf16[768,1024]{1,0:T(8,128)(2,1)S(1)} %get-tuple-element.22.s_ref, bf16[2,128,2048]{2,1,0:T(8,128)(2,1)S(1)} %get-tuple-element.23.a_ref, bf16[2,128,1024]{2,1,0:T(8,128)(2,1)S(1)} %get-tuple-element.24.g_ref), custom_call_target="tpu_custom_call" | custom-call | flops 402653184 | bytes 3145728 | tf_op jit(solution)/shard_map/down_change/pallas_call | solution.py:329
  125.0 2.8 %collective-permute-start.23 = (bf16[256,1024]{1,0:T(8,128)(2,1)}, bf16[256,1024]{1,0:T(8,128)(2,1)S(1)}, u32[]{:S(2)}, u32[]{:S(2)}) collective-permute-start(bf16[256,1024]{1,0:T(8,128)(2,1)} %copy-done.40), channel_id=1, source_target_pairs={{0,6},{1,7},{2,0},{3,1},{4,2},{5,3},{6,4},{7,5},{8,14},{9,15},{10,... | collective-permute-start | bytes 1572872 | tf_op jit(solution)/shard_map/ppermute | solution.py:54
  127.8 1.8 collective-permute-start.24
  129.6 1.7 copy-done.2
  132.3 5.4 %down_change.3 = (bf16[256,1024]{1,0:T(8,128)(2,1)S(1)}, bf16[256,1024]{1,0:T(8,128)(2,1)S(1)}, bf16[256,1024]{1,0:T(8,128)(2,1)S(1)}, bf16[256,1024]{1,0:T(8,128)(2,1)S(1)}, bf16[256,1024]{1,0:T(8,128)(2,1)S(1)}) custom-call(bf16[1280,1024]{1,0:T(8,128)(2,1)S(1)} %copy-done.2, bf16[2,128,2048]{2,1,0:T(8,128)(2,1)S(1)} %get-tuple-element.23.a_ref, ...), custom_call_target="tpu_custom_call" | custom-call | flops 671088640 | bytes 5242880 | tf_op jit(solution)/shard_map/down_change/pallas_call | solution.py:329
  137.8 2.6 %add_convert_fusion.6 = bf16[128,2048]{1,0:T(8,128)(2,1)} fusion(bf16[448,2048]{1,0:T(8,128)(2,1)} %copy-done.47, bf16[576,2048]{1,0:T(8,128)(2,1)S(1)} %up_change.2, f32[]{:T(128)S(6)} %convert.3, bf16[64,2048]{1,0:T(8,128)(2,1)} %collective-permute-done.20), kind=kLoop, calls=%fused_computation.21 | loop fusion | flops 1835008 | bytes 1835012 | tf_op jit(solution)/shard_map/convert_element_type | solution.py:106
  146.8 2.3 %collective-permute-done.21 = bf16[128,2048]{1,0:T(8,128)(2,1)} collective-permute-done((bf16[128,2048]{1,0:T(8,128)(2,1)}, bf16[128,2048]{1,0:T(8,128)(2,1)}, u32[]{:S(2)}, u32[]{:S(2)}) %collective-permute-start.21) | collective-permute-done | bytes 524320 | tf_op jit(solution)/shard_map/ppermute | solution.py:46
  149.1 2.2 %add_convert_fusion.3 = bf16[128,2048]{1,0:T(8,128)(2,1)} fusion(bf16[128,2048]{1,0:T(8,128)(2,1)} %collective-permute-done.21, bf16[448,2048]{1,0:T(8,128)(2,1)} %copy-done.47, bf16[576,2048]{1,0:T(8,128)(2,1)S(1)} %up_change.2, f32[]{:T(128)S(6)} %convert.4), kind=kLoop, calls=%fused_computation.18 | loop fusion | flops 1835008 | bytes 2097156 | tf_op jit(solution)/shard_map/convert_element_type | solution.py:106
  151.3 1.9 %collective-permute-start.25 = (bf16[128,2048]{1,0:T(8,128)(2,1)}, bf16[128,2048]{1,0:T(8,128)(2,1)}, u32[]{:S(2)}, u32[]{:S(2)}) collective-permute-start(bf16[128,2048]{1,0:T(8,128)(2,1)} %add_convert_fusion.3), channel_id=1, source_target_pairs={{0,32},{8,232},{16,48},{24,248},{32,64},{40,8},{48,80},{56,24},{64... | collective-permute-start | bytes 1572872 | tf_op jit(solution)/shard_map/ppermute | solution.py:46
  154.8 5.5 %collective-permute-done.26 = bf16[128,1024]{1,0:T(8,128)(2,1)S(1)} collective-permute-done((bf16[128,1024]{1,0:T(8,128)(2,1)}, bf16[128,1024]{1,0:T(8,128)(2,1)S(1)}, u32[]{:S(2)}, u32[]{:S(2)}) %collective-permute-start.26) | collective-permute-done | bytes 262176 | tf_op jit(solution)/shard_map/ppermute | solution.py:54
  162.4 1.6 add_convert_fusion
  164.6 2.7 %collective-permute-start.34 = (bf16[256,1024]{1,0:T(8,128)(2,1)}, bf16[256,1024]{1,0:T(8,128)(2,1)S(1)}, u32[]{:S(2)}, u32[]{:S(2)}) collective-permute-start(bf16[256,1024]{1,0:T(8,128)(2,1)} %copy-done.50), channel_id=1, source_target_pairs={{0,6},{1,7},{2,0},{3,1},{4,2},{5,3},{6,4},{7,5},{8,14},{9,15},{10,... | collective-permute-start | bytes 1572872 | tf_op jit(solution)/shard_map/ppermute | solution.py:54
  167.3 5.1 %collective-permute-done.28 = bf16[128,2048]{1,0:T(8,128)(2,1)S(1)} collective-permute-done((bf16[128,2048]{1,0:T(8,128)(2,1)S(1)}, bf16[128,2048]{1,0:T(8,128)(2,1)S(1)}, u32[]{:S(2)}, u32[]{:S(2)}) %collective-permute-start.28) | collective-permute-done | bytes 524320 | tf_op jit(solution)/shard_map/ppermute | solution.py:46
  172.5 2.7 %collective-permute-start.29 = (bf16[32,2048]{1,0:T(8,128)(2,1)S(1)}, bf16[32,2048]{1,0:T(8,128)(2,1)S(1)}, u32[]{:S(2)}, u32[]{:S(2)}) collective-permute-start(bf16[32,2048]{1,0:T(8,128)(2,1)S(1)} %get-tuple-element.38), channel_id=1, source_target_pairs={{0,16},{8,24},{16,0},{24,8},{32,48},{40,56},{48,32},{56,40},{64,80... | collective-permute-start | bytes 393224 | tf_op jit(solution)/shard_map/ppermute | solution.py:34
  175.3 6.2 %collective-permute-start.31 = (bf16[32,2048]{1,0:T(8,128)(2,1)S(1)}, bf16[32,2048]{1,0:T(8,128)(2,1)S(1)}, u32[]{:S(2)}, u32[]{:S(2)}) collective-permute-start(bf16[32,2048]{1,0:T(8,128)(2,1)S(1)} %get-tuple-element.39), channel_id=1, source_target_pairs={{0,24},{8,16},{16,8},{24,0},{32,56},{40,48},{48,40},{56,32},{64,88... | collective-permute-start | bytes 393224 | tf_op jit(solution)/shard_map/ppermute | solution.py:38
  181.5 1.9 %fusion.13 = (f32[1,256,1024]{2,1,0:T(8,128)}, f32[1,256,1024]{2,1,0:T(8,128)}) fusion(f32[1,256,1024]{2,1,0:T(8,128)S(1)} %copy-done.46, bf16[256,1024]{1,0:T(8,128)(2,1)S(1)} %collective-permute-done.34, bf16[256,1024]{1,0:T(8,128)(2,1)S(1)} %collective-permute-done.33, bf16[256,1024]{1,0:T(8,128)(2,1)S(1)} %collective-permute-done.32, ...), kind=kLoop, calls=%fused_computation.13 | loop fusion | flops 3670016 | bytes 6291456 | tf_op jit(solution)/shard_map/sub | solution.py:378
  183.4 2.8 %collective-permute-done.31 = bf16[32,2048]{1,0:T(8,128)(2,1)S(1)} collective-permute-done((bf16[32,2048]{1,0:T(8,128)(2,1)S(1)}, bf16[32,2048]{1,0:T(8,128)(2,1)S(1)}, u32[]{:S(2)}, u32[]{:S(2)}) %collective-permute-start.31) | collective-permute-done | bytes 131104 | tf_op jit(solution)/shard_map/ppermute | solution.py:38
  (192 shorter events, 56.3 us)
Async XLA Ops:
  1.7 8.5 %collective-permute-start.2 = (bf16[32,2048]{1,0:T(8,128)(2,1)S(1)}, bf16[32,2048]{1,0:T(8,128)(2,1)S(1)}, u32[]{:S(2)}, u32[]{:S(2)}) collective-permute-start(bf16[32,2048]{1,0:T(8,128)(2,1)S(1)} %convert_bitcast_fusion.1.refs_12_), channel_id=1, source_target_pairs={{0,24},{8,16},{16,8},{24,0},{32,56},{40,48},{48,40},{56,32},{64,88... | collective-permute-start | bytes 393224 | tf_op jit(solution)/shard_map/ppermute | solution.py:38
  6.1 6.3 %collective-permute-start.1 = (bf16[32,2048]{1,0:T(8,128)(2,1)S(1)}, bf16[32,2048]{1,0:T(8,128)(2,1)S(1)}, u32[]{:S(2)}, u32[]{:S(2)}) collective-permute-start(bf16[32,2048]{1,0:T(8,128)(2,1)S(1)} %convert_bitcast_fusion.1.refs_12_), channel_id=1, source_target_pairs={{0,8},{8,0},{16,24},{24,16},{32,40},{40,32},{48,56},{56,48},{64,72... | collective-permute-start | bytes 393224 | tf_op jit(solution)/shard_map/ppermute | solution.py:30
  6.1 6.4 %collective-permute-start = (bf16[32,2048]{1,0:T(8,128)(2,1)S(1)}, bf16[32,2048]{1,0:T(8,128)(2,1)S(1)}, u32[]{:S(2)}, u32[]{:S(2)}) collective-permute-start(bf16[32,2048]{1,0:T(8,128)(2,1)S(1)} %convert_bitcast_fusion.1.refs_12_), channel_id=1, source_target_pairs={{0,16},{8,24},{16,0},{24,8},{32,48},{40,56},{48,32},{56,40},{64,80... | collective-permute-start | bytes 393224 | tf_op jit(solution)/shard_map/ppermute | solution.py:34
  9.2 25.0 %collective-permute-start.10 = (bf16[256,1024]{1,0:T(8,128)(2,1)S(1)}, bf16[256,1024]{1,0:T(8,128)(2,1)}, u32[]{:S(2)}, u32[]{:S(2)}) collective-permute-start(bf16[256,1024]{1,0:T(8,128)(2,1)S(1)} %convert_bitcast_fusion.refs_20_), channel_id=1, source_target_pairs={{0,1},{1,0},{2,3},{3,2},{4,5},{5,4},{6,7},{7,6},{8,9},{9,8},{10,11... | collective-permute-start | bytes 1572872 | tf_op jit(solution)/shard_map/ppermute | solution.py:50
  9.3 13.9 %collective-permute-start.5 = (bf16[256,1024]{1,0:T(8,128)(2,1)S(1)}, bf16[256,1024]{1,0:T(8,128)(2,1)S(1)}, u32[]{:S(2)}, u32[]{:S(2)}) collective-permute-start(bf16[256,1024]{1,0:T(8,128)(2,1)S(1)} %convert_bitcast_fusion.refs_20_), channel_id=1, source_target_pairs={{0,2},{1,3},{2,4},{3,5},{4,6},{5,7},{6,0},{7,1},{8,10},{9,11},{10,... | collective-permute-start | bytes 1572872 | tf_op jit(solution)/shard_map/ppermute | solution.py:54
  10.2 13.6 %collective-permute-start.4 = (bf16[256,1024]{1,0:T(8,128)(2,1)S(1)}, bf16[256,1024]{1,0:T(8,128)(2,1)S(1)}, u32[]{:S(2)}, u32[]{:S(2)}) collective-permute-start(bf16[256,1024]{1,0:T(8,128)(2,1)S(1)} %convert_bitcast_fusion.refs_20_), channel_id=1, source_target_pairs={{0,6},{1,7},{2,0},{3,1},{4,2},{5,3},{6,4},{7,5},{8,14},{9,15},{10,... | collective-permute-start | bytes 1572872 | tf_op jit(solution)/shard_map/ppermute | solution.py:54
  12.5 13.0 %collective-permute-start.3 = (bf16[128,2048]{1,0:T(8,128)(2,1)S(1)}, bf16[128,2048]{1,0:T(8,128)(2,1)}, u32[]{:S(2)}, u32[]{:S(2)}) collective-permute-start(bf16[128,2048]{1,0:T(8,128)(2,1)S(1)} %pad_maximum_fusion), channel_id=1, source_target_pairs={{0,224},{8,40},{16,240},{24,56},{32,0},{40,72},{48,16},{56,88},{64... | collective-permute-start | bytes 1572872 | tf_op jit(solution)/shard_map/ppermute | solution.py:42
  26.9 12.2 %collective-permute-start.7 = (bf16[128,2048]{1,0:T(8,128)(2,1)}, bf16[128,2048]{1,0:T(8,128)(2,1)S(1)}, u32[]{:S(2)}, u32[]{:S(2)}) collective-permute-start(bf16[128,2048]{1,0:T(8,128)(2,1)} %fusion.19.refs_8_), channel_id=1, source_target_pairs={{0,224},{8,40},{16,240},{24,56},{32,0},{40,72},{48,16},{56,88},{64... | collective-permute-start | bytes 1572872 | tf_op jit(solution)/shard_map/ppermute | solution.py:42
  27.9 7.5 %collective-permute-start.9 = (bf16[128,1024]{1,0:T(8,128)(2,1)S(1)}, bf16[128,1024]{1,0:T(8,128)(2,1)S(1)}, u32[]{:S(2)}, u32[]{:S(2)}) collective-permute-start(bf16[128,1024]{1,0:T(8,128)(2,1)S(1)} %slice.146), channel_id=1, source_target_pairs={{0,2},{1,3},{2,4},{3,5},{4,6},{5,7},{6,0},{7,1},{8,10},{9,11},{10,... | collective-permute-start | bytes 786440 | tf_op jit(solution)/shard_map/ppermute | solution.py:54
  29.4 6.5 %collective-permute-start.8 = (bf16[128,1024]{1,0:T(8,128)(2,1)S(1)}, bf16[128,1024]{1,0:T(8,128)(2,1)S(1)}, u32[]{:S(2)}, u32[]{:S(2)}) collective-permute-start(bf16[128,1024]{1,0:T(8,128)(2,1)S(1)} %slice.144), channel_id=1, source_target_pairs={{0,6},{1,7},{2,0},{3,1},{4,2},{5,3},{6,4},{7,5},{8,14},{9,15},{10,... | collective-permute-start | bytes 786440 | tf_op jit(solution)/shard_map/ppermute | solution.py:54
  39.1 13.5 %collective-permute-start.12 = (bf16[128,2048]{1,0:T(8,128)(2,1)S(1)}, bf16[128,2048]{1,0:T(8,128)(2,1)S(1)}, u32[]{:S(2)}, u32[]{:S(2)}) collective-permute-start(bf16[128,2048]{1,0:T(8,128)(2,1)S(1)} %fusion.18.refs_9_), channel_id=1, source_target_pairs={{0,224},{8,40},{16,240},{24,56},{32,0},{40,72},{48,16},{56,88},{64... | collective-permute-start | bytes 1572872 | tf_op jit(solution)/shard_map/ppermute | solution.py:42
  43.2 11.8 %collective-permute-start.18 = (bf16[256,1024]{1,0:T(8,128)(2,1)}, bf16[256,1024]{1,0:T(8,128)(2,1)S(1)}, u32[]{:S(2)}, u32[]{:S(2)}) collective-permute-start(bf16[256,1024]{1,0:T(8,128)(2,1)} %collective-permute-done.10.refs_19_), channel_id=1, source_target_pairs={{0,2},{1,3},{2,4},{3,5},{4,6},{5,7},{6,0},{7,1},{8,10},{9,11},{10,... | collective-permute-start | bytes 1572872 | tf_op jit(solution)/shard_map/ppermute | solution.py:54
  44.5 14.5 %collective-permute-start.16 = (bf16[256,1024]{1,0:T(8,128)(2,1)}, bf16[256,1024]{1,0:T(8,128)(2,1)S(1)}, u32[]{:S(2)}, u32[]{:S(2)}) collective-permute-start(bf16[256,1024]{1,0:T(8,128)(2,1)} %collective-permute-done.10.refs_19_), channel_id=1, source_target_pairs={{0,6},{1,7},{2,0},{3,1},{4,2},{5,3},{6,4},{7,5},{8,14},{9,15},{10,... | collective-permute-start | bytes 1572872 | tf_op jit(solution)/shard_map/ppermute | solution.py:54
  45.8 21.6 %collective-permute-start.6 = (bf16[128,2048]{1,0:T(8,128)(2,1)}, bf16[128,2048]{1,0:T(8,128)(2,1)}, u32[]{:S(2)}, u32[]{:S(2)}) collective-permute-start(bf16[128,2048]{1,0:T(8,128)(2,1)} %fusion.19.refs_8_), channel_id=1, source_target_pairs={{0,8},{8,0},{16,24},{24,16},{32,40},{40,32},{48,56},{56,48},{64,72... | collective-permute-start | bytes 1572872 | tf_op jit(solution)/shard_map/ppermute | solution.py:30
  51.0 16.5 %collective-permute-start.17 = (bf16[256,1024]{1,0:T(8,128)(2,1)}, bf16[256,1024]{1,0:T(8,128)(2,1)}, u32[]{:S(2)}, u32[]{:S(2)}) collective-permute-start(bf16[256,1024]{1,0:T(8,128)(2,1)} %pad_maximum_fusion.1), channel_id=1, source_target_pairs={{0,1},{1,0},{2,3},{3,2},{4,5},{5,4},{6,7},{7,6},{8,9},{9,8},{10,11... | collective-permute-start | bytes 1572872 | tf_op jit(solution)/shard_map/ppermute | solution.py:50
  52.6 14.9 %collective-permute-start.11 = (bf16[128,2048]{1,0:T(8,128)(2,1)S(1)}, bf16[128,2048]{1,0:T(8,128)(2,1)}, u32[]{:S(2)}, u32[]{:S(2)}) collective-permute-start(bf16[128,2048]{1,0:T(8,128)(2,1)S(1)} %fusion.18.refs_9_), channel_id=1, source_target_pairs={{0,8},{8,0},{16,24},{24,16},{32,40},{40,32},{48,56},{56,48},{64,72... | collective-permute-start | bytes 1572872 | tf_op jit(solution)/shard_map/ppermute | solution.py:30
  55.7 6.6 %collective-permute-start.14 = (bf16[64,2048]{1,0:T(8,128)(2,1)S(1)}, bf16[64,2048]{1,0:T(8,128)(2,1)S(1)}, u32[]{:S(2)}, u32[]{:S(2)}) collective-permute-start(bf16[64,2048]{1,0:T(8,128)(2,1)S(1)} %slice.151), channel_id=1, source_target_pairs={{0,224},{8,40},{16,240},{24,56},{32,0},{40,72},{48,16},{56,88},{64... | collective-permute-start | bytes 786440 | tf_op jit(solution)/shard_map/ppermute | solution.py:42
  59.8 8.8 %collective-permute-start.13 = (bf16[128,2048]{1,0:T(8,128)(2,1)S(1)}, bf16[128,2048]{1,0:T(8,128)(2,1)S(1)}, u32[]{:S(2)}, u32[]{:S(2)}) collective-permute-start(bf16[128,2048]{1,0:T(8,128)(2,1)S(1)} %collective-permute-done.12.refs_10_), channel_id=1, source_target_pairs={{0,8},{8,0},{16,24},{24,16},{32,40},{40,32},{48,56},{56,48},{64,72... | collective-permute-start | bytes 1572872 | tf_op jit(solution)/shard_map/ppermute | solution.py:30
  116.6 21.2 %collective-permute-start.20 = (bf16[64,2048]{1,0:T(8,128)(2,1)}, bf16[64,2048]{1,0:T(8,128)(2,1)}, u32[]{:S(2)}, u32[]{:S(2)}) collective-permute-start(bf16[64,2048]{1,0:T(8,128)(2,1)} %add_convert_fusion.7), channel_id=1, source_target_pairs={{0,32},{8,232},{16,48},{24,248},{32,64},{40,8},{48,80},{56,24},{64... | collective-permute-start | bytes 786440 | tf_op jit(solution)/shard_map/ppermute | solution.py:46
  124.3 18.9 %collective-permute-start.22 = (bf16[256,1024]{1,0:T(8,128)(2,1)}, bf16[256,1024]{1,0:T(8,128)(2,1)}, u32[]{:S(2)}, u32[]{:S(2)}) collective-permute-start(bf16[256,1024]{1,0:T(8,128)(2,1)} %get-tuple-element.25), channel_id=1, source_target_pairs={{0,2},{1,3},{2,4},{3,5},{4,6},{5,7},{6,0},{7,1},{8,10},{9,11},{10,... | collective-permute-start | bytes 1572872 | tf_op jit(solution)/shard_map/ppermute | solution.py:54
  125.0 18.3 %collective-permute-start.23 = (bf16[256,1024]{1,0:T(8,128)(2,1)}, bf16[256,1024]{1,0:T(8,128)(2,1)S(1)}, u32[]{:S(2)}, u32[]{:S(2)}) collective-permute-start(bf16[256,1024]{1,0:T(8,128)(2,1)} %copy-done.40), channel_id=1, source_target_pairs={{0,6},{1,7},{2,0},{3,1},{4,2},{5,3},{6,4},{7,5},{8,14},{9,15},{10,... | collective-permute-start | bytes 1572872 | tf_op jit(solution)/shard_map/ppermute | solution.py:54
  127.8 13.7 %collective-permute-start.24 = (bf16[256,1024]{1,0:T(8,128)(2,1)}, bf16[256,1024]{1,0:T(8,128)(2,1)S(1)}, u32[]{:S(2)}, u32[]{:S(2)}) collective-permute-start(bf16[256,1024]{1,0:T(8,128)(2,1)} %copy-done.41), channel_id=1, source_target_pairs={{0,1},{1,0},{2,3},{3,2},{4,5},{5,4},{6,7},{7,6},{8,9},{9,8},{10,11... | collective-permute-start | bytes 1572872 | tf_op jit(solution)/shard_map/ppermute | solution.py:50
  140.4 8.6 %collective-permute-start.21 = (bf16[128,2048]{1,0:T(8,128)(2,1)}, bf16[128,2048]{1,0:T(8,128)(2,1)}, u32[]{:S(2)}, u32[]{:S(2)}) collective-permute-start(bf16[128,2048]{1,0:T(8,128)(2,1)} %add_convert_fusion.6), channel_id=1, source_target_pairs={{0,32},{8,232},{16,48},{24,248},{32,64},{40,8},{48,80},{56,24},{64... | collective-permute-start | bytes 1572872 | tf_op jit(solution)/shard_map/ppermute | solution.py:46
  143.0 10.3 %collective-permute-start.27 = (bf16[128,1024]{1,0:T(8,128)(2,1)}, bf16[128,1024]{1,0:T(8,128)(2,1)}, u32[]{:S(2)}, u32[]{:S(2)}) collective-permute-start(bf16[128,1024]{1,0:T(8,128)(2,1)} %get-tuple-element.41), channel_id=1, source_target_pairs={{0,6},{1,7},{2,0},{3,1},{4,2},{5,3},{6,4},{7,5},{8,14},{9,15},{10,... | collective-permute-start | bytes 786440 | tf_op jit(solution)/shard_map/ppermute | solution.py:54
  151.3 11.1 %collective-permute-start.25 = (bf16[128,2048]{1,0:T(8,128)(2,1)}, bf16[128,2048]{1,0:T(8,128)(2,1)}, u32[]{:S(2)}, u32[]{:S(2)}) collective-permute-start(bf16[128,2048]{1,0:T(8,128)(2,1)} %add_convert_fusion.3), channel_id=1, source_target_pairs={{0,32},{8,232},{16,48},{24,248},{32,64},{40,8},{48,80},{56,24},{64... | collective-permute-start | bytes 1572872 | tf_op jit(solution)/shard_map/ppermute | solution.py:46
  153.2 7.0 %collective-permute-start.26 = (bf16[128,1024]{1,0:T(8,128)(2,1)}, bf16[128,1024]{1,0:T(8,128)(2,1)S(1)}, u32[]{:S(2)}, u32[]{:S(2)}) collective-permute-start(bf16[128,1024]{1,0:T(8,128)(2,1)} %get-tuple-element.42), channel_id=1, source_target_pairs={{0,2},{1,3},{2,4},{3,5},{4,6},{5,7},{6,0},{7,1},{8,10},{9,11},{10,... | collective-permute-start | bytes 786440 | tf_op jit(solution)/shard_map/ppermute | solution.py:54
  164.0 8.4 %collective-permute-start.28 = (bf16[128,2048]{1,0:T(8,128)(2,1)S(1)}, bf16[128,2048]{1,0:T(8,128)(2,1)S(1)}, u32[]{:S(2)}, u32[]{:S(2)}) collective-permute-start(bf16[128,2048]{1,0:T(8,128)(2,1)S(1)} %add_convert_fusion), channel_id=1, source_target_pairs={{0,32},{8,232},{16,48},{24,248},{32,64},{40,8},{48,80},{56,24},{64... | collective-permute-start | bytes 1572872 | tf_op jit(solution)/shard_map/ppermute | solution.py:46
  164.6 16.8 %collective-permute-start.32 = (bf16[256,1024]{1,0:T(8,128)(2,1)}, bf16[256,1024]{1,0:T(8,128)(2,1)S(1)}, u32[]{:S(2)}, u32[]{:S(2)}) collective-permute-start(bf16[256,1024]{1,0:T(8,128)(2,1)} %copy-done.52), channel_id=1, source_target_pairs={{0,1},{1,0},{2,3},{3,2},{4,5},{5,4},{6,7},{7,6},{8,9},{9,8},{10,11... | collective-permute-start | bytes 1572872 | tf_op jit(solution)/shard_map/ppermute | solution.py:50
  164.6 16.8 %collective-permute-start.33 = (bf16[256,1024]{1,0:T(8,128)(2,1)}, bf16[256,1024]{1,0:T(8,128)(2,1)S(1)}, u32[]{:S(2)}, u32[]{:S(2)}) collective-permute-start(bf16[256,1024]{1,0:T(8,128)(2,1)} %copy-done.51), channel_id=1, source_target_pairs={{0,2},{1,3},{2,4},{3,5},{4,6},{5,7},{6,0},{7,1},{8,10},{9,11},{10,... | collective-permute-start | bytes 1572872 | tf_op jit(solution)/shard_map/ppermute | solution.py:54
  164.6 16.8 %collective-permute-start.34 = (bf16[256,1024]{1,0:T(8,128)(2,1)}, bf16[256,1024]{1,0:T(8,128)(2,1)S(1)}, u32[]{:S(2)}, u32[]{:S(2)}) collective-permute-start(bf16[256,1024]{1,0:T(8,128)(2,1)} %copy-done.50), channel_id=1, source_target_pairs={{0,6},{1,7},{2,0},{3,1},{4,2},{5,3},{6,4},{7,5},{8,14},{9,15},{10,... | collective-permute-start | bytes 1572872 | tf_op jit(solution)/shard_map/ppermute | solution.py:54
  172.5 10.8 %collective-permute-start.29 = (bf16[32,2048]{1,0:T(8,128)(2,1)S(1)}, bf16[32,2048]{1,0:T(8,128)(2,1)S(1)}, u32[]{:S(2)}, u32[]{:S(2)}) collective-permute-start(bf16[32,2048]{1,0:T(8,128)(2,1)S(1)} %get-tuple-element.38), channel_id=1, source_target_pairs={{0,16},{8,24},{16,0},{24,8},{32,48},{40,56},{48,32},{56,40},{64,80... | collective-permute-start | bytes 393224 | tf_op jit(solution)/shard_map/ppermute | solution.py:34
  175.3 10.9 %collective-permute-start.31 = (bf16[32,2048]{1,0:T(8,128)(2,1)S(1)}, bf16[32,2048]{1,0:T(8,128)(2,1)S(1)}, u32[]{:S(2)}, u32[]{:S(2)}) collective-permute-start(bf16[32,2048]{1,0:T(8,128)(2,1)S(1)} %get-tuple-element.39), channel_id=1, source_target_pairs={{0,24},{8,16},{16,8},{24,0},{32,56},{40,48},{48,40},{56,32},{64,88... | collective-permute-start | bytes 393224 | tf_op jit(solution)/shard_map/ppermute | solution.py:38
  (57 other events, 471.1 us)

commit v3 on v2

--- a/solution.py
+++ b/solution.py
@@ -65,9 +65,9 @@
 
 
 def after(*others):
-    total = others[0][:1, :1]
+    total = others[0][:16, :128]
     for o in others[1:]:
-        total = total + o[:1, :1]
+        total = total + o[:16, :128]
     return 0 * total
 
 
@@ -75,7 +75,7 @@
     return lax.dynamic_update_slice(a, a[:16, :128] + after(*others), (0, 0))
 
 
-def gather(up, down, normed_t):
+def gather(up, down):
     own = [up, swap_yh(up), swap_core(up), swap_both(up)]
     c1, c3, d0 = from_x(down, 1), from_x(down, -1), swap_yl(down)
     one = from_z(jnp.concatenate(own, 0))
@@ -83,7 +83,7 @@
     c2a, c2b = from_x(c1[:128], 1), from_x(c3[128:], -1)
     d1, d3 = from_x(d0, 1), from_x(d0, -1)
     two = from_z(one)
-    two = hold(two, c2a, c2b, d0, normed_t[0])
+    two = hold(two, c2a, c2b, d0)
     d2 = swap_yl(jnp.concatenate([c2a, c2b], 0))
     three = from_z(two)
     side = [one, two, three, from_z(three[:64])]
@@ -97,27 +97,27 @@
     return total
 
 
-def scatter(v_other, v_keep, v_early, v_late):
+def scatter(v_other, v_keep, v_early, late_change):
     u1, u2, u3 = v_early
-    u0, t0, t1, t2, t3 = v_late
     got = swap_core(v_other)
 
     def side(at, rows, *more):
         return add(v_keep[at : at + rows], got[at : at + rows], *more).astype(bf16)
 
     def wide(p):
-        return jnp.pad(p, ((0, 64), (0, 0)))
+        return jnp.pad(p, ((0, 128 - p.shape[0]), (0, FFW - p.shape[1])))
 
     r = to_z(side(384, 64))
+    u0, t0, t1, t2, t3 = late_change(r)
     p, m, w = from_x(u1, -1), from_x(u3, 1), swap_yl(u2)
-    r = to_z(side(256, 128, wide(r), after(u1)))
+    r = to_z(side(256, 128, wide(r), wide(after(u1))))
     u0 = add(u0, p, m).astype(bf16)
     t2 = add(t2, w).astype(bf16)
-    r = to_z(side(128, 128, r, after(u0, t2)))
+    r = to_z(side(128, 128, r, wide(after(u0, t2))))
     p, m, w = from_x(t2[:128], -1), from_x(t2[128:], 1), swap_yl(u0)
     t1 = add(t1, jnp.pad(p, ((0, 128), (0, 0)))).astype(bf16)
     t3 = add(t3, jnp.pad(m, ((128, 0), (0, 0)))).astype(bf16)
-    r = to_z(side(0, 128, r, after(t1, t3)))
+    r = to_z(side(0, 128, r, wide(after(t1, t3))))
     p, m = from_x(t1, -1), from_x(t3, 1)
     down = add(t0, w, p, m)
     last = [add(v_keep[at : at + 32], r[at - SEND : at - SEND + 32]) for at in range(SEND, SEND + 128, 32)]
@@ -126,22 +126,21 @@
     return up, down
 
 
-def hidden_place():
+def hidden_place(k):
     col = lax.axis_index("col")
     x, yl = col // 2, col % 2
-    return jnp.stack([((x + dx) % 4) * 2 + (yl + dyl) % 2 for dx, dyl in DOWN_ORDER]).astype(jnp.int32)
-
-
-def feature_order():
+    dx, dyl = DOWN_ORDER[k]
+    return ((x + dx) % 4) * 2 + (yl + dyl) % 2
+
+
+def feature_place():
     row = lax.axis_index("row")
     z, yh, core = row // 4, (row // 2) % 2, row % 2
     sign = 1 - 2 * core
     other, side, own = up_order()
-    first = jnp.stack(
-        [((z + sign * k) % 8) * 4 + ((yh + y) % 2) * 2 + (core + c) % 2 for k, y, c in other + side + own]
-    )
-    place = (first[:, None] * 32 + jnp.arange(32)[None]).reshape(1, D)
-    return (lax.broadcasted_iota(jnp.int32, (D, D), 0) == place).astype(bf16)
+    return [
+        ((z + sign * k + 8) % 8) * 4 + ((yh + y) % 2) * 2 + (core + c) % 2 for k, y, c in other + side + own
+    ]
 
 
 def dot(a, b, dims=((1,), (0,))):
@@ -175,12 +174,42 @@
     return (part_one + part_two + (1 - left * left) * start.astype(f32)).astype(bf16)
 
 
+def prepare(x):
+    def kernel(x_ref, n_ref, t_ref):
+        lane = lax.broadcasted_iota(jnp.int32, (1, D), 1)
+        place = lane
+        for i, first in enumerate(feature_place()):
+            place = jnp.where(lane // 32 == i, first * 32 + lane % 32, place)
+        feats = x_ref[...].astype(f32)
+        square_mean = jnp.mean(feats * feats, axis=-1, keepdims=True)
+        normed = (feats * lax.rsqrt(square_mean + norm_eps)).astype(bf16).reshape(2 * TOK, D)
+        for j in range(D // BLK):
+            cols = slice(j * BLK, j * BLK + BLK)
+            order = lax.broadcasted_iota(jnp.int32, (D, BLK), 0) == place[:, cols]
+            part = dot(normed, order.astype(f32).astype(bf16))
+            for t in range(2):
+                rows = part[t * TOK : t * TOK + TOK]
+                n_ref[t, :, cols] = rows.astype(bf16)
+                t_ref[t, cols, :] = rows.T.astype(bf16)
+
+    return pl.pallas_call(
+        kernel,
+        out_shape=(
+            jax.ShapeDtypeStruct((2, TOK, D), bf16),
+            jax.ShapeDtypeStruct((2, D, TOK), bf16),
+        ),
+        compiler_params=pltpu.CompilerParams(vmem_limit_bytes=12 * 1024 * 1024),
+        cost_estimate=pl.CostEstimate(flops=2 * 10**8, bytes_accessed=2**21, transcendentals=0),
+        name="prepare",
+    )(x)
+
+
 def inner_kernel(up_pieces, down_pieces, *refs):
     count = len(up_pieces) + len(down_pieces)
-    place_ref, nt_ref, x_ref, t_ref = refs[:4]
+    n_ref, nt_ref, x_ref, t_ref = refs[:4]
     pieces = refs[4 : 4 + count]
     act_ref, g_ref, gp_ref, send_ref, keep_ref, early_ref, late_ref = refs[4 + count : 11 + count]
-    su, sd, w1u, w1d, pre_ref, n_ref, sem, out_sem = refs[11 + count :]
+    su, sd, w1u, w1d, pre_ref, place_ref, sem, out_sem = refs[11 + count :]
 
     up_copies, down_copies = [], []
     for i, (start, rows, at) in enumerate(up_pieces):
@@ -194,8 +223,8 @@
         )
     for c in up_copies + down_copies:
         c.start()
-    for t in range(2):
-        n_ref[t] = nt_ref[t].T
+    for k in range(8):
+        place_ref[k] = hidden_place(k)
     for c in up_copies:
         c.wait()
 
@@ -254,9 +283,9 @@
         c.wait()
 
 
-def inner_steps(place, normed_t, x, t, up_pieces, down_pieces):
+def inner_steps(normed, normed_t, x, t, up_pieces, down_pieces):
     vmem, hbm = pl.BlockSpec(memory_space=pltpu.VMEM), pl.BlockSpec(memory_space=pl.ANY)
-    far = pl.BlockSpec(memory_space=pltpu.HBM)
+    far = pl.BlockSpec(memory_space=pl.ANY)
     pieces = [p[0] for p in up_pieces + down_pieces]
 
     def kernel(*refs):
@@ -273,7 +302,7 @@
             jax.ShapeDtypeStruct((EARLY, D), bf16),
             jax.ShapeDtypeStruct((LATE, D), bf16),
         ),
-        in_specs=[pl.BlockSpec(memory_space=pltpu.SMEM)] + [vmem] * 3 + [far] * len(pieces),
+        in_specs=[vmem] * 4 + [far] * len(pieces),
         out_specs=(vmem, vmem, vmem, hbm, hbm, hbm, hbm),
         scratch_shapes=[
             pltpu.VMEM((D, FFW), bf16),
@@ -281,14 +310,14 @@
             pltpu.VMEM((D, BLK), bf16),
             pltpu.VMEM((FFW, D), bf16),
             pltpu.VMEM((TOK, FFW), f32),
-            pltpu.VMEM((2, TOK, D), bf16),
+            pltpu.SMEM((8,), jnp.int32),
             pltpu.SemaphoreType.DMA((len(pieces),)),
             pltpu.SemaphoreType.DMA((4,)),
         ],
-        compiler_params=pltpu.CompilerParams(vmem_limit_bytes=36 * 1024 * 1024),
+        compiler_params=pltpu.CompilerParams(vmem_limit_bytes=20 * 1024 * 1024),
         cost_estimate=pl.CostEstimate(flops=5 * 10**9, bytes_accessed=24 * 2**20, transcendentals=0),
         name="inner_steps",
-    )(place, normed_t, x, t, *pieces)
+    )(normed, normed_t, x, t, *pieces)
 
 
 def up_change(start, normed_t, grad_pre, first):
@@ -310,16 +339,17 @@
             pl.BlockSpec((2, TOK, wide), lambda j: (0, 0, j)),
         ],
         out_specs=pl.BlockSpec((rows, wide), lambda j: (0, j)),
-        compiler_params=pltpu.CompilerParams(vmem_limit_bytes=24 * 1024 * 1024),
+        compiler_params=pltpu.CompilerParams(vmem_limit_bytes=10 * 1024 * 1024),
         cost_estimate=pl.CostEstimate(flops=4 * rows * TOK * FFW, bytes_accessed=4 * rows * FFW, transcendentals=0),
         name="up_change",
     )(start, normed_t, grad_pre)
 
 
-def down_change(start, act, grad_out, first):
+def down_change(start, act, grad_out, first, *awaited):
     rows = start.shape[0]
 
-    def kernel(s_ref, a_ref, g_ref, *o_refs):
+    def kernel(s_ref, a_ref, g_ref, *refs):
+        o_refs = refs[len(awaited) :]
         one = dot(a_ref[0, :, pl.ds(first, rows)], g_ref[0], ((0,), (0,)))
         two = dot(a_ref[1, :, pl.ds(first, rows)], g_ref[1], ((0,), (0,)))
         change = change_of(s_ref[...], one, two, hidden_scale)
@@ -334,24 +364,20 @@
             pl.BlockSpec((rows, BLK), lambda j: (0, j)),
             pl.BlockSpec((2, TOK, FFW), lambda j: (0, 0, 0)),
             pl.BlockSpec((2, TOK, BLK), lambda j: (0, 0, j)),
-        ],
+        ]
+        + [pl.BlockSpec(memory_space=pl.ANY)] * len(awaited),
         out_specs=(pl.BlockSpec((BLK, BLK), lambda j: (0, j)),) * (rows // BLK),
-        compiler_params=pltpu.CompilerParams(vmem_limit_bytes=24 * 1024 * 1024),
+        compiler_params=pltpu.CompilerParams(vmem_limit_bytes=10 * 1024 * 1024),
         cost_estimate=pl.CostEstimate(flops=4 * rows * TOK * D, bytes_accessed=4 * rows * D, transcendentals=0),
         name="down_change",
-    )(start, act, grad_out)
+    )(start, act, grad_out, *awaited)
 
 
 def local(inputs, targets, up_master, up_momentum, down_master, down_momentum):
     x, t = inputs[0, 0], targets[0, 0]
-    feats = x.astype(f32)
-    square_mean = jnp.mean(feats * feats, axis=-1, keepdims=True)
-    normed = (feats * lax.rsqrt(square_mean + norm_eps)).astype(bf16)
-    order = feature_order()
-    rel_t = jnp.einsum("de,tnd->ten", order, normed, preferred_element_type=f32).astype(bf16)
-
+    rel, rel_t = prepare(x)
     other, side, own, down_blocks = gather(
-        up_master[0].astype(bf16), down_master[0].astype(bf16), rel_t
+        up_master[0].astype(bf16), down_master[0].astype(bf16)
     )
     down_pieces, at = [], 0
     for a in down_blocks:
@@ -363,13 +389,13 @@
         at += a.shape[0]
 
     act, grad_out, grad_pre, up_other, up_keep, down_early, down_late = inner_steps(
-        hidden_place(), rel_t, x, t, up_pieces, down_pieces
+        rel, rel_t, x, t, up_pieces, down_pieces
     )
     up_sum, down_sum = scatter(
         up_change(up_other, rel_t, grad_pre, 0),
         up_change(up_keep, rel_t, grad_pre, SEND),
         down_change(down_early, act, grad_out, 0),
-        down_change(down_late, act, grad_out, EARLY),
+        lambda r: down_change(down_late, act, grad_out, EARLY, r),
     )
     up_avg, down_avg = up_sum / 32, down_sum / 8
     new_up_momentum = outer_beta * up_momentum + up_avg[None]

time: 188 us -> 144 us (0.77)
  local copies, waits for them, and re-layouts: 35.8 us -> 0.13 us
  waiting for transfers between devices: 25.9 us -> 39.6 us
  other arithmetic: 17.6 us -> 6.63 us
  between operations: 8.42 us -> 1 us
  starting transfers between devices: 61 us -> 59.1 us
    unnamed x108 -> x12, local copies, waits for them, and re-layouts: 27.5 us -> 0.04 us
    ppermute x4, starting transfers between devices: 9.84 us -> 1.63 us  [from_z(): lax.ppermute(a, 'row', [(i, (i + (4 if i % 2 else -4)) % 32) for i in ran...]
    slice x11 -> x0, local copies, waits for them, and re-layouts: 7.2 us -> none  [the longest x6 3.85 us: after(): total = total + o[:1, :1]]
    convert_element_type x4, other arithmetic: 7.36 us -> 0.72 us  [side(): return add(v_keep[at:at + rows], got[at:at + rows], *more).astype(bf16)]
    ppermute x4, waiting for transfers between devices: 0.01 us -> 5.15 us  [swap_yl(): return lax.ppermute(a, 'col', [(i, i ^ 1) for i in range(8)])]
    ppermute x7, starting transfers between devices: 13 us -> 17.8 us  [swap_core(): return lax.ppermute(a, 'row', [(i, i ^ 1) for i in range(32)])]
    ppermute x4, waiting for transfers between devices: 0.98 us -> 5.65 us  [from_z(): lax.ppermute(a, 'row', [(i, (i + (4 if i % 2 else -4)) % 32) for i in ran...]
    ppermute x12, waiting for transfers between devices: 14.3 us -> 17.6 us  [from_x(): return lax.ppermute(a, 'col', [(i, (i - 2 * k) % 8) for i in range(8)])]
  transfers between devices with their start and end apart: 35 -> 35, of which waited for: 8 -> 13; matrix products, arithmetic and copies ran while one was open for 12% -> 3% of each run, Pallas kernels for 7% -> 10%
where the time goes in v3:
time: 144 us
  starting transfers between devices  59.1 us (41%)
  waiting for transfers between devices  39.6 us (28%)
  Pallas kernels  37.4 us (26%)
  other arithmetic  6.63 us (5%)
    pallas_call x1, Pallas kernels, inner_steps(): pl.pallas_call(kernel, out_shape=(jax.ShapeDtypeStruct((2, TOK, FFW), bf1...  18.9 us
    ppermute x7, starting transfers between devices, swap_core(): return lax.ppermute(a, 'row', [(i, i ^ 1) for i in range(32)])  17.8 us
    ppermute x12, waiting for transfers between devices, from_x(): return lax.ppermute(a, 'col', [(i, (i - 2 * k) % 8) for i in range(8)])  17.6 us
    ppermute x12, starting transfers between devices, from_x(): return lax.ppermute(a, 'col', [(i, (i - 2 * k) % 8) for i in range(8)])  14.4 us
    pallas_call x2, Pallas kernels, down_change(): pl.pallas_call(kernel, grid=(D // BLK,), out_shape=(jax.ShapeDtypeStruct(...  9 us
    ppermute x2, starting transfers between devices, swap_both(): return lax.ppermute(a, 'row', [(i, i ^ 3) for i in range(32)])  8.98 us
    pallas_call x2, Pallas kernels, up_change(): pl.pallas_call(kernel, grid=(FFW // wide,), out_shape=jax.ShapeDtypeStruc...  8.51 us
    ppermute x4, starting transfers between devices, swap_yl(): return lax.ppermute(a, 'col', [(i, i ^ 1) for i in range(8)])  6.51 us
  transfers between devices with their start and end apart: 35, of which 13 were waited for; matrix products, arithmetic and copies ran while one was open for 3% of the time, Pallas kernels for 10%

profile of v3, /device:TPU:1, one launch (start us, length us, event | category | flops | bytes accessed | tf_op | source)
XLA Modules:
  0.0 143.8 jit_solution(1153173986989383170)
XLA Ops:
  1.6 4.4 %collective-permute-start.2 = (bf16[32,2048]{1,0:T(8,128)(2,1)S(1)}, bf16[32,2048]{1,0:T(8,128)(2,1)S(1)}, u32[]{:S(2)}, u32[]{:S(2)}) collective-permute-start(bf16[32,2048]{1,0:T(8,128)(2,1)S(1)} %convert_bitcast_fusion.1.refs_12_), channel_id=1, source_target_pairs={{0,24},{8,16},{16,8},{24,0},{32,56},{40,48},{48,40},{56,32},{64,88... | collective-permute-start | bytes 393224 | tf_op jit(solution)/shard_map/ppermute | solution.py:38
  6.0 1.8 %collective-permute-start = (bf16[32,2048]{1,0:T(8,128)(2,1)S(1)}, bf16[32,2048]{1,0:T(8,128)(2,1)S(1)}, u32[]{:S(2)}, u32[]{:S(2)}) collective-permute-start(bf16[32,2048]{1,0:T(8,128)(2,1)S(1)} %convert_bitcast_fusion.1.refs_12_), channel_id=1, source_target_pairs={{0,16},{8,24},{16,0},{24,8},{32,48},{40,56},{48,32},{56,40},{64,80... | collective-permute-start | bytes 393224 | tf_op jit(solution)/shard_map/ppermute | solution.py:34
  9.2 2.7 %collective-permute-start.4 = (bf16[256,1024]{1,0:T(8,128)(2,1)S(1)}, bf16[256,1024]{1,0:T(8,128)(2,1)S(1)}, u32[]{:S(2)}, u32[]{:S(2)}) collective-permute-start(bf16[256,1024]{1,0:T(8,128)(2,1)S(1)} %convert_bitcast_fusion.refs_20_), channel_id=1, source_target_pairs={{0,6},{1,7},{2,0},{3,1},{4,2},{5,3},{6,4},{7,5},{8,14},{9,15},{10,... | collective-permute-start | bytes 1572872 | tf_op jit(solution)/shard_map/ppermute | solution.py:54
  13.9 1.9 %collective-permute-start.10 = (bf16[256,1024]{1,0:T(8,128)(2,1)S(1)}, bf16[256,1024]{1,0:T(8,128)(2,1)S(1)}, u32[]{:S(2)}, u32[]{:S(2)}) collective-permute-start(bf16[256,1024]{1,0:T(8,128)(2,1)S(1)} %convert_bitcast_fusion.refs_20_), channel_id=1, source_target_pairs={{0,1},{1,0},{2,3},{3,2},{4,5},{5,4},{6,7},{7,6},{8,9},{9,8},{10,11... | collective-permute-start | bytes 1572872 | tf_op jit(solution)/shard_map/ppermute | solution.py:50
  15.7 7.3 %collective-permute-done.5.refs_24_ = bf16[256,1024]{1,0:T(8,128)(2,1)S(1)} collective-permute-done((bf16[256,1024]{1,0:T(8,128)(2,1)S(1)}, bf16[256,1024]{1,0:T(8,128)(2,1)S(1)}, u32[]{:S(2)}, u32[]{:S(2)}) %collective-permute-start.5) | collective-permute-done | bytes 524320 | tf_op jit(solution)/shard_map/ppermute | solution.py:54
  25.8 1.5 %collective-permute-start.8 = (bf16[128,1024]{1,0:T(8,128)(2,1)S(1)}, bf16[128,1024]{1,0:T(8,128)(2,1)S(1)}, u32[]{:S(2)}, u32[]{:S(2)}) collective-permute-start(bf16[128,1024]{1,0:T(8,128)(2,1)S(1)} %slice.136), channel_id=1, source_target_pairs={{0,6},{1,7},{2,0},{3,1},{4,2},{5,3},{6,4},{7,5},{8,14},{9,15},{10,... | collective-permute-start | bytes 786440 | tf_op jit(solution)/shard_map/ppermute | solution.py:54
  27.4 3.7 %collective-permute-done.9.refs_23_ = bf16[128,1024]{1,0:T(8,128)(2,1)S(1)} collective-permute-done((bf16[128,1024]{1,0:T(8,128)(2,1)S(1)}, bf16[128,1024]{1,0:T(8,128)(2,1)S(1)}, u32[]{:S(2)}, u32[]{:S(2)}) %collective-permute-start.9) | collective-permute-done | bytes 262176 | tf_op jit(solution)/shard_map/ppermute | solution.py:54
  31.4 2.5 %collective-permute-done.7 = bf16[128,2048]{1,0:T(8,128)(2,1)S(1)} collective-permute-done((bf16[128,2048]{1,0:T(8,128)(2,1)S(1)}, bf16[128,2048]{1,0:T(8,128)(2,1)S(1)}, u32[]{:S(2)}, u32[]{:S(2)}) %collective-permute-start.7) | collective-permute-done | bytes 524320 | tf_op jit(solution)/shard_map/ppermute | solution.py:42
  35.1 1.7 %collective-permute-start.16 = (bf16[256,1024]{1,0:T(8,128)(2,1)S(1)}, bf16[256,1024]{1,0:T(8,128)(2,1)S(1)}, u32[]{:S(2)}, u32[]{:S(2)}) collective-permute-start(bf16[256,1024]{1,0:T(8,128)(2,1)S(1)} %collective-permute-done.10.refs_19_), channel_id=1, source_target_pairs={{0,6},{1,7},{2,0},{3,1},{4,2},{5,3},{6,4},{7,5},{8,14},{9,15},{10,... | collective-permute-start | bytes 1572872 | tf_op jit(solution)/shard_map/ppermute | solution.py:54
  36.8 6.8 %collective-permute-start.6 = (bf16[128,2048]{1,0:T(8,128)(2,1)S(1)}, bf16[128,2048]{1,0:T(8,128)(2,1)S(1)}, u32[]{:S(2)}, u32[]{:S(2)}) collective-permute-start(bf16[128,2048]{1,0:T(8,128)(2,1)S(1)} %fusion.11.refs_8_), channel_id=1, source_target_pairs={{0,8},{8,0},{16,24},{24,16},{32,40},{40,32},{48,56},{56,48},{64,72... | collective-permute-start | bytes 1572872 | tf_op jit(solution)/shard_map/ppermute | solution.py:30
  44.9 2.3 %collective-permute-start.11 = (bf16[128,2048]{1,0:T(8,128)(2,1)S(1)}, bf16[128,2048]{1,0:T(8,128)(2,1)S(1)}, u32[]{:S(2)}, u32[]{:S(2)}) collective-permute-start(bf16[128,2048]{1,0:T(8,128)(2,1)S(1)} %fusion.8.refs_9_), channel_id=1, source_target_pairs={{0,8},{8,0},{16,24},{24,16},{32,40},{40,32},{48,56},{56,48},{64,72... | collective-permute-start | bytes 1572872 | tf_op jit(solution)/shard_map/ppermute | solution.py:30
  47.4 5.2 %collective-permute-start.13 = (bf16[128,2048]{1,0:T(8,128)(2,1)S(1)}, bf16[128,2048]{1,0:T(8,128)(2,1)S(1)}, u32[]{:S(2)}, u32[]{:S(2)}) collective-permute-start(bf16[128,2048]{1,0:T(8,128)(2,1)S(1)} %collective-permute-done.12.refs_10_), channel_id=1, source_target_pairs={{0,8},{8,0},{16,24},{24,16},{32,40},{40,32},{48,56},{56,48},{64,72... | collective-permute-start | bytes 1572872 | tf_op jit(solution)/shard_map/ppermute | solution.py:30
  52.5 1.8 %collective-permute-done.14.refs_11_ = bf16[64,2048]{1,0:T(8,128)(2,1)S(1)} collective-permute-done((bf16[64,2048]{1,0:T(8,128)(2,1)S(1)}, bf16[64,2048]{1,0:T(8,128)(2,1)S(1)}, u32[]{:S(2)}, u32[]{:S(2)}) %collective-permute-start.14) | collective-permute-done | bytes 262176 | tf_op jit(solution)/shard_map/ppermute | solution.py:42
  54.4 2.8 %collective-permute-start.15 = (bf16[64,2048]{1,0:T(8,128)(2,1)S(1)}, bf16[64,2048]{1,0:T(8,128)(2,1)S(1)}, u32[]{:S(2)}, u32[]{:S(2)}) collective-permute-start(bf16[64,2048]{1,0:T(8,128)(2,1)S(1)} %collective-permute-done.14.refs_11_), channel_id=1, source_target_pairs={{0,8},{8,0},{16,24},{24,16},{32,40},{40,32},{48,56},{56,48},{64,72... | collective-permute-start | bytes 786440 | tf_op jit(solution)/shard_map/ppermute | solution.py:30
  58.3 18.9 %inner_steps.1 = (bf16[2,128,2048]{2,1,0:T(8,128)(2,1)S(1)}, bf16[2,128,1024]{2,1,0:T(8,128)(2,1)S(1)}, bf16[2,128,2048]{2,1,0:T(8,128)(2,1)S(1)}, bf16[448,2048...) custom-call(bf16[2,128,1024]{2,1,0:T(8,128)(2,1)S(1)} %get-tuple-ele, ...), custom_call_target="tpu_custom_call" | custom-call | flops 5000000000 | bytes 25165824 | tf_op jit(solution)/shard_map/inner_steps/pallas_call | solution.py:294
  77.2 3.8 %up_change.3 = bf16[448,2048]{1,0:T(8,128)(2,1)S(1)} custom-call(bf16[448,2048]{1,0:T(8,128)(2,1)S(1)} %get-tuple-element.25.s_ref, bf16[2,1024,128]{2,1,0:T(8,128)(2,1)S(1)} %get-tuple-element.22.refs_1_.n_ref, bf16[2,128,2048]{2,1,0:T(8,128)(2,1)S(1)} %get-tuple-element.24.g_ref), custom_call_target="tpu_custom_call" | custom-call | flops 469762048 | bytes 3670016 | tf_op jit(solution)/shard_map/up_change/pallas_call | solution.py:332
  81.5 4.7 %up_change.2 = bf16[576,2048]{1,0:T(8,128)(2,1)S(1)} custom-call(bf16[576,2048]{1,0:T(8,128)(2,1)S(1)} %get-tuple-element.23.s_ref, bf16[2,1024,128]{2,1,0:T(8,128)(2,1)S(1)} %get-tuple-element.22.refs_1_.n_ref, bf16[2,128,2048]{2,1,0:T(8,128)(2,1)S(1)} %get-tuple-element.24.g_ref), custom_call_target="tpu_custom_call" | custom-call | flops 603979776 | bytes 4718592 | tf_op jit(solution)/shard_map/up_change/pallas_call | solution.py:332
  86.3 2.8 %collective-permute-start.20 = (bf16[64,2048]{1,0:T(8,128)(2,1)S(1)}, bf16[64,2048]{1,0:T(8,128)(2,1)S(1)}, u32[]{:S(2)}, u32[]{:S(2)}) collective-permute-start(bf16[64,2048]{1,0:T(8,128)(2,1)S(1)} %add_convert_fusion.7), channel_id=1, source_target_pairs={{0,32},{8,232},{16,48},{24,248},{32,64},{40,8},{48,80},{56,24},{64... | collective-permute-start | bytes 786440 | tf_op jit(solution)/shard_map/ppermute | solution.py:46
  89.0 3.6 %down_change.2 = (bf16[256,1024]{1,0:T(8,128)(2,1)S(1)}, bf16[256,1024]{1,0:T(8,128)(2,1)S(1)}, bf16[256,1024]{1,0:T(8,128)(2,1)S(1)}) custom-call(bf16[768,1024]{1,0:T(8,128)(2,1)S(1)} %get-tuple-element.26.s_ref, bf16[2,128,2048]{2,1,0:T(8,128)(2,1)S(1)} %get-tuple-element.27.a_ref, bf16[2,128,1024]{2,1,0:T(8,128)(2,1)S(1)} %get-tuple-element.28.g_ref), custom_call_target="tpu_custom_call" | custom-call | flops 402653184 | bytes 3145728 | tf_op jit(solution)/shard_map/down_change/pallas_call | solution.py:359
  94.0 1.7 %collective-permute-start.24 = (bf16[256,1024]{1,0:T(8,128)(2,1)S(1)}, bf16[256,1024]{1,0:T(8,128)(2,1)S(1)}, u32[]{:S(2)}, u32[]{:S(2)}) collective-permute-start(bf16[256,1024]{1,0:T(8,128)(2,1)S(1)} %get-tuple-element.34), channel_id=1, source_target_pairs={{0,1},{1,0},{2,3},{3,2},{4,5},{5,4},{6,7},{7,6},{8,9},{9,8},{10,11... | collective-permute-start | bytes 1572872 | tf_op jit(solution)/shard_map/ppermute | solution.py:50
  96.6 5.4 %down_change.3 = (bf16[256,1024]{1,0:T(8,128)(2,1)S(1)}, bf16[256,1024]{1,0:T(8,128)(2,1)S(1)}, bf16[256,1024]{1,0:T(8,128)(2,1)S(1)}, bf16[256,1024]{1,0:T(8,128)(2,1)S(1)}, bf16[256,1024]{1,0:T(8,128)(2,1)S(1)}) custom-call(bf16[1280,1024]{1,0:T(8,128)(2,1)S(1)} %get-tuple-element.30.s_ref, bf16[2,128,2048]{2,1,0:T(8,128)(2,1)S(1)} %get-tuple-element.27.a_ref, ...), custom_call_target="tpu_custom_call" | custom-call | flops 671088640 | bytes 5242880 | tf_op jit(solution)/shard_map/down_change/pallas_call | solution.py:359
  102.1 5.1 %collective-permute-done.24 = bf16[256,1024]{1,0:T(8,128)(2,1)S(1)} collective-permute-done((bf16[256,1024]{1,0:T(8,128)(2,1)S(1)}, bf16[256,1024]{1,0:T(8,128)(2,1)S(1)}, u32[]{:S(2)}, u32[]{:S(2)}) %collective-permute-start.24) | collective-permute-done | bytes 524320 | tf_op jit(solution)/shard_map/ppermute | solution.py:50
  107.8 2.4 %collective-permute-start.27 = (bf16[128,1024]{1,0:T(8,128)(2,1)S(1)}, bf16[128,1024]{1,0:T(8,128)(2,1)S(1)}, u32[]{:S(2)}, u32[]{:S(2)}) collective-permute-start(bf16[128,1024]{1,0:T(8,128)(2,1)S(1)} %get-tuple-element.46), channel_id=1, source_target_pairs={{0,6},{1,7},{2,0},{3,1},{4,2},{5,3},{6,4},{7,5},{8,14},{9,15},{10,... | collective-permute-start | bytes 786440 | tf_op jit(solution)/shard_map/ppermute | solution.py:54
  110.9 6.2 %collective-permute-done.26 = bf16[128,1024]{1,0:T(8,128)(2,1)S(1)} collective-permute-done((bf16[128,1024]{1,0:T(8,128)(2,1)S(1)}, bf16[128,1024]{1,0:T(8,128)(2,1)S(1)}, u32[]{:S(2)}, u32[]{:S(2)}) %collective-permute-start.26) | collective-permute-done | bytes 262176 | tf_op jit(solution)/shard_map/ppermute | solution.py:54
  117.2 1.9 %collective-permute-done.25 = bf16[128,2048]{1,0:T(8,128)(2,1)S(1)} collective-permute-done((bf16[128,2048]{1,0:T(8,128)(2,1)S(1)}, bf16[128,2048]{1,0:T(8,128)(2,1)S(1)}, u32[]{:S(2)}, u32[]{:S(2)}) %collective-permute-start.25) | collective-permute-done | bytes 524320 | tf_op jit(solution)/shard_map/ppermute | solution.py:46
  120.4 1.7 %collective-permute-start.32 = (bf16[256,1024]{1,0:T(8,128)(2,1)S(1)}, bf16[256,1024]{1,0:T(8,128)(2,1)S(1)}, u32[]{:S(2)}, u32[]{:S(2)}) collective-permute-start(bf16[256,1024]{1,0:T(8,128)(2,1)S(1)} %add_convert_fusion.5), channel_id=1, source_target_pairs={{0,1},{1,0},{2,3},{3,2},{4,5},{5,4},{6,7},{7,6},{8,9},{9,8},{10,11... | collective-permute-start | bytes 1572872 | tf_op jit(solution)/shard_map/ppermute | solution.py:50
  122.1 1.5 %collective-permute-start.33 = (bf16[256,1024]{1,0:T(8,128)(2,1)S(1)}, bf16[256,1024]{1,0:T(8,128)(2,1)S(1)}, u32[]{:S(2)}, u32[]{:S(2)}) collective-permute-start(bf16[256,1024]{1,0:T(8,128)(2,1)S(1)} %add_convert_fusion.2), channel_id=1, source_target_pairs={{0,2},{1,3},{2,4},{3,5},{4,6},{5,7},{6,0},{7,1},{8,10},{9,11},{10,... | collective-permute-start | bytes 1572872 | tf_op jit(solution)/shard_map/ppermute | solution.py:54
  123.6 4.2 %collective-permute-done.28 = bf16[128,2048]{1,0:T(8,128)(2,1)S(1)} collective-permute-done((bf16[128,2048]{1,0:T(8,128)(2,1)S(1)}, bf16[128,2048]{1,0:T(8,128)(2,1)S(1)}, u32[]{:S(2)}, u32[]{:S(2)}) %collective-permute-start.28) | collective-permute-done | bytes 524320 | tf_op jit(solution)/shard_map/ppermute | solution.py:46
  127.9 3.8 %collective-permute-start.29 = (bf16[32,2048]{1,0:T(8,128)(2,1)S(1)}, bf16[32,2048]{1,0:T(8,128)(2,1)S(1)}, u32[]{:S(2)}, u32[]{:S(2)}) collective-permute-start(bf16[32,2048]{1,0:T(8,128)(2,1)S(1)} %get-tuple-element.42), channel_id=1, source_target_pairs={{0,16},{8,24},{16,0},{24,8},{32,48},{40,56},{48,32},{56,40},{64,80... | collective-permute-start | bytes 393224 | tf_op jit(solution)/shard_map/ppermute | solution.py:34
  131.7 4.6 %collective-permute-start.31 = (bf16[32,2048]{1,0:T(8,128)(2,1)S(1)}, bf16[32,2048]{1,0:T(8,128)(2,1)S(1)}, u32[]{:S(2)}, u32[]{:S(2)}) collective-permute-start(bf16[32,2048]{1,0:T(8,128)(2,1)S(1)} %get-tuple-element.43), channel_id=1, source_target_pairs={{0,24},{8,16},{16,8},{24,0},{32,56},{40,48},{48,40},{56,32},{64,88... | collective-permute-start | bytes 393224 | tf_op jit(solution)/shard_map/ppermute | solution.py:38
  136.6 1.9 %fusion.1 = (f32[1,256,1024]{2,1,0:T(8,128)}, f32[1,256,1024]{2,1,0:T(8,128)}) fusion(f32[1,256,1024]{2,1,0:T(8,128)S(1)} %copy-done.2, bf16[256,1024]{1,0:T(8,128)(2,1)S(1)} %collective-permute-done.34, bf16[256,1024]{1,0:T(8,128)(2,1)S(1)} %collective-permute-done.33, bf16[256,1024]{1,0:T(8,128)(2,1)S(1)} %collective-permute-done.32, ...), kind=kLoop, calls=%fused_computation.3 | loop fusion | flops 3670016 | bytes 6291456 | tf_op jit(solution)/shard_map/sub | solution.py:404
  138.5 4.3 %collective-permute-done.31 = bf16[32,2048]{1,0:T(8,128)(2,1)S(1)} collective-permute-done((bf16[32,2048]{1,0:T(8,128)(2,1)S(1)}, bf16[32,2048]{1,0:T(8,128)(2,1)S(1)}, u32[]{:S(2)}, u32[]{:S(2)}) %collective-permute-start.31) | collective-permute-done | bytes 131104 | tf_op jit(solution)/shard_map/ppermute | solution.py:38
  (80 shorter events, 18.1 us)
Async XLA Ops:
  1.6 10.3 %collective-permute-start.2 = (bf16[32,2048]{1,0:T(8,128)(2,1)S(1)}, bf16[32,2048]{1,0:T(8,128)(2,1)S(1)}, u32[]{:S(2)}, u32[]{:S(2)}) collective-permute-start(bf16[32,2048]{1,0:T(8,128)(2,1)S(1)} %convert_bitcast_fusion.1.refs_12_), channel_id=1, source_target_pairs={{0,24},{8,16},{16,8},{24,0},{32,56},{40,48},{48,40},{56,32},{64,88... | collective-permute-start | bytes 393224 | tf_op jit(solution)/shard_map/ppermute | solution.py:38
  6.0 5.9 %collective-permute-start.1 = (bf16[32,2048]{1,0:T(8,128)(2,1)S(1)}, bf16[32,2048]{1,0:T(8,128)(2,1)S(1)}, u32[]{:S(2)}, u32[]{:S(2)}) collective-permute-start(bf16[32,2048]{1,0:T(8,128)(2,1)S(1)} %convert_bitcast_fusion.1.refs_12_), channel_id=1, source_target_pairs={{0,8},{8,0},{16,24},{24,16},{32,40},{40,32},{48,56},{56,48},{64,72... | collective-permute-start | bytes 393224 | tf_op jit(solution)/shard_map/ppermute | solution.py:30
  6.0 6.4 %collective-permute-start = (bf16[32,2048]{1,0:T(8,128)(2,1)S(1)}, bf16[32,2048]{1,0:T(8,128)(2,1)S(1)}, u32[]{:S(2)}, u32[]{:S(2)}) collective-permute-start(bf16[32,2048]{1,0:T(8,128)(2,1)S(1)} %convert_bitcast_fusion.1.refs_12_), channel_id=1, source_target_pairs={{0,16},{8,24},{16,0},{24,8},{32,48},{40,56},{48,32},{56,40},{64,80... | collective-permute-start | bytes 393224 | tf_op jit(solution)/shard_map/ppermute | solution.py:34
  9.1 13.9 %collective-permute-start.5 = (bf16[256,1024]{1,0:T(8,128)(2,1)S(1)}, bf16[256,1024]{1,0:T(8,128)(2,1)S(1)}, u32[]{:S(2)}, u32[]{:S(2)}) collective-permute-start(bf16[256,1024]{1,0:T(8,128)(2,1)S(1)} %convert_bitcast_fusion.refs_20_), channel_id=1, source_target_pairs={{0,2},{1,3},{2,4},{3,5},{4,6},{5,7},{6,0},{7,1},{8,10},{9,11},{10,... | collective-permute-start | bytes 1572872 | tf_op jit(solution)/shard_map/ppermute | solution.py:54
  9.2 13.9 %collective-permute-start.4 = (bf16[256,1024]{1,0:T(8,128)(2,1)S(1)}, bf16[256,1024]{1,0:T(8,128)(2,1)S(1)}, u32[]{:S(2)}, u32[]{:S(2)}) collective-permute-start(bf16[256,1024]{1,0:T(8,128)(2,1)S(1)} %convert_bitcast_fusion.refs_20_), channel_id=1, source_target_pairs={{0,6},{1,7},{2,0},{3,1},{4,2},{5,3},{6,4},{7,5},{8,14},{9,15},{10,... | collective-permute-start | bytes 1572872 | tf_op jit(solution)/shard_map/ppermute | solution.py:54
  12.5 11.9 %collective-permute-start.3 = (bf16[128,2048]{1,0:T(8,128)(2,1)S(1)}, bf16[128,2048]{1,0:T(8,128)(2,1)S(1)}, u32[]{:S(2)}, u32[]{:S(2)}) collective-permute-start(bf16[128,2048]{1,0:T(8,128)(2,1)S(1)} %pad_maximum_fusion), channel_id=1, source_target_pairs={{0,224},{8,40},{16,240},{24,56},{32,0},{40,72},{48,16},{56,88},{64... | collective-permute-start | bytes 1572872 | tf_op jit(solution)/shard_map/ppermute | solution.py:42
  13.9 13.5 %collective-permute-start.10 = (bf16[256,1024]{1,0:T(8,128)(2,1)S(1)}, bf16[256,1024]{1,0:T(8,128)(2,1)S(1)}, u32[]{:S(2)}, u32[]{:S(2)}) collective-permute-start(bf16[256,1024]{1,0:T(8,128)(2,1)S(1)} %convert_bitcast_fusion.refs_20_), channel_id=1, source_target_pairs={{0,1},{1,0},{2,3},{3,2},{4,5},{5,4},{6,7},{7,6},{8,9},{9,8},{10,11... | collective-permute-start | bytes 1572872 | tf_op jit(solution)/shard_map/ppermute | solution.py:50
  24.4 9.5 %collective-permute-start.7 = (bf16[128,2048]{1,0:T(8,128)(2,1)S(1)}, bf16[128,2048]{1,0:T(8,128)(2,1)S(1)}, u32[]{:S(2)}, u32[]{:S(2)}) collective-permute-start(bf16[128,2048]{1,0:T(8,128)(2,1)S(1)} %fusion.11.refs_8_), channel_id=1, source_target_pairs={{0,224},{8,40},{16,240},{24,56},{32,0},{40,72},{48,16},{56,88},{64... | collective-permute-start | bytes 1572872 | tf_op jit(solution)/shard_map/ppermute | solution.py:42
  24.5 6.5 %collective-permute-start.9 = (bf16[128,1024]{1,0:T(8,128)(2,1)S(1)}, bf16[128,1024]{1,0:T(8,128)(2,1)S(1)}, u32[]{:S(2)}, u32[]{:S(2)}) collective-permute-start(bf16[128,1024]{1,0:T(8,128)(2,1)S(1)} %slice.138), channel_id=1, source_target_pairs={{0,2},{1,3},{2,4},{3,5},{4,6},{5,7},{6,0},{7,1},{8,10},{9,11},{10,... | collective-permute-start | bytes 786440 | tf_op jit(solution)/shard_map/ppermute | solution.py:54
  33.9 11.0 %collective-permute-start.12 = (bf16[128,2048]{1,0:T(8,128)(2,1)S(1)}, bf16[128,2048]{1,0:T(8,128)(2,1)S(1)}, u32[]{:S(2)}, u32[]{:S(2)}) collective-permute-start(bf16[128,2048]{1,0:T(8,128)(2,1)S(1)} %fusion.8.refs_9_), channel_id=1, source_target_pairs={{0,224},{8,40},{16,240},{24,56},{32,0},{40,72},{48,16},{56,88},{64... | collective-permute-start | bytes 1572872 | tf_op jit(solution)/shard_map/ppermute | solution.py:42
  34.0 13.2 %collective-permute-start.18 = (bf16[256,1024]{1,0:T(8,128)(2,1)S(1)}, bf16[256,1024]{1,0:T(8,128)(2,1)S(1)}, u32[]{:S(2)}, u32[]{:S(2)}) collective-permute-start(bf16[256,1024]{1,0:T(8,128)(2,1)S(1)} %collective-permute-done.10.refs_19_), channel_id=1, source_target_pairs={{0,2},{1,3},{2,4},{3,5},{4,6},{5,7},{6,0},{7,1},{8,10},{9,11},{10,... | collective-permute-start | bytes 1572872 | tf_op jit(solution)/shard_map/ppermute | solution.py:54
  35.1 12.2 %collective-permute-start.16 = (bf16[256,1024]{1,0:T(8,128)(2,1)S(1)}, bf16[256,1024]{1,0:T(8,128)(2,1)S(1)}, u32[]{:S(2)}, u32[]{:S(2)}) collective-permute-start(bf16[256,1024]{1,0:T(8,128)(2,1)S(1)} %collective-permute-done.10.refs_19_), channel_id=1, source_target_pairs={{0,6},{1,7},{2,0},{3,1},{4,2},{5,3},{6,4},{7,5},{8,14},{9,15},{10,... | collective-permute-start | bytes 1572872 | tf_op jit(solution)/shard_map/ppermute | solution.py:54
  36.8 21.4 %collective-permute-start.6 = (bf16[128,2048]{1,0:T(8,128)(2,1)S(1)}, bf16[128,2048]{1,0:T(8,128)(2,1)S(1)}, u32[]{:S(2)}, u32[]{:S(2)}) collective-permute-start(bf16[128,2048]{1,0:T(8,128)(2,1)S(1)} %fusion.11.refs_8_), channel_id=1, source_target_pairs={{0,8},{8,0},{16,24},{24,16},{32,40},{40,32},{48,56},{56,48},{64,72... | collective-permute-start | bytes 1572872 | tf_op jit(solution)/shard_map/ppermute | solution.py:30
  43.6 14.5 %collective-permute-start.17 = (bf16[256,1024]{1,0:T(8,128)(2,1)S(1)}, bf16[256,1024]{1,0:T(8,128)(2,1)S(1)}, u32[]{:S(2)}, u32[]{:S(2)}) collective-permute-start(bf16[256,1024]{1,0:T(8,128)(2,1)S(1)} %pad_maximum_fusion.1), channel_id=1, source_target_pairs={{0,1},{1,0},{2,3},{3,2},{4,5},{5,4},{6,7},{7,6},{8,9},{9,8},{10,11... | collective-permute-start | bytes 1572872 | tf_op jit(solution)/shard_map/ppermute | solution.py:50
  44.9 13.2 %collective-permute-start.11 = (bf16[128,2048]{1,0:T(8,128)(2,1)S(1)}, bf16[128,2048]{1,0:T(8,128)(2,1)S(1)}, u32[]{:S(2)}, u32[]{:S(2)}) collective-permute-start(bf16[128,2048]{1,0:T(8,128)(2,1)S(1)} %fusion.8.refs_9_), channel_id=1, source_target_pairs={{0,8},{8,0},{16,24},{24,16},{32,40},{40,32},{48,56},{56,48},{64,72... | collective-permute-start | bytes 1572872 | tf_op jit(solution)/shard_map/ppermute | solution.py:30
  47.3 7.1 %collective-permute-start.14 = (bf16[64,2048]{1,0:T(8,128)(2,1)S(1)}, bf16[64,2048]{1,0:T(8,128)(2,1)S(1)}, u32[]{:S(2)}, u32[]{:S(2)}) collective-permute-start(bf16[64,2048]{1,0:T(8,128)(2,1)S(1)} %slice.141), channel_id=1, source_target_pairs={{0,224},{8,40},{16,240},{24,56},{32,0},{40,72},{48,16},{56,88},{64... | collective-permute-start | bytes 786440 | tf_op jit(solution)/shard_map/ppermute | solution.py:42
  47.4 10.9 %collective-permute-start.13 = (bf16[128,2048]{1,0:T(8,128)(2,1)S(1)}, bf16[128,2048]{1,0:T(8,128)(2,1)S(1)}, u32[]{:S(2)}, u32[]{:S(2)}) collective-permute-start(bf16[128,2048]{1,0:T(8,128)(2,1)S(1)} %collective-permute-done.12.refs_10_), channel_id=1, source_target_pairs={{0,8},{8,0},{16,24},{24,16},{32,40},{40,32},{48,56},{56,48},{64,72... | collective-permute-start | bytes 1572872 | tf_op jit(solution)/shard_map/ppermute | solution.py:30
  86.3 9.9 %collective-permute-start.20 = (bf16[64,2048]{1,0:T(8,128)(2,1)S(1)}, bf16[64,2048]{1,0:T(8,128)(2,1)S(1)}, u32[]{:S(2)}, u32[]{:S(2)}) collective-permute-start(bf16[64,2048]{1,0:T(8,128)(2,1)S(1)} %add_convert_fusion.7), channel_id=1, source_target_pairs={{0,32},{8,232},{16,48},{24,248},{32,64},{40,8},{48,80},{56,24},{64... | collective-permute-start | bytes 786440 | tf_op jit(solution)/shard_map/ppermute | solution.py:46
  92.6 17.6 %collective-permute-start.23 = (bf16[256,1024]{1,0:T(8,128)(2,1)S(1)}, bf16[256,1024]{1,0:T(8,128)(2,1)S(1)}, u32[]{:S(2)}, u32[]{:S(2)}) collective-permute-start(bf16[256,1024]{1,0:T(8,128)(2,1)S(1)} %get-tuple-element.32), channel_id=1, source_target_pairs={{0,6},{1,7},{2,0},{3,1},{4,2},{5,3},{6,4},{7,5},{8,14},{9,15},{10,... | collective-permute-start | bytes 1572872 | tf_op jit(solution)/shard_map/ppermute | solution.py:54
  94.0 13.3 %collective-permute-start.24 = (bf16[256,1024]{1,0:T(8,128)(2,1)S(1)}, bf16[256,1024]{1,0:T(8,128)(2,1)S(1)}, u32[]{:S(2)}, u32[]{:S(2)}) collective-permute-start(bf16[256,1024]{1,0:T(8,128)(2,1)S(1)} %get-tuple-element.34), channel_id=1, source_target_pairs={{0,1},{1,0},{2,3},{3,2},{4,5},{5,4},{6,7},{7,6},{8,9},{9,8},{10,11... | collective-permute-start | bytes 1572872 | tf_op jit(solution)/shard_map/ppermute | solution.py:50
  95.6 14.6 %collective-permute-start.22 = (bf16[256,1024]{1,0:T(8,128)(2,1)S(1)}, bf16[256,1024]{1,0:T(8,128)(2,1)S(1)}, u32[]{:S(2)}, u32[]{:S(2)}) collective-permute-start(bf16[256,1024]{1,0:T(8,128)(2,1)S(1)} %get-tuple-element.29), channel_id=1, source_target_pairs={{0,2},{1,3},{2,4},{3,5},{4,6},{5,7},{6,0},{7,1},{8,10},{9,11},{10,... | collective-permute-start | bytes 1572872 | tf_op jit(solution)/shard_map/ppermute | solution.py:54
  96.3 14.2 %collective-permute-start.21 = (bf16[128,2048]{1,0:T(8,128)(2,1)S(1)}, bf16[128,2048]{1,0:T(8,128)(2,1)S(1)}, u32[]{:S(2)}, u32[]{:S(2)}) collective-permute-start(bf16[128,2048]{1,0:T(8,128)(2,1)S(1)} %add_convert_fusion.6), channel_id=1, source_target_pairs={{0,32},{8,232},{16,48},{24,248},{32,64},{40,8},{48,80},{56,24},{64... | collective-permute-start | bytes 1572872 | tf_op jit(solution)/shard_map/ppermute | solution.py:46
  107.4 9.6 %collective-permute-start.26 = (bf16[128,1024]{1,0:T(8,128)(2,1)S(1)}, bf16[128,1024]{1,0:T(8,128)(2,1)S(1)}, u32[]{:S(2)}, u32[]{:S(2)}) collective-permute-start(bf16[128,1024]{1,0:T(8,128)(2,1)S(1)} %get-tuple-element.45), channel_id=1, source_target_pairs={{0,2},{1,3},{2,4},{3,5},{4,6},{5,7},{6,0},{7,1},{8,10},{9,11},{10,... | collective-permute-start | bytes 786440 | tf_op jit(solution)/shard_map/ppermute | solution.py:54
  107.8 9.4 %collective-permute-start.27 = (bf16[128,1024]{1,0:T(8,128)(2,1)S(1)}, bf16[128,1024]{1,0:T(8,128)(2,1)S(1)}, u32[]{:S(2)}, u32[]{:S(2)}) collective-permute-start(bf16[128,1024]{1,0:T(8,128)(2,1)S(1)} %get-tuple-element.46), channel_id=1, source_target_pairs={{0,6},{1,7},{2,0},{3,1},{4,2},{5,3},{6,4},{7,5},{8,14},{9,15},{10,... | collective-permute-start | bytes 786440 | tf_op jit(solution)/shard_map/ppermute | solution.py:54
  110.8 8.4 %collective-permute-start.25 = (bf16[128,2048]{1,0:T(8,128)(2,1)S(1)}, bf16[128,2048]{1,0:T(8,128)(2,1)S(1)}, u32[]{:S(2)}, u32[]{:S(2)}) collective-permute-start(bf16[128,2048]{1,0:T(8,128)(2,1)S(1)} %add_convert_fusion.3), channel_id=1, source_target_pairs={{0,32},{8,232},{16,48},{24,248},{32,64},{40,8},{48,80},{56,24},{64... | collective-permute-start | bytes 1572872 | tf_op jit(solution)/shard_map/ppermute | solution.py:46
  119.4 8.4 %collective-permute-start.28 = (bf16[128,2048]{1,0:T(8,128)(2,1)S(1)}, bf16[128,2048]{1,0:T(8,128)(2,1)S(1)}, u32[]{:S(2)}, u32[]{:S(2)}) collective-permute-start(bf16[128,2048]{1,0:T(8,128)(2,1)S(1)} %add_convert_fusion), channel_id=1, source_target_pairs={{0,32},{8,232},{16,48},{24,248},{32,64},{40,8},{48,80},{56,24},{64... | collective-permute-start | bytes 1572872 | tf_op jit(solution)/shard_map/ppermute | solution.py:46
  120.4 15.9 %collective-permute-start.32 = (bf16[256,1024]{1,0:T(8,128)(2,1)S(1)}, bf16[256,1024]{1,0:T(8,128)(2,1)S(1)}, u32[]{:S(2)}, u32[]{:S(2)}) collective-permute-start(bf16[256,1024]{1,0:T(8,128)(2,1)S(1)} %add_convert_fusion.5), channel_id=1, source_target_pairs={{0,1},{1,0},{2,3},{3,2},{4,5},{5,4},{6,7},{7,6},{8,9},{9,8},{10,11... | collective-permute-start | bytes 1572872 | tf_op jit(solution)/shard_map/ppermute | solution.py:50
  122.1 14.5 %collective-permute-start.34 = (bf16[256,1024]{1,0:T(8,128)(2,1)S(1)}, bf16[256,1024]{1,0:T(8,128)(2,1)S(1)}, u32[]{:S(2)}, u32[]{:S(2)}) collective-permute-start(bf16[256,1024]{1,0:T(8,128)(2,1)S(1)} %add_convert_fusion.1), channel_id=1, source_target_pairs={{0,6},{1,7},{2,0},{3,1},{4,2},{5,3},{6,4},{7,5},{8,14},{9,15},{10,... | collective-permute-start | bytes 1572872 | tf_op jit(solution)/shard_map/ppermute | solution.py:54
  122.1 14.5 %collective-permute-start.33 = (bf16[256,1024]{1,0:T(8,128)(2,1)S(1)}, bf16[256,1024]{1,0:T(8,128)(2,1)S(1)}, u32[]{:S(2)}, u32[]{:S(2)}) collective-permute-start(bf16[256,1024]{1,0:T(8,128)(2,1)S(1)} %add_convert_fusion.2), channel_id=1, source_target_pairs={{0,2},{1,3},{2,4},{3,5},{4,6},{5,7},{6,0},{7,1},{8,10},{9,11},{10,... | collective-permute-start | bytes 1572872 | tf_op jit(solution)/shard_map/ppermute | solution.py:54
  127.9 10.6 %collective-permute-start.29 = (bf16[32,2048]{1,0:T(8,128)(2,1)S(1)}, bf16[32,2048]{1,0:T(8,128)(2,1)S(1)}, u32[]{:S(2)}, u32[]{:S(2)}) collective-permute-start(bf16[32,2048]{1,0:T(8,128)(2,1)S(1)} %get-tuple-element.42), channel_id=1, source_target_pairs={{0,16},{8,24},{16,0},{24,8},{32,48},{40,56},{48,32},{56,40},{64,80... | collective-permute-start | bytes 393224 | tf_op jit(solution)/shard_map/ppermute | solution.py:34
  131.7 11.1 %collective-permute-start.31 = (bf16[32,2048]{1,0:T(8,128)(2,1)S(1)}, bf16[32,2048]{1,0:T(8,128)(2,1)S(1)}, u32[]{:S(2)}, u32[]{:S(2)}) collective-permute-start(bf16[32,2048]{1,0:T(8,128)(2,1)S(1)} %get-tuple-element.43), channel_id=1, source_target_pairs={{0,24},{8,16},{16,8},{24,0},{32,56},{40,48},{48,40},{56,32},{64,88... | collective-permute-start | bytes 393224 | tf_op jit(solution)/shard_map/ppermute | solution.py:38
  136.3 6.5 %collective-permute-start.30 = (bf16[32,2048]{1,0:T(8,128)(2,1)S(1)}, bf16[32,2048]{1,0:T(8,128)(2,1)S(1)}, u32[]{:S(2)}, u32[]{:S(2)}) collective-permute-start(bf16[32,2048]{1,0:T(8,128)(2,1)S(1)} %get-tuple-element.44), channel_id=1, source_target_pairs={{0,8},{8,0},{16,24},{24,16},{32,40},{40,32},{48,56},{56,48},{64,72... | collective-permute-start | bytes 393224 | tf_op jit(solution)/shard_map/ppermute | solution.py:30
  (9 other events, 170.9 us)
